TPU v7x, 128 devices: a whole 4x4x4 slice. The times are simulated.
128 devices in a mesh: owner: 16 (over z, y), sub: 8 (over x, core).
Axes of the slice: x: 4, y: 4, z: 4, core: 2. Of those that a mesh axis runs over, the one named last changes fastest.
Arguments:
- guess: float32 [1024, 32, 1024], P(('owner', 'sub')), may hold values from -6 to 6
- rhs: float32 [1024, 32, 1024], P(('owner', 'sub')), may hold values from -6 to 6
- coef: float32 [1024, 32, 1024], P(('owner', 'sub')), may hold values from 0.1 to 10
- occupied: int32 [1024], P(('owner', 'sub')), may hold values 0 or 1
- neighbours: int32 [1024, 4], P(('owner', 'sub')), may hold values from -1 to 1023, as said below
- swap_slot: int32 [128, 16], P(('owner', 'sub')), may hold values from -1 to 7, as said below
- send_list: int32 [128, 16], P(('owner', 'sub')), may hold values from -1 to 15, as said below
- recv_list: int32 [128, 16], P(('owner', 'sub')), may hold values from -1 to 15, as said below
Outputs:
- solution: float32 [1024, 32, 1024], P(('owner', 'sub'))
- coarse_residual: float32 [1024, 16, 256], P(('owner', 'sub'))
Inputs may be any that keep to these rules, and one draw needn't show every extreme that they name: The x-minus and x-plus neighbours of a slot lie on the same device; the z-minus neighbour lies on the device with owner index one lower and the same sub index, the z-plus neighbour on the one with owner index one higher. Neighbourhood is mutual across opposite faces. An entry is >= 0 only where the owner indices differ in exactly one bit; entries are mutual (swap_slot[d, q] >= 0 exactly when the partner's entry for d's owner index is), and the slots of one row are distinct. `send_list`: at most 2 faces go from one device to one device of its segment; a device reaches it towards itself. Every face named is received by exactly one ghost, consistent with recv_list. `recv_list`: each ghost of a device is named at most once.
All inputs are finite; a program needn't handle non-finite values. No bound on the sum of `occupied` on one device may be relied on, other than what follows from the above.
Results may differ from a plain program's by a relative error of at most 0.0003.
Values sent between devices are 32-bit elements; how exact they have to be, the bound alone decides.
No kernel may reach another device: no remote copies, remote signals or barrier semaphores. Data moves between devices by JAX's collectives and lax.ppermute only.
A program may use at most 128 MiB of HBM per device.

v0:
```python
import jax
import jax.numpy as jnp
from jax import lax
from jax.experimental import pallas as pl
from jax.experimental.pallas import tpu as pltpu
from jax.sharding import PartitionSpec as P

SWEEPS = 3
OMEGA = 0.8
SLOTS = 8
EDGE = 32
PLANE = EDGE * EDGE
ROWS = SLOTS * EDGE
LANES = 128
COLS = PLANE // LANES
FIELD = (ROWS, PLANE)
FACES = 2 * SLOTS
FACE = (8, LANES)
SMEM = pl.BlockSpec(memory_space=pltpu.SMEM)
VMEM = pl.BlockSpec(memory_space=pltpu.VMEM)


def f32(*shape):
    return jax.ShapeDtypeStruct(shape, jnp.float32)


def params(mib):
    return pltpu.CompilerParams(vmem_limit_bytes=mib << 20)


def cost(flops, bytes_accessed):
    return pl.CostEstimate(flops=flops, bytes_accessed=bytes_accessed, transcendentals=0)


def column(c):
    return slice(c * LANES, (c + 1) * LANES)


def block_rows(j):
    return pl.ds(pl.multiple_of(j * EDGE, EDGE), EDGE)


def scaled_neighbour(neighbours, j, side):
    entry = neighbours[j, side]
    return jnp.maximum(entry, 0) % SLOTS, (entry >= 0).astype(jnp.float32)


def pack_face(first, side):
    group = lax.broadcasted_iota(jnp.int32, FACE, 1) // EDGE
    face = None
    for g in range(4):
        turn = (EDGE * g + EDGE * side) % LANES
        part = first(g)
        part = pltpu.roll(part, turn, 1) if turn else part
        face = part if face is None else jnp.where(group == g, part, face)
    return face


def unpack_face(face, side):
    parts = []
    for g in range(4):
        turn = (-EDGE * g - EDGE * side) % LANES
        parts.append(pltpu.roll(face, turn, 1) if turn else face)
    return jnp.concatenate(parts, axis=0)


def pack_faces(field, packed):
    def one(j, carry):
        for side in range(2):
            cols = column(0) if side == 0 else column(COLS - 1)
            packed[2 * j + side] = pack_face(
                lambda g: field[pl.ds(pl.multiple_of(j * EDGE + 8 * g, 8), 8), cols], side
            )
        return carry

    lax.fori_loop(0, SLOTS, one, 0)


def send_faces(packed, send_list, out, offset, stride):
    for entry in range(FACES):
        face = send_list[0, entry]
        out[entry * stride + offset] = packed[jnp.maximum(face, 0)] * (face >= 0).astype(jnp.float32)


def receive_faces(arrived, recv_list, ghost, offset, stride):
    ghost[...] = jnp.zeros(ghost.shape, jnp.float32)
    for entry in range(FACES):
        face = recv_list[0, entry]
        ghost[jnp.where(face >= 0, face, FACES)] = arrived[entry * stride + offset]


def send_layers(field, parity, out_even, out_odd, offset):
    even = parity[0] == 0
    for j in range(SLOTS):
        for c in range(COLS):
            bottom = field[j * EDGE : j * EDGE + 1, column(c)]
            top = field[(j + 1) * EDGE - 1 : (j + 1) * EDGE, column(c)]
            out_even[offset + j, c : c + 1, :] = jnp.where(even, top, bottom)
            out_odd[offset + j, c : c + 1, :] = jnp.where(even, bottom, top)


def receive_layers(in_even, in_odd, parity, below, above, offset):
    from_even = in_even[offset : offset + SLOTS]
    from_odd = in_odd[offset : offset + SLOTS]
    even = parity[0] == 0
    above[...] = jnp.where(even, from_even, from_odd)
    below[...] = jnp.where(even, from_odd, from_even)


def six_neighbours(field, j, neighbours, ghost, below, above):
    lane = lax.broadcasted_iota(jnp.int32, (EDGE, LANES), 1)
    row = lax.broadcasted_iota(jnp.int32, (EDGE, LANES), 0)
    x = lane % EDGE
    xm, has_xm = scaled_neighbour(neighbours, j, 0)
    xp, has_xp = scaled_neighbour(neighbours, j, 1)
    zm, has_zm = scaled_neighbour(neighbours, j, 2)
    zp, has_zp = scaled_neighbour(neighbours, j, 3)
    under_face, over_face = below[zm] * has_zm, above[zp] * has_zp
    own, minus_rows, plus_rows = block_rows(j), block_rows(xm), block_rows(xp)
    values = [field[own, column(c)] for c in range(COLS)]
    forth = [pltpu.roll(v, EDGE, 1) for v in values]
    back = [pltpu.roll(v, LANES - EDGE, 1) for v in values]
    forth.insert(0, unpack_face(ghost[2 * j], 0))
    back.append(unpack_face(ghost[2 * j + 1], 1))
    for c in range(COLS):
        v = values[c]
        left = field[minus_rows, column(c)] * has_xm
        right = field[plus_rows, column(c)] * has_xp
        under = under_face[c : c + 1, :]
        over = over_face[c : c + 1, :]
        yield (
            c,
            v,
            (
                jnp.where(x == 0, pltpu.roll(left, LANES - EDGE + 1, 1), pltpu.roll(v, 1, 1)),
                jnp.where(x == EDGE - 1, pltpu.roll(right, EDGE - 1, 1), pltpu.roll(v, LANES - 1, 1)),
                jnp.where(lane < EDGE, forth[c], forth[c + 1]),
                jnp.where(lane >= LANES - EDGE, back[c + 1], back[c]),
                jnp.where(row == 0, under, pltpu.roll(v, 1, 0)),
                jnp.where(row == EDGE - 1, over, pltpu.roll(v, EDGE - 1, 0)),
            ),
        )


def swap_pack_kernel(bits, pairs, owner, occupied, *refs):
    outs = refs[3 * bits :]
    for bit in range(bits):
        slot = jnp.maximum(pairs[0, owner[0] ^ (1 << bit)], 0)
        alive = occupied[slot].astype(jnp.float32)
        for k in range(3):
            outs[bit][k * EDGE : (k + 1) * EDGE, :] = refs[3 * bit + k][...] * alive


def swap_pack(fields, occupied, pairs, owner, bits):
    def spec(bit):
        return pl.BlockSpec(
            (EDGE, PLANE),
            lambda i, pairs, owner, occupied: (jnp.maximum(pairs[0, owner[0] ^ (1 << bit)], 0), 0),
        )

    return pl.pallas_call(
        lambda *refs: swap_pack_kernel(bits, *refs),
        grid_spec=pltpu.PrefetchScalarGridSpec(
            num_scalar_prefetch=3,
            grid=(1,),
            in_specs=[spec(bit) for bit in range(bits) for k in range(3)],
            out_specs=[pl.BlockSpec((3 * EDGE, PLANE), lambda i, *refs: (0, 0)) for bit in range(bits)],
        ),
        out_shape=[f32(3 * EDGE, PLANE) for bit in range(bits)],
        compiler_params=params(16),
        cost_estimate=cost(1 << 19, 3 << 20),
        name="swap_pack",
    )(pairs, owner, occupied, *(fields * bits))


def merge_kernel(
    bits, pairs, owner, occupied, send_list, parity, guess, rhs, coef, *refs
):
    incoming = refs[:bits]
    v, f, c, ze, zo, ys, packed = refs[bits:]

    def one(j, carry):
        alive = occupied[j].astype(jnp.float32)
        rows = block_rows(j)
        for source, target in ((guess, v), (rhs, f), (coef, c)):
            target[rows, :] = source[rows, :] * alive
        return carry

    lax.fori_loop(0, SLOTS, one, 0)
    for bit in range(bits):
        slot = pairs[0, owner[0] ^ (1 << bit)]

        @pl.when(slot >= 0)
        def _(bit=bit, slot=slot):
            rows = block_rows(jnp.maximum(slot, 0))
            for k, target in enumerate((v, f, c)):
                target[rows, :] = incoming[bit][k * EDGE : (k + 1) * EDGE, :]

    for k, field in enumerate((v, c)):
        send_layers(field, parity, ze, zo, k * SLOTS)
        pack_faces(field, packed)
        send_faces(packed, send_list, ys, k, 2)


def merge(fields, incoming, occupied, pairs, owner, send_list, parity):
    bits = len(incoming)
    return pl.pallas_call(
        lambda *refs: merge_kernel(bits, *refs),
        in_specs=[SMEM] * 5 + [VMEM] * (3 + bits),
        out_specs=[VMEM] * 6,
        out_shape=[f32(*FIELD)] * 3 + [f32(2 * SLOTS, *FACE)] * 2 + [f32(2 * FACES, *FACE)],
        scratch_shapes=[pltpu.VMEM((FACES,) + FACE, jnp.float32)],
        compiler_params=params(24),
        cost_estimate=cost(1 << 20, 8 << 20),
        name="merge",
    )(pairs, owner, occupied, send_list, parity, *fields, *incoming)


def first_kernel(
    neighbours, send_list, recv_list, parity, v, f, c, ie, io, ya,
    wk, wf, dg, u, ze, zo, ys,
    below, above, ghost, below_c, above_c, ghost_c, packed,
):
    receive_layers(ie, io, parity, below, above, 0)
    receive_layers(ie, io, parity, below_c, above_c, SLOTS)
    receive_faces(ya, recv_list, ghost, 0, 2)
    receive_faces(ya, recv_list, ghost_c, 1, 2)

    def one(j, carry):
        rows = block_rows(j)
        for n, k, around in six_neighbours(c, j, neighbours, ghost_c, below_c, above_c):
            faces = [0.5 * (k + jnp.where(other > 0.0, other, k)) for other in around]
            total = faces[0]
            for face in faces[1:]:
                total = total + face
            alive = k > 0.0
            weight = jnp.where(alive, OMEGA / jnp.where(alive, total, 1.0), 0.0)
            for d in range(6):
                wk[d, rows, column(n)] = weight * faces[d]
            wf[rows, column(n)] = weight * f[rows, column(n)]
            dg[rows, column(n)] = jnp.where(alive, total * (1.0 / OMEGA), 0.0)
        return carry

    lax.fori_loop(0, SLOTS, one, 0)
    sweep_blocks(neighbours, v, wk, wf, u, ghost, below, above)
    send_all(u, send_list, parity, ze, zo, ys, packed)


def sweep_blocks(neighbours, v, wk, wf, u, ghost, below, above):
    def one(j, carry):
        rows = block_rows(j)
        for n, centre, around in six_neighbours(v, j, neighbours, ghost, below, above):
            total = wf[rows, column(n)] + (1.0 - OMEGA) * centre
            for d in range(6):
                total = total + wk[d, rows, column(n)] * around[d]
            u[rows, column(n)] = total
        return carry

    lax.fori_loop(0, SLOTS, one, 0)


def send_all(u, send_list, parity, ze, zo, ys, packed):
    send_layers(u, parity, ze, zo, 0)
    pack_faces(u, packed)
    send_faces(packed, send_list, ys, 0, 1)


LAYERS = pltpu.VMEM((SLOTS,) + FACE, jnp.float32)
GHOSTS = pltpu.VMEM((FACES + 1,) + FACE, jnp.float32)


def first(v, f, c, ie, io, ya, neighbours, send_list, recv_list, parity):
    return pl.pallas_call(
        first_kernel,
        in_specs=[SMEM] * 4 + [VMEM] * 6,
        out_specs=[VMEM] * 7,
        out_shape=[f32(6, *FIELD)] + [f32(*FIELD)] * 3 + [f32(SLOTS, *FACE)] * 2 + [f32(FACES, *FACE)],
        scratch_shapes=[LAYERS, LAYERS, GHOSTS, LAYERS, LAYERS, GHOSTS, pltpu.VMEM((FACES,) + FACE, jnp.float32)],
        compiler_params=params(24),
        cost_estimate=cost(1 << 24, 12 << 20),
        name="first",
    )(neighbours, send_list, recv_list, parity, v, f, c, ie, io, ya)


def sweep_kernel(
    neighbours, send_list, recv_list, parity, v, wk, wf, ie, io, ya,
    u, ze, zo, ys,
    below, above, ghost, packed,
):
    receive_layers(ie, io, parity, below, above, 0)
    receive_faces(ya, recv_list, ghost, 0, 1)
    sweep_blocks(neighbours, v, wk, wf, u, ghost, below, above)
    send_all(u, send_list, parity, ze, zo, ys, packed)


def sweep(v, wk, wf, ie, io, ya, neighbours, send_list, recv_list, parity):
    return pl.pallas_call(
        sweep_kernel,
        in_specs=[SMEM] * 4 + [VMEM] * 6,
        out_specs=[VMEM] * 4,
        out_shape=[f32(*FIELD)] + [f32(SLOTS, *FACE)] * 2 + [f32(FACES, *FACE)],
        scratch_shapes=[LAYERS, LAYERS, GHOSTS, pltpu.VMEM((FACES,) + FACE, jnp.float32)],
        compiler_params=params(24),
        cost_estimate=cost(1 << 22, 9 << 20),
        name="sweep",
    )(neighbours, send_list, recv_list, parity, v, wk, wf, ie, io, ya)


def last_kernel(
    neighbours, recv_list, parity, v, wk, wf, dg, ie, io, ya,
    coarse,
    below, above, ghost, residual,
):
    receive_layers(ie, io, parity, below, above, 0)
    receive_faces(ya, recv_list, ghost, 0, 1)

    def one(j, carry):
        rows = block_rows(j)
        for n, centre, around in six_neighbours(v, j, neighbours, ghost, below, above):
            total = wf[rows, column(n)] - OMEGA * centre
            for d in range(6):
                total = total + wk[d, rows, column(n)] * around[d]
            residual[n, rows, :] = total * dg[rows, column(n)]
        return carry

    lax.fori_loop(0, SLOTS, one, 0)
    lane = lax.broadcasted_iota(jnp.int32, (LANES, LANES), 0)
    target = lax.broadcasted_iota(jnp.int32, (LANES, LANES), 1)
    place = (lane // (2 * EDGE)) * (EDGE // 2) + (lane % EDGE) // 2
    half = ROWS // 2
    for part in range(2):
        total = jnp.zeros((half, LANES), jnp.float32)
        for n in range(4):
            column_sum = (
                residual[part * 4 + n, pl.ds(0, half, stride=2), :]
                + residual[part * 4 + n, pl.ds(1, half, stride=2), :]
            )
            gather = jnp.where(place + EDGE * n == target, 0.125, 0.0)
            total = total + jnp.dot(
                column_sum, gather, precision=lax.Precision.HIGHEST, preferred_element_type=jnp.float32
            )
        coarse[:, part * LANES : (part + 1) * LANES] = total


def last(v, wk, wf, dg, ie, io, ya, neighbours, recv_list, parity):
    return pl.pallas_call(
        last_kernel,
        in_specs=[SMEM] * 3 + [VMEM] * 7,
        out_specs=VMEM,
        out_shape=f32(ROWS // 2, PLANE // 4),
        scratch_shapes=[LAYERS, LAYERS, GHOSTS, pltpu.VMEM((COLS, ROWS, LANES), jnp.float32)],
        compiler_params=params(24),
        cost_estimate=cost(1 << 24, 10 << 20),
        name="last",
    )(neighbours, recv_list, parity, v, wk, wf, dg, ie, io, ya)


def pair_swap(values, stride):
    count = lax.axis_size("owner")
    return lax.ppermute(values, "owner", [(i, i ^ stride) for i in range(count)])


def odd_pair_swap(values):
    count = lax.axis_size("owner")
    return lax.ppermute(values, "owner", [(i, ((i - 1) ^ 1) + 1) for i in range(1, count - 1)])


def exchange(ze, zo, ys):
    arrived = lax.all_to_all(ys, "sub", split_axis=0, concat_axis=0, tiled=True)
    return pair_swap(ze, 1), odd_pair_swap(zo), arrived


def body(guess, rhs, coef, occupied, neighbours, swap_slot, send_list, recv_list):
    my_owner = lax.axis_index("owner").astype(jnp.int32)
    owner = my_owner.reshape(1)
    parity = (my_owner % 2).reshape(1)
    bits = lax.axis_size("owner").bit_length() - 1
    fields = tuple(values.reshape(FIELD) for values in (guess, rhs, coef))
    outgoing = swap_pack(fields, occupied, swap_slot, owner, bits)
    incoming = tuple(pair_swap(outgoing[bit], 1 << bit) for bit in range(bits))
    v, f, c, ze, zo, ys = merge(fields, incoming, occupied, swap_slot, owner, send_list, parity)
    ghosts = exchange(ze, zo, ys)
    wk, wf, dg, v, ze, zo, ys = first(v, f, c, *ghosts, neighbours, send_list, recv_list, parity)
    for _ in range(SWEEPS - 1):
        ghosts = exchange(ze, zo, ys)
        v, ze, zo, ys = sweep(v, wk, wf, *ghosts, neighbours, send_list, recv_list, parity)
    ghosts = exchange(ze, zo, ys)
    coarse = last(v, wk, wf, dg, *ghosts, neighbours, recv_list, parity)
    return v.reshape(SLOTS, EDGE, PLANE), coarse.reshape(SLOTS, EDGE // 2, PLANE // 4)


def solution(mesh):
    wide, flat, single = P(("owner", "sub"), None, None), P(("owner", "sub"), None), P(("owner", "sub"))
    return jax.shard_map(
        body,
        mesh=mesh,
        in_specs=(wide, wide, wide, single, flat, flat, flat, flat),
        out_specs=(wide, wide),
        check_vma=False,
    )
```

profile of v0, /device:TPU:32, one launch (start us, length us, event | category | flops | bytes accessed | tf_op | source)
XLA Modules:
  0.0 130.5 jit_solution(3626442639640393898)
XLA Ops:
  3.1 1.2 copy-done.8
  5.7 1.8 %swap_pack.1 = (f32[96,1024]{1,0:T(8,128)}, f32[96,1024]{1,0:T(8,128)}, f32[96,1024]{1,0:T(8,128)}, f32[96,1024]{1,0:T(8,128)}) custom-call(s32[1,16]{1,0:T(1,128)S(1)} %copy-done.22, s32[1]{0:T(128)} %bitcast.1.refs_1_, s32[8]{0:T(128)S(1)} %copy-done.24, f32[256,1024]{1,0:T(8,128)S(1)} %bitcast.7, f32[256,1024]{1,0:T(8,128)S(1)} %bitcast.12, ...), custom_call_target="tpu_custom_call" | custom-call | flops 524288 | bytes 3145728 | tf_op jit(solution)/shard_map/swap_pack/pallas_call | solution.py:161
  7.5 1.6 %collective-permute-start = (f32[96,1024]{1,0:T(8,128)}, f32[96,1024]{1,0:T(8,128)S(1)}, u32[]{:S(2)}, u32[]{:S(2)}) collective-permute-start(f32[96,1024]{1,0:T(8,128)} %get-tuple-element.27), channel_id=1, source_target_pairs={{0,8},{8,0},{16,24},{24,16},{32,40},{40,32},{48,56},{56,48},{64,72... | collective-permute-start | bytes 1179656 | tf_op jit(solution)/shard_map/ppermute | solution.py:360
  9.0 2.9 %collective-permute-start.1 = (f32[96,1024]{1,0:T(8,128)}, f32[96,1024]{1,0:T(8,128)}, u32[]{:S(2)}, u32[]{:S(2)}) collective-permute-start(f32[96,1024]{1,0:T(8,128)} %get-tuple-element.28), channel_id=1, source_target_pairs={{0,16},{8,24},{16,0},{24,8},{32,48},{40,56},{48,32},{56,40},{64,80... | collective-permute-start | bytes 1179656 | tf_op jit(solution)/shard_map/ppermute | solution.py:360
  12.1 3.3 %collective-permute-start.3 = (f32[96,1024]{1,0:T(8,128)}, f32[96,1024]{1,0:T(8,128)}, u32[]{:S(2)}, u32[]{:S(2)}) collective-permute-start(f32[96,1024]{1,0:T(8,128)} %get-tuple-element.30), channel_id=1, source_target_pairs={{0,64},{8,72},{16,80},{24,88},{32,96},{40,104},{48,112},{56,120},{... | collective-permute-start | bytes 1179656 | tf_op jit(solution)/shard_map/ppermute | solution.py:360
  15.3 4.4 %collective-permute-done.refs_8_ = f32[96,1024]{1,0:T(8,128)S(1)} collective-permute-done((f32[96,1024]{1,0:T(8,128)}, f32[96,1024]{1,0:T(8,128)S(1)}, u32[]{:S(2)}, u32[]{:S(2)}) %collective-permute-start) | collective-permute-done | bytes 393248 | tf_op jit(solution)/shard_map/ppermute | solution.py:360
  19.7 9.8 %collective-permute-done.1.refs_9_ = f32[96,1024]{1,0:T(8,128)} collective-permute-done((f32[96,1024]{1,0:T(8,128)}, f32[96,1024]{1,0:T(8,128)}, u32[]{:S(2)}, u32[]{:S(2)}) %collective-permute-start.1) | collective-permute-done | bytes 393248 | tf_op jit(solution)/shard_map/ppermute | solution.py:360
  29.5 2.8 %collective-permute-done.3.refs_11_ = f32[96,1024]{1,0:T(8,128)} collective-permute-done((f32[96,1024]{1,0:T(8,128)}, f32[96,1024]{1,0:T(8,128)}, u32[]{:S(2)}, u32[]{:S(2)}) %collective-permute-start.3) | collective-permute-done | bytes 393248 | tf_op jit(solution)/shard_map/ppermute | solution.py:360
  32.4 2.9 %merge.1 = (f32[256,1024]{1,0:T(8,128)S(1)}, f32[256,1024]{1,0:T(8,128)S(1)}, f32[256,1024]{1,0:T(8,128)S(1)}, f32[16,8,128]{2,1,0:T(8,128)S(1)}, f32[16,8,128]{2,1,0:T(8,128)S(1)}, /*index=5*/f32[32,8,128]{2,1,0:T(8,128)S(1)}) custom-call(s32[1,16]{1,0:T(1,128)S(1)} %copy-done.23, s32[1]{0:T(128)} %bitcast.1.refs_1_, s32[8]{0:T(128)S(1)} %copy-done.25, ...), custom_call_target="tpu_custom_call" | custom-call | flops 1048576 | bytes 8388608 | tf_op jit(solution)/shard_map/merge/pallas_call | solution.py:207
  40.2 4.4 %all-to-all-start = ((f32[32,8,128]{2,1,0:T(8,128)}), f32[32,8,128]{2,1,0:T(8,128)S(1)}, u32[]{:S(2)}, u32[]{:S(2)}) async-start(f32[32,8,128]{2,1,0:T(8,128)} %copy-done.19), calls=%async_computation | async-start | bytes 262144 | tf_op jit(solution)/shard_map/all_to_all | solution.py:369
  44.7 4.6 %collective-permute-start.5 = (f32[16,8,128]{2,1,0:T(8,128)}, f32[16,8,128]{2,1,0:T(8,128)S(1)}, u32[]{:S(2)}, u32[]{:S(2)}) collective-permute-start(f32[16,8,128]{2,1,0:T(8,128)} %copy-done.26), channel_id=1, source_target_pairs={{8,16},{16,8},{24,32},{32,24},{40,48},{48,40},{56,64},{64,56},{72,... | collective-permute-start | bytes 196616 | tf_op jit(solution)/shard_map/ppermute | solution.py:365
  50.1 3.2 %collective-permute-done.5.io = f32[16,8,128]{2,1,0:T(8,128)S(1)} collective-permute-done((f32[16,8,128]{2,1,0:T(8,128)}, f32[16,8,128]{2,1,0:T(8,128)S(1)}, u32[]{:S(2)}, u32[]{:S(2)}) %collective-permute-start.5) | collective-permute-done | bytes 65568 | tf_op jit(solution)/shard_map/ppermute | solution.py:365
  54.5 1.2 copy-done.16
  55.7 1.2 copy-done.18
  56.9 7.5 %first.1 = (f32[6,256,1024]{2,1,0:T(8,128)S(1)}, f32[256,1024]{1,0:T(8,128)S(1)}, f32[256,1024]{1,0:T(8,128)S(1)}, f32[256,1024]{1,0:T(8,128)S(1)}, f32[8,8,128]...) custom-call(s32[8,4]{1,0:T(8,128)S(1)} %copy.12.neighbours, s32[1,16]{1,0:T(1,128)S(1)} %copy-done.20, ...), custom_call_target="tpu_custom_call" | custom-call | flops 16777216 | bytes 12582912 | tf_op jit(solution)/shard_map/first/pallas_call | solution.py:273
  64.4 2.7 %copy-done = f32[6,256,1024]{2,1,0:T(8,128)} copy-done((f32[6,256,1024]{2,1,0:T(8,128)}, f32[6,256,1024]{2,1,0:T(8,128)S(1)}, u32[]{:S(2)}) %copy-start) | copy-done | bytes 6291480
  67.1 4.7 %all-to-all-start.1 = ((f32[16,8,128]{2,1,0:T(8,128)}), f32[16,8,128]{2,1,0:T(8,128)S(1)}, u32[]{:S(2)}, u32[]{:S(2)}) async-start(f32[16,8,128]{2,1,0:T(8,128)} %get-tuple-element.42), calls=%async_computation.1 | async-start | bytes 131072 | tf_op jit(solution)/shard_map/all_to_all | solution.py:369
  71.8 4.6 %collective-permute-start.7 = (f32[8,8,128]{2,1,0:T(8,128)S(1)}, f32[8,8,128]{2,1,0:T(8,128)S(1)}, u32[]{:S(2)}, u32[]{:S(2)}) collective-permute-start(f32[8,8,128]{2,1,0:T(8,128)S(1)} %get-tuple-element.41), channel_id=1, source_target_pairs={{8,16},{16,8},{24,32},{32,24},{40,48},{48,40},{56,64},{64,56},{72,... | collective-permute-start | bytes 98312 | tf_op jit(solution)/shard_map/ppermute | solution.py:365
  76.5 3.3 %collective-permute-done.7.io = f32[8,8,128]{2,1,0:T(8,128)S(1)} collective-permute-done((f32[8,8,128]{2,1,0:T(8,128)S(1)}, f32[8,8,128]{2,1,0:T(8,128)S(1)}, u32[]{:S(2)}, u32[]{:S(2)}) %collective-permute-start.7) | collective-permute-done | bytes 32800 | tf_op jit(solution)/shard_map/ppermute | solution.py:365
  79.7 2.8 %copy-done.1 = f32[6,256,1024]{2,1,0:T(8,128)S(1)} copy-done((f32[6,256,1024]{2,1,0:T(8,128)S(1)}, f32[6,256,1024]{2,1,0:T(8,128)}, u32[]{:S(2)}) %copy-start.1) | copy-done | bytes 6291480
  82.5 4.4 %sweep.2 = (f32[256,1024]{1,0:T(8,128)S(1)}, f32[8,8,128]{2,1,0:T(8,128)S(1)}, f32[8,8,128]{2,1,0:T(8,128)S(1)}, f32[16,8,128]{2,1,0:T(8,128)}) custom-call(s32[8,4]{1,0:T(8,128)S(1)} %copy.12.neighbours, s32[1,16]{1,0:T(1,128)S(1)} %copy-done.20, s32[1,16]{1,0:T(1,128)S(1)} %copy-done.21, s32[1]{0:T(128)} %bitcast.refs_4_.parity, ...), custom_call_target="tpu_custom_call" | custom-call | flops 4194304 | bytes 9437184 | tf_op jit(solution)/shard_map/sweep/pallas_call | solution.py:297
  87.9 4.8 %all-to-all-start.2 = ((f32[16,8,128]{2,1,0:T(8,128)}), f32[16,8,128]{2,1,0:T(8,128)S(1)}, u32[]{:S(2)}, u32[]{:S(2)}) async-start(f32[16,8,128]{2,1,0:T(8,128)} %get-tuple-element.46), calls=%async_computation.2 | async-start | bytes 131072 | tf_op jit(solution)/shard_map/all_to_all | solution.py:369
  92.7 4.6 %collective-permute-start.9 = (f32[8,8,128]{2,1,0:T(8,128)S(1)}, f32[8,8,128]{2,1,0:T(8,128)S(1)}, u32[]{:S(2)}, u32[]{:S(2)}) collective-permute-start(f32[8,8,128]{2,1,0:T(8,128)S(1)} %get-tuple-element.45), channel_id=1, source_target_pairs={{8,16},{16,8},{24,32},{32,24},{40,48},{48,40},{56,64},{64,56},{72,... | collective-permute-start | bytes 98312 | tf_op jit(solution)/shard_map/ppermute | solution.py:365
  97.3 3.3 %collective-permute-done.9.io = f32[8,8,128]{2,1,0:T(8,128)S(1)} collective-permute-done((f32[8,8,128]{2,1,0:T(8,128)S(1)}, f32[8,8,128]{2,1,0:T(8,128)S(1)}, u32[]{:S(2)}, u32[]{:S(2)}) %collective-permute-start.9) | collective-permute-done | bytes 32800 | tf_op jit(solution)/shard_map/ppermute | solution.py:365
  100.6 2.8 %copy-done.2 = f32[6,256,1024]{2,1,0:T(8,128)S(1)} copy-done((f32[6,256,1024]{2,1,0:T(8,128)S(1)}, f32[6,256,1024]{2,1,0:T(8,128)}, u32[]{:S(2)}) %copy-start.2) | copy-done | bytes 6291480
  104.6 4.7 %sweep.3 = (f32[256,1024]{1,0:T(8,128)}, f32[8,8,128]{2,1,0:T(8,128)S(1)}, f32[8,8,128]{2,1,0:T(8,128)S(1)}, f32[16,8,128]{2,1,0:T(8,128)}) custom-call(s32[8,4]{1,0:T(8,128)S(1)} %copy.12.neighbours, s32[1,16]{1,0:T(1,128)S(1)} %copy-done.20, s32[1,16]{1,0:T(1,128)S(1)} %copy-done.21, s32[1]{0:T(128)} %bitcast.refs_4_.parity, f32[256,1024]{1,0:T(8,128)S(1)} %copy-done.12, ...), custom_call_target="tpu_custom_call" | custom-call | flops 4194304 | bytes 9437184 | tf_op jit(solution)/shard_map/sweep/pallas_call | solution.py:297
  109.3 4.8 %all-to-all-start.3 = ((f32[16,8,128]{2,1,0:T(8,128)}), f32[16,8,128]{2,1,0:T(8,128)S(1)}, u32[]{:S(2)}, u32[]{:S(2)}) async-start(f32[16,8,128]{2,1,0:T(8,128)} %get-tuple-element.51), calls=%async_computation.3 | async-start | bytes 131072 | tf_op jit(solution)/shard_map/all_to_all | solution.py:369
  114.1 4.6 %collective-permute-start.11 = (f32[8,8,128]{2,1,0:T(8,128)S(1)}, f32[8,8,128]{2,1,0:T(8,128)S(1)}, u32[]{:S(2)}, u32[]{:S(2)}) collective-permute-start(f32[8,8,128]{2,1,0:T(8,128)S(1)} %get-tuple-element.50), channel_id=1, source_target_pairs={{8,16},{16,8},{24,32},{32,24},{40,48},{48,40},{56,64},{64,56},{72,... | collective-permute-start | bytes 98312 | tf_op jit(solution)/shard_map/ppermute | solution.py:365
  118.8 3.3 %collective-permute-done.11.io = f32[8,8,128]{2,1,0:T(8,128)S(1)} collective-permute-done((f32[8,8,128]{2,1,0:T(8,128)S(1)}, f32[8,8,128]{2,1,0:T(8,128)S(1)}, u32[]{:S(2)}, u32[]{:S(2)}) %collective-permute-start.11) | collective-permute-done | bytes 32800 | tf_op jit(solution)/shard_map/ppermute | solution.py:365
  122.1 2.8 %copy-done.3 = f32[6,256,1024]{2,1,0:T(8,128)S(1)} copy-done((f32[6,256,1024]{2,1,0:T(8,128)S(1)}, f32[6,256,1024]{2,1,0:T(8,128)}, u32[]{:S(2)}) %copy-start.3) | copy-done | bytes 6291480
  124.8 1.2 copy-done.10
  126.1 4.4 %last.1 = f32[128,256]{1,0:T(8,128)} custom-call(s32[8,4]{1,0:T(8,128)S(1)} %copy.12.neighbours, s32[1,16]{1,0:T(1,128)S(1)} %copy-done.21, s32[1]{0:T(128)} %bitcast.refs_4_.parity, f32[256,1024]{1,0:T(8,128)S(1)} %copy-done.10, f32[6,256,1024]{2,1,0:T(8,128)S(1)} %copy-done.3, f32[256,1024]{1,0:T(8,128)S(1)} %get-tuple-element.39.wf, ...), custom_call_target="tpu_custom_call" | custom-call | flops 16777216 | bytes 10485760 | tf_op jit(solution)/shard_map/last/pallas_call | solution.py:346
  (63 shorter events, 13.1 us)
Async XLA Ops:
  0.6 1.2 copy-start.4
  3.1 1.2 copy-start.8
  5.6 26.7 %copy-start.5 = (f32[8,32,1024]{2,1,0:T(8,128)S(1)}, f32[8,32,1024]{2,1,0:T(8,128)}, u32[]{:S(2)}) copy-start(f32[8,32,1024]{2,1,0:T(8,128)} %param.8) | copy-start | bytes 3145732
  5.6 26.7 %copy-start.7 = (f32[8,32,1024]{2,1,0:T(8,128)S(1)}, f32[8,32,1024]{2,1,0:T(8,128)}, u32[]{:S(2)}) copy-start(f32[8,32,1024]{2,1,0:T(8,128)} %param.9) | copy-start | bytes 3145732
  5.6 26.7 %copy-start.9 = (f32[8,32,1024]{2,1,0:T(8,128)S(1)}, f32[8,32,1024]{2,1,0:T(8,128)}, u32[]{:S(2)}) copy-start(f32[8,32,1024]{2,1,0:T(8,128)} %param.10) | copy-start | bytes 3145732
  5.6 26.7 %copy-start.20 = (s32[1,16]{1,0:T(1,128)S(1)}, s32[1,16]{1,0:T(1,128)}, u32[]{:S(2)}) copy-start(s32[1,16]{1,0:T(1,128)} %send_list.5) | copy-start | bytes 196
  5.6 26.7 %copy-start.23 = (s32[1,16]{1,0:T(1,128)S(1)}, s32[1,16]{1,0:T(1,128)}, u32[]{:S(2)}) copy-start(s32[1,16]{1,0:T(1,128)} %refs_0_.3) | copy-start | bytes 196
  5.6 26.7 %copy-start.25 = (s32[8]{0:T(128)S(1)}, s32[8]{0:T(128)}, u32[]{:S(2)}) copy-start(s32[8]{0:T(128)} %refs_2_.3) | copy-start | bytes 100
  5.7 47.6 %copy-start.21 = (s32[1,16]{1,0:T(1,128)S(1)}, s32[1,16]{1,0:T(1,128)}, u32[]{:S(2)}) copy-start(s32[1,16]{1,0:T(1,128)} %recv_list.7) | copy-start | bytes 196
  7.5 12.2 %collective-permute-start = (f32[96,1024]{1,0:T(8,128)}, f32[96,1024]{1,0:T(8,128)S(1)}, u32[]{:S(2)}, u32[]{:S(2)}) collective-permute-start(f32[96,1024]{1,0:T(8,128)} %get-tuple-element.27), channel_id=1, source_target_pairs={{0,8},{8,0},{16,24},{24,16},{32,40},{40,32},{48,56},{56,48},{64,72... | collective-permute-start | bytes 1179656 | tf_op jit(solution)/shard_map/ppermute | solution.py:360
  9.0 20.5 %collective-permute-start.1 = (f32[96,1024]{1,0:T(8,128)}, f32[96,1024]{1,0:T(8,128)}, u32[]{:S(2)}, u32[]{:S(2)}) collective-permute-start(f32[96,1024]{1,0:T(8,128)} %get-tuple-element.28), channel_id=1, source_target_pairs={{0,16},{8,24},{16,0},{24,8},{32,48},{40,56},{48,32},{56,40},{64,80... | collective-permute-start | bytes 1179656 | tf_op jit(solution)/shard_map/ppermute | solution.py:360
  11.9 17.6 %collective-permute-start.2 = (f32[96,1024]{1,0:T(8,128)}, f32[96,1024]{1,0:T(8,128)}, u32[]{:S(2)}, u32[]{:S(2)}) collective-permute-start(f32[96,1024]{1,0:T(8,128)} %get-tuple-element.29), channel_id=1, source_target_pairs={{0,32},{8,40},{16,48},{24,56},{32,0},{40,8},{48,16},{56,24},{64,96... | collective-permute-start | bytes 1179656 | tf_op jit(solution)/shard_map/ppermute | solution.py:360
  12.1 20.3 %collective-permute-start.3 = (f32[96,1024]{1,0:T(8,128)}, f32[96,1024]{1,0:T(8,128)}, u32[]{:S(2)}, u32[]{:S(2)}) collective-permute-start(f32[96,1024]{1,0:T(8,128)} %get-tuple-element.30), channel_id=1, source_target_pairs={{0,64},{8,72},{16,80},{24,88},{32,96},{40,104},{48,112},{56,120},{... | collective-permute-start | bytes 1179656 | tf_op jit(solution)/shard_map/ppermute | solution.py:360
  40.2 13.1 %all-to-all-start = ((f32[32,8,128]{2,1,0:T(8,128)}), f32[32,8,128]{2,1,0:T(8,128)S(1)}, u32[]{:S(2)}, u32[]{:S(2)}) async-start(f32[32,8,128]{2,1,0:T(8,128)} %copy-done.19), calls=%async_computation | async-start | bytes 262144 | tf_op jit(solution)/shard_map/all_to_all | solution.py:369
  44.5 5.5 %collective-permute-start.4 = (f32[16,8,128]{2,1,0:T(8,128)}, f32[16,8,128]{2,1,0:T(8,128)S(1)}, u32[]{:S(2)}, u32[]{:S(2)}) collective-permute-start(f32[16,8,128]{2,1,0:T(8,128)} %copy-done.27), channel_id=1, source_target_pairs={{0,8},{8,0},{16,24},{24,16},{32,40},{40,32},{48,56},{56,48},{64,72... | collective-permute-start | bytes 196616 | tf_op jit(solution)/shard_map/ppermute | solution.py:360
  44.7 8.6 %collective-permute-start.5 = (f32[16,8,128]{2,1,0:T(8,128)}, f32[16,8,128]{2,1,0:T(8,128)S(1)}, u32[]{:S(2)}, u32[]{:S(2)}) collective-permute-start(f32[16,8,128]{2,1,0:T(8,128)} %copy-done.26), channel_id=1, source_target_pairs={{8,16},{16,8},{24,32},{32,24},{40,48},{48,40},{56,64},{64,56},{72,... | collective-permute-start | bytes 196616 | tf_op jit(solution)/shard_map/ppermute | solution.py:365
  53.2 1.2 copy-start.14
  54.5 1.2 copy-start.16
  55.7 1.2 copy-start.18
  64.4 2.7 %copy-start = (f32[6,256,1024]{2,1,0:T(8,128)}, f32[6,256,1024]{2,1,0:T(8,128)S(1)}, u32[]{:S(2)}) copy-start(f32[6,256,1024]{2,1,0:T(8,128)S(1)} %get-tuple-element.38.wk) | copy-start | bytes 18874372
  67.1 12.6 %all-to-all-start.1 = ((f32[16,8,128]{2,1,0:T(8,128)}), f32[16,8,128]{2,1,0:T(8,128)S(1)}, u32[]{:S(2)}, u32[]{:S(2)}) async-start(f32[16,8,128]{2,1,0:T(8,128)} %get-tuple-element.42), calls=%async_computation.1 | async-start | bytes 131072 | tf_op jit(solution)/shard_map/all_to_all | solution.py:369
  71.8 4.7 %collective-permute-start.6 = (f32[8,8,128]{2,1,0:T(8,128)S(1)}, f32[8,8,128]{2,1,0:T(8,128)S(1)}, u32[]{:S(2)}, u32[]{:S(2)}) collective-permute-start(f32[8,8,128]{2,1,0:T(8,128)S(1)} %get-tuple-element.40), channel_id=1, source_target_pairs={{0,8},{8,0},{16,24},{24,16},{32,40},{40,32},{48,56},{56,48},{64,72... | collective-permute-start | bytes 98312 | tf_op jit(solution)/shard_map/ppermute | solution.py:360
  71.8 7.9 %collective-permute-start.7 = (f32[8,8,128]{2,1,0:T(8,128)S(1)}, f32[8,8,128]{2,1,0:T(8,128)S(1)}, u32[]{:S(2)}, u32[]{:S(2)}) collective-permute-start(f32[8,8,128]{2,1,0:T(8,128)S(1)} %get-tuple-element.41), channel_id=1, source_target_pairs={{8,16},{16,8},{24,32},{32,24},{40,48},{48,40},{56,64},{64,56},{72,... | collective-permute-start | bytes 98312 | tf_op jit(solution)/shard_map/ppermute | solution.py:365
  79.7 2.8 %copy-start.1 = (f32[6,256,1024]{2,1,0:T(8,128)S(1)}, f32[6,256,1024]{2,1,0:T(8,128)}, u32[]{:S(2)}) copy-start(f32[6,256,1024]{2,1,0:T(8,128)} %copy-done) | copy-start | bytes 18874372
  87.9 12.7 %all-to-all-start.2 = ((f32[16,8,128]{2,1,0:T(8,128)}), f32[16,8,128]{2,1,0:T(8,128)S(1)}, u32[]{:S(2)}, u32[]{:S(2)}) async-start(f32[16,8,128]{2,1,0:T(8,128)} %get-tuple-element.46), calls=%async_computation.2 | async-start | bytes 131072 | tf_op jit(solution)/shard_map/all_to_all | solution.py:369
  92.7 4.7 %collective-permute-start.8 = (f32[8,8,128]{2,1,0:T(8,128)S(1)}, f32[8,8,128]{2,1,0:T(8,128)S(1)}, u32[]{:S(2)}, u32[]{:S(2)}) collective-permute-start(f32[8,8,128]{2,1,0:T(8,128)S(1)} %get-tuple-element.44), channel_id=1, source_target_pairs={{0,8},{8,0},{16,24},{24,16},{32,40},{40,32},{48,56},{56,48},{64,72... | collective-permute-start | bytes 98312 | tf_op jit(solution)/shard_map/ppermute | solution.py:360
  92.7 7.9 %collective-permute-start.9 = (f32[8,8,128]{2,1,0:T(8,128)S(1)}, f32[8,8,128]{2,1,0:T(8,128)S(1)}, u32[]{:S(2)}, u32[]{:S(2)}) collective-permute-start(f32[8,8,128]{2,1,0:T(8,128)S(1)} %get-tuple-element.45), channel_id=1, source_target_pairs={{8,16},{16,8},{24,32},{32,24},{40,48},{48,40},{56,64},{64,56},{72,... | collective-permute-start | bytes 98312 | tf_op jit(solution)/shard_map/ppermute | solution.py:365
  100.6 2.8 %copy-start.2 = (f32[6,256,1024]{2,1,0:T(8,128)S(1)}, f32[6,256,1024]{2,1,0:T(8,128)}, u32[]{:S(2)}) copy-start(f32[6,256,1024]{2,1,0:T(8,128)} %copy-done) | copy-start | bytes 18874372
  109.3 12.7 %all-to-all-start.3 = ((f32[16,8,128]{2,1,0:T(8,128)}), f32[16,8,128]{2,1,0:T(8,128)S(1)}, u32[]{:S(2)}, u32[]{:S(2)}) async-start(f32[16,8,128]{2,1,0:T(8,128)} %get-tuple-element.51), calls=%async_computation.3 | async-start | bytes 131072 | tf_op jit(solution)/shard_map/all_to_all | solution.py:369
  114.1 4.7 %collective-permute-start.10 = (f32[8,8,128]{2,1,0:T(8,128)S(1)}, f32[8,8,128]{2,1,0:T(8,128)S(1)}, u32[]{:S(2)}, u32[]{:S(2)}) collective-permute-start(f32[8,8,128]{2,1,0:T(8,128)S(1)} %get-tuple-element.49), channel_id=1, source_target_pairs={{0,8},{8,0},{16,24},{24,16},{32,40},{40,32},{48,56},{56,48},{64,72... | collective-permute-start | bytes 98312 | tf_op jit(solution)/shard_map/ppermute | solution.py:360
  114.1 7.9 %collective-permute-start.11 = (f32[8,8,128]{2,1,0:T(8,128)S(1)}, f32[8,8,128]{2,1,0:T(8,128)S(1)}, u32[]{:S(2)}, u32[]{:S(2)}) collective-permute-start(f32[8,8,128]{2,1,0:T(8,128)S(1)} %get-tuple-element.50), channel_id=1, source_target_pairs={{8,16},{16,8},{24,32},{32,24},{40,48},{48,40},{56,64},{64,56},{72,... | collective-permute-start | bytes 98312 | tf_op jit(solution)/shard_map/ppermute | solution.py:365
  122.1 2.8 %copy-start.3 = (f32[6,256,1024]{2,1,0:T(8,128)S(1)}, f32[6,256,1024]{2,1,0:T(8,128)}, u32[]{:S(2)}) copy-start(f32[6,256,1024]{2,1,0:T(8,128)} %copy-done) | copy-start | bytes 18874372
  (12 other events, 10.8 us)
where the time goes:
time: 132 us; the launch traced here: 130 us
  starting transfers between devices  45.2 us (34%)
  waiting for transfers between devices  30 us (23%)
  local copies, waits for them, and re-layouts  28.7 us (22%)
  Pallas kernels  25.8 us (20%)
    unnamed x57, local copies, waits for them, and re-layouts  28.7 us
    all_to_all x4, starting transfers between devices, exchange(): arrived = lax.all_to_all(ys, 'sub', split_axis=0, concat_axis=0, tiled=True)  18.6 us
    ppermute x4, starting transfers between devices, odd_pair_swap(): lax.ppermute(values, 'owner', [(i, (i - 1 ^ 1) + 1) for i in range(1, cou...  18.5 us
    ppermute x8, waiting for transfers between devices, pair_swap(): lax.ppermute(values, 'owner', [(i, i ^ stride) for i in range(count)])  17 us
    ppermute x4, waiting for transfers between devices, odd_pair_swap(): lax.ppermute(values, 'owner', [(i, (i - 1 ^ 1) + 1) for i in range(1, cou...  13 us
    pallas_call x2, Pallas kernels, sweep(): pl.pallas_call(sweep_kernel, in_specs=[SMEM] * 4 + [VMEM] * 6, out_specs=...  9.12 us
    ppermute x8, starting transfers between devices, pair_swap(): lax.ppermute(values, 'owner', [(i, i ^ stride) for i in range(count)])  8 us
    pallas_call x1, Pallas kernels, first(): pl.pallas_call(first_kernel, in_specs=[SMEM] * 4 + [VMEM] * 6, out_specs=...  7.51 us
  transfers between devices with their start and end apart: 16, of which 7 were waited for; matrix products, arithmetic and copies ran while one was open for 1% of the time, Pallas kernels for 0%

commit v1 on v0

v1 whole, which is shorter than its diff:
```python
import jax
import jax.numpy as jnp
from jax import lax
from jax.experimental import pallas as pl
from jax.experimental.pallas import tpu as pltpu
from jax.sharding import PartitionSpec as P

OMEGA = 0.8
SLOTS = 8
EDGE = 32
PLANE = EDGE * EDGE
ROWS = SLOTS * EDGE
LANES = 128
COLS = PLANE // LANES
FIELD = (ROWS, PLANE)
FACES = 2 * SLOTS
TILE = (8, LANES)
BITS = 4
V1, V2, C1, C2, F1 = range(5)
KINDS = 5
SEND = 4 * SLOTS
RECV = SEND + FACES
SMEM = pl.BlockSpec(memory_space=pltpu.SMEM)
VMEM = pl.BlockSpec(memory_space=pltpu.VMEM)
HBM = pl.BlockSpec(memory_space=pltpu.HBM)


def f32(*shape):
    return jax.ShapeDtypeStruct(shape, jnp.float32)


def tiles(count):
    return f32(count, *TILE)


def scratch(*shape):
    return pltpu.VMEM(shape, jnp.float32)


def params(mib):
    return pltpu.CompilerParams(vmem_limit_bytes=mib << 20)


def cost(flops, bytes_accessed):
    return pl.CostEstimate(flops=flops, bytes_accessed=bytes_accessed, transcendentals=0)


def column(c):
    return slice(c * LANES, (c + 1) * LANES)


def block_rows(j):
    return pl.ds(pl.multiple_of(j * EDGE, EDGE), EDGE)


def iotas(shape):
    rank = len(shape)
    sub = lax.broadcasted_iota(jnp.int32, shape, rank - 2)
    lane = lax.broadcasted_iota(jnp.int32, shape, rank - 1)
    return sub, lane


def slot_or(entry, none):
    return jnp.where(entry >= 0, jnp.maximum(entry, 0) % SLOTS, none)


def layer_tile(field, row, out, index):
    for c in range(COLS):
        out[index, c : c + 1, :] = field[row : row + 1, column(c)]


def face_tile(field, first_row, side):
    group = lax.broadcasted_iota(jnp.int32, TILE, 1) // EDGE
    cols = column(0) if side == 0 else column(COLS - 1)
    face = None
    for g in range(4):
        turn = (EDGE * g + EDGE * side) % LANES
        part = field[pl.ds(pl.multiple_of(first_row + 8 * g, 8), 8), cols]
        part = pltpu.roll(part, turn, 1) if turn else part
        face = part if face is None else jnp.where(group == g, part, face)
    return face


def unpack_face(face, side):
    parts = []
    for g in range(4):
        turn = (-EDGE * g - EDGE * side) % LANES
        parts.append(pltpu.roll(face, turn, 1) if turn else face)
    return jnp.concatenate(parts, axis=0)


def all_faces(field, out):
    def one(j, carry):
        for side in range(2):
            out[2 * j + side] = face_tile(field, j * EDGE, side)
        return carry

    lax.fori_loop(0, SLOTS, one, 0)


def pick_faces(faces, mine, out, offset, stride):
    for entry in range(FACES):
        face = mine[SEND + entry]
        out[(entry // 2) * stride + entry % 2 + offset] = faces[jnp.maximum(face, 0)] * (face >= 0).astype(
            jnp.float32
        )


def place_faces(arrived, mine, ghost, offset, stride):
    ghost[...] = jnp.zeros(ghost.shape, jnp.float32)
    for entry in range(FACES):
        face = mine[RECV + entry]
        ghost[jnp.where(face >= 0, face, FACES)] = arrived[(entry // 2) * stride + entry % 2 + offset]


class Lists:
    def __init__(self, even, from_even, from_odd, side):
        self.take_even = even if side else jnp.logical_not(even)
        self.from_even, self.from_odd = from_even, from_odd

    def at(self, i):
        return jnp.where(self.take_even, self.from_even[i], self.from_odd[i])

    def neighbour(self, slot, direction):
        return self.at(4 * slot + direction)

    def send(self, entry):
        return self.at(SEND + entry)

    def recv(self, entry):
        return self.at(RECV + entry)


def sheet_of(even, from_even, from_odd, kind, side):
    rows = slice(kind * SLOTS, (kind + 1) * SLOTS)
    pair = (from_even[rows], from_odd[rows])
    return jnp.where(even, *(pair if side else pair[::-1]))


def own_end(even, to_even, to_odd, kind, side):
    return sheet_of(even, to_even, to_odd, kind, side)


def fill_sheet(store, value):
    store[:SLOTS] = value
    store[SLOTS] = jnp.zeros(TILE, jnp.float32)


def pack_lines(sheets, lists, out, tile, stride):
    sub, lane = iotas(TILE)
    for peer in range(SLOTS):
        total = jnp.zeros(TILE, jnp.float32)
        row = 0
        for side in range(2):
            for i in range(2):
                face = lists[side].send(2 * peer + i)
                slot = jnp.where(face >= 0, jnp.maximum(face, 0) // 2, SLOTS)
                high = jnp.maximum(face, 0) % 2 == 1
                for store in sheets[side]:
                    line = store[slot]
                    low_line = line[0:1, :]
                    high_line = pltpu.roll(line, EDGE, 1)[7:8, :]
                    total = jnp.where(sub == row, jnp.where(high, high_line, low_line), total)
                    row += 1
        out[peer * stride + tile] = total


def place_lines(arrived, lists, edges, tile, stride):
    for pair in edges:
        for store in pair:
            store[...] = jnp.zeros(store.shape, jnp.float32)
    sub, lane = iotas(TILE)
    first = (sub == 0) & (lane < EDGE)
    final = (sub == 7) & (lane >= LANES - EDGE)
    for peer in range(SLOTS):
        got = arrived[peer * stride + tile]
        turned = pltpu.roll(got, LANES - EDGE, 1)
        row = 0
        for side in range(2):
            for i in range(2):
                ghost = lists[side].recv(2 * peer + i)
                slot = jnp.where(ghost >= 0, jnp.maximum(ghost, 0) // 2, SLOTS)
                high = jnp.maximum(ghost, 0) % 2 == 1
                for store in edges[side]:
                    low_part = jnp.where(first, got[row : row + 1, :], 0.0)
                    high_part = jnp.where(final, turned[row : row + 1, :], 0.0)
                    store[slot] = store[slot] + jnp.where(high, high_part, low_part)
                    row += 1


def sheet_around(store, inner, outer_tiles, edge, lists, side, gathered):
    shape = (SLOTS,) + TILE
    sub, lane = iotas(shape)
    x = lane % EDGE
    minus, plus, outer = gathered
    for slot in range(SLOTS):
        minus[slot] = store[slot_or(lists.neighbour(slot, 0), SLOTS)]
        plus[slot] = store[slot_or(lists.neighbour(slot, 1), SLOTS)]
        entry = lists.neighbour(slot, 2 if side else 3)
        outer[slot] = outer_tiles[slot_or(entry, 0)] * (entry >= 0).astype(jnp.float32)
    value = store[:SLOTS]
    edges = edge[:SLOTS]
    forth = pltpu.roll(value, EDGE, 2)
    back = pltpu.roll(value, LANES - EDGE, 2)
    before = jnp.where(lane < EDGE, pltpu.roll(forth, 1, 1), forth)
    after = jnp.where(lane >= LANES - EDGE, pltpu.roll(back, 7, 1), back)
    out = outer[...]
    return (
        jnp.where(x == 0, pltpu.roll(minus[...], LANES - EDGE + 1, 2), pltpu.roll(value, 1, 2)),
        jnp.where(x == EDGE - 1, pltpu.roll(plus[...], EDGE - 1, 2), pltpu.roll(value, LANES - 1, 2)),
        jnp.where((lane < EDGE) & (sub == 0), edges, before),
        jnp.where((lane >= LANES - EDGE) & (sub == 7), edges, after),
        out if side else inner,
        inner if side else out,
    )


def weights(k, around):
    faces = [0.5 * (k + jnp.where(other > 0.0, other, k)) for other in around]
    total = faces[0]
    for face in faces[1:]:
        total = total + face
    alive = k > 0.0
    weight = jnp.where(alive, OMEGA / jnp.where(alive, total, 1.0), 0.0)
    return [weight * face for face in faces], weight, jnp.where(alive, total * (1.0 / OMEGA), 0.0)


def six_neighbours(field, j, mine, ghost, below, above):
    _, lane = iotas((EDGE, LANES))
    x = lane % EDGE

    def scaled(side):
        entry = mine[4 * j + side]
        return slot_or(entry, 0), (entry >= 0).astype(jnp.float32)

    (xm, has_xm), (xp, has_xp), (zm, has_zm), (zp, has_zp) = [scaled(side) for side in range(4)]
    under_face, over_face = below[zm] * has_zm, above[zp] * has_zp
    own, minus_rows, plus_rows = block_rows(j), block_rows(xm), block_rows(xp)
    values = [field[own, column(c)] for c in range(COLS)]
    forth = [pltpu.roll(v, EDGE, 1) for v in values]
    back = [pltpu.roll(v, LANES - EDGE, 1) for v in values]
    forth.insert(0, unpack_face(ghost[2 * j], 0))
    back.append(unpack_face(ghost[2 * j + 1], 1))
    for c in range(COLS):
        v = values[c]
        left = field[minus_rows, column(c)] * has_xm
        right = field[plus_rows, column(c)] * has_xp
        yield (
            c,
            v,
            (
                jnp.where(x == 0, pltpu.roll(left, LANES - EDGE + 1, 1), pltpu.roll(v, 1, 1)),
                jnp.where(x == EDGE - 1, pltpu.roll(right, EDGE - 1, 1), pltpu.roll(v, LANES - 1, 1)),
                jnp.where(lane < EDGE, forth[c], forth[c + 1]),
                jnp.where(lane >= LANES - EDGE, back[c + 1], back[c]),
                jnp.concatenate([under_face[c : c + 1, :], v[: EDGE - 1]], axis=0),
                jnp.concatenate([v[1:], over_face[c : c + 1, :]], axis=0),
            ),
        )


def sweep_blocks(mine, v, wk, wf, u, ghost, below, above):
    def one(j, carry):
        rows = block_rows(j)
        for n, centre, around in six_neighbours(v, j, mine, ghost, below, above):
            total = wf[rows, column(n)] + (1.0 - OMEGA) * centre
            for d in range(6):
                total = total + wk[d, rows, column(n)] * around[d]
            u[rows, column(n)] = total
        return carry

    lax.fori_loop(0, SLOTS, one, 0)


def pair_slot(pairs, owner, bit):
    return pairs[0, owner[0] ^ (1 << bit)]


def early_tiles(v, f, c, row, out):
    for end in range(2):
        for kind, field, depth in ((V1, v, 0), (V2, v, 1), (C1, c, 0), (C2, c, 1), (F1, f, 0)):
            layer_tile(field, row + (depth if end else EDGE - 1 - depth), out, end * KINDS + kind)
    for k, field in enumerate((v, c)):
        for side in range(2):
            out[2 * KINDS + 2 * k + side] = face_tile(field, row, side)


def swap_pack_kernel(pairs, owner, occupied, guess, rhs, coef, *refs):
    early, bulk, sems = refs[:BITS], refs[BITS : 2 * BITS], refs[2 * BITS]
    slots = [jnp.maximum(pair_slot(pairs, owner, bit), 0) for bit in range(BITS)]

    def copies(bit):
        return [
            pltpu.make_async_copy(
                source.at[block_rows(slots[bit])], bulk[bit].at[pl.ds(k * EDGE, EDGE)], sems.at[bit, k]
            )
            for k, source in enumerate((guess, rhs, coef))
        ]

    for bit in range(BITS):
        for copy in copies(bit):
            copy.start()
    for bit in range(BITS):
        for copy in copies(bit):
            copy.wait()

        @pl.when(occupied[slots[bit]] == 0)
        def _(bit=bit):
            bulk[bit][...] = jnp.zeros((3 * EDGE, PLANE), jnp.float32)

        out = bulk[bit]
        early_tiles(
            out.at[pl.ds(0, EDGE)], out.at[pl.ds(EDGE, EDGE)], out.at[pl.ds(2 * EDGE, EDGE)], 0, early[bit]
        )


def swap_pack(fields, occupied, pairs, owner):
    outs = pl.pallas_call(
        swap_pack_kernel,
        in_specs=[SMEM] * 3 + [HBM] * 3,
        out_specs=[VMEM] * (2 * BITS),
        out_shape=[tiles(2 * KINDS + 4)] * BITS + [f32(3 * EDGE, PLANE)] * BITS,
        scratch_shapes=[pltpu.SemaphoreType.DMA((BITS, 3))],
        compiler_params=params(8),
        cost_estimate=cost(1 << 19, 3 << 20),
        name="swap_pack",
    )(pairs, owner, occupied, *fields)
    return outs[:BITS], outs[BITS:]


def local_kernel(occupied, guess, rhs, coef, top, bottom, faces, v, f, c, out, sems):
    copies = [
        pltpu.make_async_copy(source, target, sems.at[k])
        for k, (source, target) in enumerate(((guess, v), (rhs, f), (coef, c)))
    ]
    for copy in copies:
        copy.start()
    for copy in copies:
        copy.wait()
    for j in range(SLOTS):
        early_tiles(v, f, c, j * EDGE, out)
        alive = occupied[j].astype(jnp.float32)
        for kind in range(KINDS):
            top[kind * SLOTS + j] = out[kind] * alive
            bottom[kind * SLOTS + j] = out[KINDS + kind] * alive
        for k in range(2):
            for side in range(2):
                faces[k * FACES + 2 * j + side] = out[2 * KINDS + 2 * k + side] * alive


def local(fields, occupied):
    return pl.pallas_call(
        local_kernel,
        in_specs=[SMEM] + [HBM] * 3,
        out_specs=[VMEM] * 3,
        out_shape=[tiles(KINDS * SLOTS)] * 2 + [tiles(2 * FACES)],
        scratch_shapes=[scratch(*FIELD)] * 3 + [scratch(2 * KINDS + 4, *TILE), pltpu.SemaphoreType.DMA((3,))],
        compiler_params=params(8),
        cost_estimate=cost(1 << 20, 4 << 20),
        name="local",
    )(occupied, *fields)


def ends_kernel(pairs, owner, mine, parity, top, bottom, faces, *refs):
    early = refs[:BITS]
    ze, zo, ys, held = refs[BITS:]
    even = parity[0] == 0
    ze[...] = jnp.where(even, top[...], bottom[...])
    zo[...] = jnp.where(even, bottom[...], top[...])
    held[...] = faces[...]
    for bit in range(BITS):
        slot = pair_slot(pairs, owner, bit)

        @pl.when(slot >= 0)
        def _(bit=bit, slot=jnp.maximum(slot, 0)):
            fresh = early[bit]
            for kind in range(KINDS):
                high, low = fresh[kind], fresh[KINDS + kind]
                ze[kind * SLOTS + slot] = jnp.where(even, high, low)
                zo[kind * SLOTS + slot] = jnp.where(even, low, high)
            for k in range(2):
                for side in range(2):
                    held[k * FACES + 2 * slot + side] = fresh[2 * KINDS + 2 * k + side]

    for k in range(2):
        pick_faces(held.at[pl.ds(k * FACES, FACES)], mine, ys, 2 * k, 4)


def ends(top, bottom, faces, early, pairs, owner, mine, parity):
    return pl.pallas_call(
        ends_kernel,
        in_specs=[SMEM] * 4 + [VMEM] * (3 + BITS),
        out_specs=[VMEM] * 3,
        out_shape=[tiles(KINDS * SLOTS)] * 2 + [tiles(2 * FACES)],
        scratch_shapes=[scratch(2 * FACES, *TILE)],
        compiler_params=params(4),
        cost_estimate=cost(1 << 18, 1 << 20),
        name="ends",
    )(pairs, owner, mine, parity, top, bottom, faces, *early)


def first_kernel(
    pairs, owner, occupied, mine, parity, lists_e, lists_o, ie, io, ya, *refs
):
    bulk, fields = refs[:BITS], refs[BITS : BITS + 3]
    wk, wf, dg, u, ys, v, f, c, ghost, ghost_c, below, above, below_c, above_c, faces, sems = refs[BITS + 3 :]
    even = parity[0] == 0
    merged = (v, f, c)
    slots = [pair_slot(pairs, owner, bit) for bit in range(BITS)]
    for k in (2, 0, 1):
        for j in range(SLOTS):
            swapped = slots[0] == j
            for slot in slots[1:]:
                swapped = swapped | (slot == j)
            rows = pl.ds(j * EDGE, EDGE)

            @pl.when(jnp.logical_not(swapped))
            def _(k=k, rows=rows):
                pltpu.make_async_copy(fields[k].at[rows], merged[k].at[rows], sems.at[k]).start()

        for bit in range(BITS):

            @pl.when(slots[bit] >= 0)
            def _(k=k, bit=bit):
                pltpu.make_async_copy(
                    bulk[bit].at[pl.ds(k * EDGE, EDGE)],
                    merged[k].at[block_rows(jnp.maximum(slots[bit], 0))],
                    sems.at[k],
                ).start()

    sheets = ((below, below_c), (above, above_c))
    for side in range(2):
        for store, kind in zip(sheets[side], (V1, C1)):
            fill_sheet(store, sheet_of(even, ie, io, kind, side))
    place_faces(ya, mine, ghost, 0, 4)
    place_faces(ya, mine, ghost_c, 2, 4)
    lists = [Lists(even, lists_e, lists_o, side) for side in range(2)]
    pack_lines(sheets, lists, ys, 2, 3)

    def settle(k):
        pltpu.make_async_copy(fields[k], merged[k], sems.at[k]).wait()
        for j in range(SLOTS):
            swapped = slots[0] == j
            for slot in slots[1:]:
                swapped = swapped | (slot == j)

            @pl.when((occupied[j] == 0) & jnp.logical_not(swapped))
            def _(j=j):
                merged[k][j * EDGE : (j + 1) * EDGE, :] = jnp.zeros((EDGE, PLANE), jnp.float32)

    for k in (2, 0, 1):
        settle(k)

    def one(j, carry):
        rows = block_rows(j)
        for n, k, around in six_neighbours(c, j, mine, ghost_c, below_c, above_c):
            scaled, weight, inverse = weights(k, around)
            for d in range(6):
                wk[d, rows, column(n)] = scaled[d]
            wf[rows, column(n)] = weight * f[rows, column(n)]
            dg[rows, column(n)] = inverse
        return carry

    lax.fori_loop(0, SLOTS, one, 0)
    sweep_blocks(mine, v, wk, wf, u, ghost, below, above)
    all_faces(u, faces)
    pick_faces(faces, mine, ys, 0, 3)


SHEET = scratch(SLOTS + 1, *TILE)
GHOSTS = scratch(FACES + 1, *TILE)
GATHERED = [scratch(SLOTS, *TILE)] * 3


def first(pairs, owner, occupied, mine, parity, lists, ends_in, ya, bulk, fields):
    return pl.pallas_call(
        first_kernel,
        in_specs=[SMEM] * 7 + [VMEM] * 3 + [HBM] * (BITS + 3),
        out_specs=[VMEM] * 5,
        out_shape=[f32(6, *FIELD)] + [f32(*FIELD)] * 3 + [tiles(3 * SLOTS)],
        scratch_shapes=[scratch(*FIELD)] * 3
        + [GHOSTS] * 2
        + [SHEET] * 4
        + [scratch(FACES, *TILE), pltpu.SemaphoreType.DMA((3,))],
        compiler_params=params(20),
        cost_estimate=cost(1 << 24, 12 << 20),
        name="first",
    )(pairs, owner, occupied, mine, parity, *lists, *ends_in, ya, *bulk, *fields)


def second_kernel(
    mine, parity, lists_e, lists_o,
    v, wk, wf, ye, yo, ie, io, ya,
    u, ze, zo, ys, kept,
    ghost, below, above, below_c, above_c, edge_bv, edge_bc, edge_av, edge_ac, gm, gp, go, faces, ends_out,
):
    even = parity[0] == 0
    lists = [Lists(even, lists_e, lists_o, side) for side in range(2)]
    place_faces(ya, mine, ghost, 0, 3)
    edges = ((edge_bv, edge_bc), (edge_av, edge_ac))
    place_lines(ya, lists, edges, 2, 3)
    for side, (store, store_c) in enumerate(((below, below_c), (above, above_c))):
        fill_sheet(store, sheet_of(even, ie, io, V1, side))
        fill_sheet(store_c, sheet_of(even, ie, io, C1, side))
        k = store_c[:SLOTS]
        ends_out[...] = own_end(even, ye, yo, C1, side)
        inner = sheet_of(even, ie, io, C2, side)
        around = sheet_around(store_c, inner, ends_out, edges[side][1], lists[side], side, (gm, gp, go))
        scaled, weight, _ = weights(k, around)
        forced = weight * sheet_of(even, ie, io, F1, side)
        for d in range(6):
            kept[(side * 7 + d) * SLOTS : (side * 7 + d + 1) * SLOTS] = scaled[d]
        kept[(side * 7 + 6) * SLOTS : (side * 7 + 7) * SLOTS] = forced
        ends_out[...] = own_end(even, ye, yo, V1, side)
        inner = sheet_of(even, ie, io, V2, side)
        around = sheet_around(store, inner, ends_out, edges[side][0], lists[side], side, (gm, gp, go))
        total = forced + (1.0 - OMEGA) * store[:SLOTS]
        for d in range(6):
            total = total + scaled[d] * around[d]
        store[:SLOTS] = total
    sweep_blocks(mine, v, wk, wf, u, ghost, below, above)
    all_faces(u, faces)
    pick_faces(faces, mine, ys, 0, 2)
    for j in range(SLOTS):
        for depth in range(2):
            layer_tile(u, j * EDGE + EDGE - 1 - depth, ends_out, 0)
            layer_tile(u, j * EDGE + depth, ends_out, 1)
            ze[depth * SLOTS + j] = jnp.where(even, ends_out[0], ends_out[1])
            zo[depth * SLOTS + j] = jnp.where(even, ends_out[1], ends_out[0])


def second(v, wk, wf, sent, got, ya, mine, parity, lists):
    return pl.pallas_call(
        second_kernel,
        in_specs=[SMEM] * 4 + [VMEM] * 8,
        out_specs=[VMEM] * 5,
        out_shape=[f32(*FIELD), tiles(2 * SLOTS), tiles(2 * SLOTS), tiles(FACES), tiles(14 * SLOTS)],
        scratch_shapes=[GHOSTS] + [SHEET] * 8 + GATHERED + [scratch(FACES, *TILE), scratch(SLOTS, *TILE)],
        compiler_params=params(16),
        cost_estimate=cost(1 << 22, 9 << 20),
        name="second",
    )(mine, parity, *lists, v, wk, wf, *sent, *got, ya)


def third_kernel(
    mine, parity, lists_e, lists_o,
    v, wk, wf, ie, io, ya,
    u, ys,
    ghost, below, above, faces,
):
    even = parity[0] == 0
    lists = [Lists(even, lists_e, lists_o, side) for side in range(2)]
    place_faces(ya, mine, ghost, 0, 2)
    for side, store in enumerate((below, above)):
        fill_sheet(store, sheet_of(even, ie, io, V1, side))
    pack_lines(((below,), (above,)), lists, ys, 2, 3)
    sweep_blocks(mine, v, wk, wf, u, ghost, below, above)
    all_faces(u, faces)
    pick_faces(faces, mine, ys, 0, 3)


def third(v, wk, wf, got, ya, mine, parity, lists):
    return pl.pallas_call(
        third_kernel,
        in_specs=[SMEM] * 4 + [VMEM] * 6,
        out_specs=[VMEM] * 2,
        out_shape=[f32(*FIELD), tiles(3 * SLOTS)],
        scratch_shapes=[GHOSTS] + [SHEET] * 2 + [scratch(FACES, *TILE)],
        compiler_params=params(16),
        cost_estimate=cost(1 << 22, 9 << 20),
        name="third",
    )(mine, parity, *lists, v, wk, wf, *got, ya)


def last_kernel(
    mine, parity, lists_e, lists_o,
    v, wk, wf, dg, kept, ye, yo, ie, io, ya,
    out, coarse,
    ghost, below, above, edge_b, edge_a, gm, gp, go, ends_out, residual, sem,
):
    write = pltpu.make_async_copy(v, out, sem)
    write.start()
    even = parity[0] == 0
    lists = [Lists(even, lists_e, lists_o, side) for side in range(2)]
    place_faces(ya, mine, ghost, 0, 3)
    edges = ((edge_b,), (edge_a,))
    place_lines(ya, lists, edges, 2, 3)
    for side, store in enumerate((below, above)):
        fill_sheet(store, sheet_of(even, ie, io, V1, side))
        ends_out[...] = own_end(even, ye, yo, V1, side)
        inner = sheet_of(even, ie, io, V2, side)
        around = sheet_around(store, inner, ends_out, edges[side][0], lists[side], side, (gm, gp, go))
        total = kept[(side * 7 + 6) * SLOTS : (side * 7 + 7) * SLOTS] + (1.0 - OMEGA) * store[:SLOTS]
        for d in range(6):
            total = total + kept[(side * 7 + d) * SLOTS : (side * 7 + d + 1) * SLOTS] * around[d]
        store[:SLOTS] = total

    def one(j, carry):
        rows = block_rows(j)
        for n, centre, around in six_neighbours(v, j, mine, ghost, below, above):
            total = wf[rows, column(n)] - OMEGA * centre
            for d in range(6):
                total = total + wk[d, rows, column(n)] * around[d]
            residual[n, rows, :] = total * dg[rows, column(n)]
        return carry

    lax.fori_loop(0, SLOTS, one, 0)
    lane = lax.broadcasted_iota(jnp.int32, (LANES, LANES), 0)
    target = lax.broadcasted_iota(jnp.int32, (LANES, LANES), 1)
    place = (lane // (2 * EDGE)) * (EDGE // 2) + (lane % EDGE) // 2
    half = ROWS // 2
    for part in range(2):
        total = jnp.zeros((half, LANES), jnp.float32)
        for n in range(4):
            column_sum = (
                residual[part * 4 + n, pl.ds(0, half, stride=2), :]
                + residual[part * 4 + n, pl.ds(1, half, stride=2), :]
            )
            gather = jnp.where(place + EDGE * n == target, 0.125, 0.0)
            total = total + jnp.dot(
                column_sum, gather, precision=lax.Precision.HIGHEST, preferred_element_type=jnp.float32
            )
        coarse[:, part * LANES : (part + 1) * LANES] = total
    write.wait()


def last(v, wk, wf, dg, kept, sent, got, ya, mine, parity, lists):
    return pl.pallas_call(
        last_kernel,
        in_specs=[SMEM] * 4 + [VMEM] * 10,
        out_specs=[HBM, VMEM],
        out_shape=[f32(*FIELD), f32(ROWS // 2, PLANE // 4)],
        scratch_shapes=[GHOSTS] + [SHEET] * 4 + GATHERED + [scratch(SLOTS, *TILE), scratch(COLS, ROWS, LANES), pltpu.SemaphoreType.DMA],
        compiler_params=params(16),
        cost_estimate=cost(1 << 24, 10 << 20),
        name="last",
    )(mine, parity, *lists, v, wk, wf, dg, kept, *sent, *got, ya)


def pair_swap(values, stride):
    count = lax.axis_size("owner")
    return lax.ppermute(values, "owner", [(i, i ^ stride) for i in range(count)])


def odd_pair_swap(values):
    count = lax.axis_size("owner")
    return lax.ppermute(values, "owner", [(i, ((i - 1) ^ 1) + 1) for i in range(1, count - 1)])


def in_hbm(values):
    return pltpu.with_memory_space_constraint(values, pltpu.HBM)


def segment_swap(ys):
    return lax.all_to_all(ys, "sub", split_axis=0, concat_axis=0, tiled=True)


def body(guess, rhs, coef, occupied, neighbours, swap_slot, send_list, recv_list):
    my_owner = lax.axis_index("owner").astype(jnp.int32)
    owner = my_owner.reshape(1)
    parity = (my_owner % 2).reshape(1)
    fields = tuple(values.reshape(FIELD) for values in (guess, rhs, coef))
    fields = tuple(in_hbm(x) for x in fields)
    occupied, swap_slot = in_hbm(occupied), in_hbm(swap_slot)
    early, bulk = swap_pack(fields, occupied, swap_slot, owner)
    early = [pair_swap(early[bit], 1 << bit) for bit in range(BITS)]
    early, bulk = lax.optimization_barrier((early, bulk))
    bulk = [pair_swap(bulk[bit], 1 << bit) for bit in range(BITS)]
    mine = jnp.concatenate([neighbours.reshape(-1), send_list.reshape(-1), recv_list.reshape(-1)])
    lists = (pair_swap(mine, 1), odd_pair_swap(mine))
    top, bottom, faces = local(fields, occupied)
    ze, zo, ys = ends(top, bottom, faces, early, swap_slot, owner, mine, parity)
    sent, got, ya = (ze, zo), (pair_swap(ze, 1), odd_pair_swap(zo)), segment_swap(ys)
    wk, wf, dg, v, ys = first(
        swap_slot, owner, occupied, mine, parity, lists, got, ya, bulk, fields
    )
    v, ze, zo, ys, kept = second(
        v, wk, wf, sent, got, segment_swap(ys), mine, parity, lists
    )
    sent, got = (ze, zo), (pair_swap(ze, 1), odd_pair_swap(zo))
    v, ys = third(v, wk, wf, got, segment_swap(ys), mine, parity, lists)
    v, coarse = last(v, wk, wf, dg, kept, sent, got, segment_swap(ys), mine, parity, lists)
    return v.reshape(SLOTS, EDGE, PLANE), coarse.reshape(SLOTS, EDGE // 2, PLANE // 4)


def solution(mesh):
    wide, flat, single = P(("owner", "sub"), None, None), P(("owner", "sub"), None), P(("owner", "sub"))
    return jax.shard_map(
        body,
        mesh=mesh,
        in_specs=(wide, wide, wide, single, flat, flat, flat, flat),
        out_specs=(wide, wide),
        check_vma=False,
    )
```

time: 132 us -> 104 us (0.79)
  blocking collectives: 0 us -> 35.1 us
  local copies, waits for them, and re-layouts: 28.7 us -> 0.84 us
  waiting for transfers between devices: 30 us -> 10 us
  starting transfers between devices: 45.2 us -> 27.7 us
  Pallas kernels: 25.8 us -> 27.5 us
    all_to_all x0 -> x4, blocking collectives: none -> 35.1 us  [segment_swap(): return lax.all_to_all(ys, 'sub', split_axis=0, concat_axis=0, tiled=True)]
    unnamed x57 -> x1, local copies, waits for them, and re-layouts: 28.7 us -> 0.76 us
    all_to_all x4 -> x0, starting transfers between devices: 18.6 us -> none  [exchange(): arrived = lax.all_to_all(ys, 'sub', split_axis=0, concat_axis=0, tiled=True)]
    ppermute x4 -> x3, waiting for transfers between devices: 13 us -> 0.01 us  [odd_pair_swap(): lax.ppermute(values, 'owner', [(i, (i - 1 ^ 1) + 1) for i in range(1, cou...]
    ppermute x8 -> x11, waiting for transfers between devices: 17 us -> 10 us  [pair_swap(): lax.ppermute(values, 'owner', [(i, i ^ stride) for i in range(count)])]
    ppermute x8 -> x11, starting transfers between devices: 8 us -> 14.4 us  [pair_swap(): lax.ppermute(values, 'owner', [(i, i ^ stride) for i in range(count)])]
    ppermute x4 -> x3, starting transfers between devices: 18.5 us -> 13.4 us  [odd_pair_swap(): lax.ppermute(values, 'owner', [(i, (i - 1 ^ 1) + 1) for i in range(1, cou...]
    pallas_call x6 -> x7, Pallas kernels: 25.8 us -> 27.5 us  [the longest x1 8.82 us: first(): pl.pallas_call(first_kernel, in_specs=[SMEM] * 7 + [VMEM] * 3 + [HBM] * (...]
  transfers between devices with their start and end apart: 16 -> 14, of which waited for: 7 -> 3; matrix products, arithmetic and copies ran while one was open for 1% -> 2% of each run, Pallas kernels for 0% -> 4%
where the time goes in v1:
time: 104 us; the launch traced here: 103 us
  blocking collectives  35.1 us (34%)
  starting transfers between devices  27.7 us (27%)
  Pallas kernels  27.5 us (26%)
  waiting for transfers between devices  10 us (10%)
    all_to_all x4, blocking collectives, segment_swap(): return lax.all_to_all(ys, 'sub', split_axis=0, concat_axis=0, tiled=True)  35.1 us
    ppermute x11, starting transfers between devices, pair_swap(): lax.ppermute(values, 'owner', [(i, i ^ stride) for i in range(count)])  14.4 us
    ppermute x3, starting transfers between devices, odd_pair_swap(): lax.ppermute(values, 'owner', [(i, (i - 1 ^ 1) + 1) for i in range(1, cou...  13.4 us
    ppermute x11, waiting for transfers between devices, pair_swap(): lax.ppermute(values, 'owner', [(i, i ^ stride) for i in range(count)])  10 us
    pallas_call x1, Pallas kernels, first(): pl.pallas_call(first_kernel, in_specs=[SMEM] * 7 + [VMEM] * 3 + [HBM] * (...  8.82 us
    pallas_call x1, Pallas kernels, last(): pl.pallas_call(last_kernel, in_specs=[SMEM] * 4 + [VMEM] * 10, out_specs=...  4.61 us
    pallas_call x1, Pallas kernels, second(): pl.pallas_call(second_kernel, in_specs=[SMEM] * 4 + [VMEM] * 8, out_specs...  4.29 us
    pallas_call x1, Pallas kernels, third(): pl.pallas_call(third_kernel, in_specs=[SMEM] * 4 + [VMEM] * 6, out_specs=...  3.89 us
  transfers between devices with their start and end apart: 14, of which 3 were waited for; matrix products, arithmetic and copies ran while one was open for 2% of the time, Pallas kernels for 4%

profile of v1, /device:TPU:32, one launch (start us, length us, event | category | flops | bytes accessed | tf_op | source)
XLA Modules:
  0.0 102.8 jit_solution(11132863978791981524)
XLA Ops:
  0.6 2.3 %swap_pack.1 = (f32[14,8,128]{2,1,0:T(8,128)S(1)}, f32[14,8,128]{2,1,0:T(8,128)S(1)}, f32[14,8,128]{2,1,0:T(8,128)S(1)}, f32[14,8,128]{2,1,0:T(8,128)S(1)}, f32[...) custom-call(s32[1,16]{1,0:T(1,128)} %pairs.5, s32[1]{0:T(128)} %bitcast.3.owner, ...), custom_call_target="tpu_custom_call" | custom-call | flops 524288 | bytes 3145728 | tf_op jit(solution)/shard_map/swap_pack/pallas_call | solution.py:318
  3.0 1.7 %collective-permute-start.2 = (f32[14,8,128]{2,1,0:T(8,128)S(1)}, f32[14,8,128]{2,1,0:T(8,128)S(1)}, u32[]{:S(2)}, u32[]{:S(2)}) collective-permute-start(f32[14,8,128]{2,1,0:T(8,128)S(1)} %get-tuple-element.41), channel_id=1, source_target_pairs={{0,8},{8,0},{16,24},{24,16},{32,40},{40,32},{48,56},{56,48},{64,72... | collective-permute-start | bytes 172040 | tf_op jit(solution)/shard_map/ppermute | solution.py:642
  4.7 2.8 %collective-permute-start.3 = (f32[14,8,128]{2,1,0:T(8,128)S(1)}, f32[14,8,128]{2,1,0:T(8,128)S(1)}, u32[]{:S(2)}, u32[]{:S(2)}) collective-permute-start(f32[14,8,128]{2,1,0:T(8,128)S(1)} %get-tuple-element.42), channel_id=1, source_target_pairs={{0,16},{8,24},{16,0},{24,8},{32,48},{40,56},{48,32},{56,40},{64,80... | collective-permute-start | bytes 172040 | tf_op jit(solution)/shard_map/ppermute | solution.py:642
  7.5 0.1 collective-permute-start.4
  7.6 3.3 %collective-permute-start.5 = (f32[14,8,128]{2,1,0:T(8,128)S(1)}, f32[14,8,128]{2,1,0:T(8,128)S(1)}, u32[]{:S(2)}, u32[]{:S(2)}) collective-permute-start(f32[14,8,128]{2,1,0:T(8,128)S(1)} %get-tuple-element.44), channel_id=1, source_target_pairs={{0,64},{8,72},{16,80},{24,88},{32,96},{40,104},{48,112},{56,120},{... | collective-permute-start | bytes 172040 | tf_op jit(solution)/shard_map/ppermute | solution.py:642
  10.9 0.8 copy.11
  11.7 0.1 reshape.34
  11.8 1.9 %collective-permute-done.5.refs_3_ = f32[14,8,128]{2,1,0:T(8,128)S(1)} collective-permute-done((f32[14,8,128]{2,1,0:T(8,128)S(1)}, f32[14,8,128]{2,1,0:T(8,128)S(1)}, u32[]{:S(2)}, u32[]{:S(2)}) %collective-permute-start.5) | collective-permute-done | bytes 57376 | tf_op jit(solution)/shard_map/ppermute | solution.py:642
  13.7 0.1 collective-permute-start.8
  13.8 1.5 %collective-permute-start.9 = (f32[96,1024]{1,0:T(8,128)S(1)}, f32[96,1024]{1,0:T(8,128)S(1)}, u32[]{:S(2)}, u32[]{:S(2)}) collective-permute-start(f32[96,1024]{1,0:T(8,128)S(1)} %get-tuple-element.57), channel_id=1, source_target_pairs={{0,16},{8,24},{16,0},{24,8},{32,48},{40,56},{48,32},{56,40},{64,80... | collective-permute-start | bytes 1179656 | tf_op jit(solution)/shard_map/ppermute | solution.py:642
  15.4 2.2 %collective-permute-start.10 = (f32[96,1024]{1,0:T(8,128)S(1)}, f32[96,1024]{1,0:T(8,128)S(1)}, u32[]{:S(2)}, u32[]{:S(2)}) collective-permute-start(f32[96,1024]{1,0:T(8,128)S(1)} %get-tuple-element.58), channel_id=1, source_target_pairs={{0,32},{8,40},{16,48},{24,56},{32,0},{40,8},{48,16},{56,24},{64,96... | collective-permute-start | bytes 1179656 | tf_op jit(solution)/shard_map/ppermute | solution.py:642
  17.6 2.3 %collective-permute-start.11 = (f32[96,1024]{1,0:T(8,128)S(1)}, f32[96,1024]{1,0:T(8,128)S(1)}, u32[]{:S(2)}, u32[]{:S(2)}) collective-permute-start(f32[96,1024]{1,0:T(8,128)S(1)} %get-tuple-element.59), channel_id=1, source_target_pairs={{0,64},{8,72},{16,80},{24,88},{32,96},{40,104},{48,112},{56,120},{... | collective-permute-start | bytes 1179656 | tf_op jit(solution)/shard_map/ppermute | solution.py:642
  19.9 0.7 pad_add_fusion.mine
  20.7 5.4 %collective-permute-start.1 = (s32[64]{0:T(128)S(1)}, s32[64]{0:T(128)S(1)}, u32[]{:S(2)}, u32[]{:S(2)}) collective-permute-start(s32[64]{0:T(128)S(1)} %pad_add_fusion.mine), channel_id=1, source_target_pairs={{8,16},{16,8},{24,32},{32,24},{40,48},{48,40},{56,64},{64,56},{72,... | collective-permute-start | bytes 776 | tf_op jit(solution)/shard_map/ppermute | solution.py:647
  26.0 2.8 %local.1 = (f32[40,8,128]{2,1,0:T(8,128)S(1)}, f32[40,8,128]{2,1,0:T(8,128)S(1)}, f32[32,8,128]{2,1,0:T(8,128)S(1)}) custom-call(s32[8]{0:T(128)} %occupied.5, f32[256,1024]{1,0:T(8,128)} %bitcast.10, f32[256,1024]{1,0:T(8,128)} %bitcast.13, f32[256,1024]{1,0:T(8,128)} %bitcast.16), custom_call_target="tpu_custom_call" | custom-call | flops 1048576 | bytes 4194304 | tf_op jit(solution)/shard_map/local/pallas_call | solution.py:352
  28.9 0.0 collective-permute-done.1.lists_o
  28.9 0.1 collective-permute-start
  29.0 0.8 ends.1
  29.8 2.8 %collective-permute-done.lists_e = s32[64]{0:T(128)S(1)} collective-permute-done((s32[64]{0:T(128)S(1)}, s32[64]{0:T(128)S(1)}, u32[]{:S(2)}, u32[]{:S(2)}) %collective-permute-start) | collective-permute-done | bytes 288 | tf_op jit(solution)/shard_map/ppermute | solution.py:642
  32.6 5.3 %collective-permute-done.6.ie = f32[40,8,128]{2,1,0:T(8,128)S(1)} collective-permute-done((f32[40,8,128]{2,1,0:T(8,128)S(1)}, f32[40,8,128]{2,1,0:T(8,128)S(1)}, u32[]{:S(2)}, u32[]{:S(2)}) %collective-permute-start.6) | collective-permute-done | bytes 163872 | tf_op jit(solution)/shard_map/ppermute | solution.py:642
  37.9 4.6 %collective-permute-start.7 = (f32[40,8,128]{2,1,0:T(8,128)S(1)}, f32[40,8,128]{2,1,0:T(8,128)S(1)}, u32[]{:S(2)}, u32[]{:S(2)}) collective-permute-start(f32[40,8,128]{2,1,0:T(8,128)S(1)} %get-tuple-element.54.yo), channel_id=1, source_target_pairs={{8,16},{16,8},{24,32},{32,24},{40,48},{48,40},{56,64},{64,56},{72,... | collective-permute-start | bytes 491528 | tf_op jit(solution)/shard_map/ppermute | solution.py:647
  42.5 10.2 %all_to_all.20.ya = f32[32,8,128]{2,1,0:T(8,128)S(1)} all-to-all(f32[32,8,128]{2,1,0:T(8,128)S(1)} %get-tuple-element.55), channel_id=1, replica_groups=mesh['owner'=16,'sub'=8] {'sub'}, dimensions={0} | all-to-all | bytes 262144 | tf_op jit(solution)/shard_map/all_to_all | solution.py:655
  52.7 0.0 collective-permute-done.7.io
  52.7 8.8 %first.1 = (f32[6,256,1024]{2,1,0:T(8,128)S(1)}, f32[256,1024]{1,0:T(8,128)S(1)}, f32[256,1024]{1,0:T(8,128)S(1)}, f32[256,1024]{1,0:T(8,128)S(1)}, f32[24,8,128]{2,1,0:T(8,128)S(1)}) custom-call(s32[1,16]{1,0:T(1,128)} %pairs.5, s32[1]{0:T(128)} %bitcast.3.owner, s32[8]{0:T(128)} %occupied.5, s32[64]{0:T(128)S(1)} %pad_add_fusion.mine, s32[1]{0:T(128)} %bitcast.2.parity, ...), custom_call_target="tpu_custom_call" | custom-call | flops 16777216 | bytes 12582912 | tf_op jit(solution)/shard_map/first/pallas_call | solution.py:476
  61.5 8.7 %all_to_all.21.ya = f32[24,8,128]{2,1,0:T(8,128)S(1)} all-to-all(f32[24,8,128]{2,1,0:T(8,128)S(1)} %get-tuple-element.63), channel_id=1, replica_groups=mesh['owner'=16,'sub'=8] {'sub'}, dimensions={0} | all-to-all | bytes 196608 | tf_op jit(solution)/shard_map/all_to_all | solution.py:655
  70.2 4.3 %second.1 = (f32[256,1024]{1,0:T(8,128)S(1)}, f32[16,8,128]{2,1,0:T(8,128)S(1)}, f32[16,8,128]{2,1,0:T(8,128)S(1)}, f32[16,8,128]{2,1,0:T(8,128)S(1)}, f32[112,8,128]{2,1,0:T(8,128)S(1)}) custom-call(s32[64]{0:T(128)S(1)} %pad_add_fusion.mine, s32[1]{0:T(128)} %bitcast.2.parity, s32[64]{0:T(128)S(1)} %collective-permute-done.lists_e, ...), custom_call_target="tpu_custom_call" | custom-call | flops 4194304 | bytes 9437184 | tf_op jit(solution)/shard_map/second/pallas_call | solution.py:533
  74.5 0.1 collective-permute-start.12
  74.6 3.4 %collective-permute-start.13 = (f32[16,8,128]{2,1,0:T(8,128)S(1)}, f32[16,8,128]{2,1,0:T(8,128)S(1)}, u32[]{:S(2)}, u32[]{:S(2)}) collective-permute-start(f32[16,8,128]{2,1,0:T(8,128)S(1)} %get-tuple-element.66.yo), channel_id=1, source_target_pairs={{8,16},{16,8},{24,32},{32,24},{40,48},{48,40},{56,64},{64,56},{72,... | collective-permute-start | bytes 196616 | tf_op jit(solution)/shard_map/ppermute | solution.py:647
  78.1 8.0 %all_to_all.22.ya = f32[16,8,128]{2,1,0:T(8,128)S(1)} all-to-all(f32[16,8,128]{2,1,0:T(8,128)S(1)} %get-tuple-element.67), channel_id=1, replica_groups=mesh['owner'=16,'sub'=8] {'sub'}, dimensions={0} | all-to-all | bytes 131072 | tf_op jit(solution)/shard_map/all_to_all | solution.py:655
  86.1 3.9 %third.1 = (f32[256,1024]{1,0:T(8,128)S(1)}, f32[24,8,128]{2,1,0:T(8,128)S(1)}) custom-call(s32[64]{0:T(128)S(1)} %pad_add_fusion.mine, s32[1]{0:T(128)} %bitcast.2.parity, s32[64]{0:T(128)S(1)} %collective-permute-done.lists_e, s32[64]{0:T(128)S(1)} %collective-permute-done.1.lists_o, f32[256,1024]{1,0:T(8,128)S(1)} %get-tuple-element.64.v, ...), custom_call_target="tpu_custom_call" | custom-call | flops 4194304 | bytes 9437184 | tf_op jit(solution)/shard_map/third/pallas_call | solution.py:563
  90.0 8.2 %all_to_all.23.ya = f32[24,8,128]{2,1,0:T(8,128)S(1)} all-to-all(f32[24,8,128]{2,1,0:T(8,128)S(1)} %get-tuple-element.71), channel_id=1, replica_groups=mesh['owner'=16,'sub'=8] {'sub'}, dimensions={0} | all-to-all | bytes 196608 | tf_op jit(solution)/shard_map/all_to_all | solution.py:655
  98.1 4.6 %last.1 = (f32[256,1024]{1,0:T(8,128)}, f32[128,256]{1,0:T(8,128)}) custom-call(s32[64]{0:T(128)S(1)} %pad_add_fusion.mine, s32[1]{0:T(128)} %bitcast.2.parity, s32[64]{0:T(128)S(1)} %collective-permute-done.lists_e, s32[64]{0:T(128)S(1)} %collective-permute-done.1.lists_o, f32[256,1024]{1,0:T(8,128)S(1)} %get-tuple-element.68.v, ...), custom_call_target="tpu_custom_call" | custom-call | flops 16777216 | bytes 10485760 | tf_op jit(solution)/shard_map/last/pallas_call | solution.py:628
  (10 shorter events, 0.0 us)
Async XLA Ops:
  3.0 8.8 %collective-permute-start.2 = (f32[14,8,128]{2,1,0:T(8,128)S(1)}, f32[14,8,128]{2,1,0:T(8,128)S(1)}, u32[]{:S(2)}, u32[]{:S(2)}) collective-permute-start(f32[14,8,128]{2,1,0:T(8,128)S(1)} %get-tuple-element.41), channel_id=1, source_target_pairs={{0,8},{8,0},{16,24},{24,16},{32,40},{40,32},{48,56},{56,48},{64,72... | collective-permute-start | bytes 172040 | tf_op jit(solution)/shard_map/ppermute | solution.py:642
  4.7 7.1 %collective-permute-start.3 = (f32[14,8,128]{2,1,0:T(8,128)S(1)}, f32[14,8,128]{2,1,0:T(8,128)S(1)}, u32[]{:S(2)}, u32[]{:S(2)}) collective-permute-start(f32[14,8,128]{2,1,0:T(8,128)S(1)} %get-tuple-element.42), channel_id=1, source_target_pairs={{0,16},{8,24},{16,0},{24,8},{32,48},{40,56},{48,32},{56,40},{64,80... | collective-permute-start | bytes 172040 | tf_op jit(solution)/shard_map/ppermute | solution.py:642
  7.5 4.3 %collective-permute-start.4 = (f32[14,8,128]{2,1,0:T(8,128)S(1)}, f32[14,8,128]{2,1,0:T(8,128)S(1)}, u32[]{:S(2)}, u32[]{:S(2)}) collective-permute-start(f32[14,8,128]{2,1,0:T(8,128)S(1)} %get-tuple-element.43), channel_id=1, source_target_pairs={{0,32},{8,40},{16,48},{24,56},{32,0},{40,8},{48,16},{56,24},{64,96... | collective-permute-start | bytes 172040 | tf_op jit(solution)/shard_map/ppermute | solution.py:642
  7.6 6.1 %collective-permute-start.5 = (f32[14,8,128]{2,1,0:T(8,128)S(1)}, f32[14,8,128]{2,1,0:T(8,128)S(1)}, u32[]{:S(2)}, u32[]{:S(2)}) collective-permute-start(f32[14,8,128]{2,1,0:T(8,128)S(1)} %get-tuple-element.44), channel_id=1, source_target_pairs={{0,64},{8,72},{16,80},{24,88},{32,96},{40,104},{48,112},{56,120},{... | collective-permute-start | bytes 172040 | tf_op jit(solution)/shard_map/ppermute | solution.py:642
  13.7 39.0 %collective-permute-start.8 = (f32[96,1024]{1,0:T(8,128)S(1)}, f32[96,1024]{1,0:T(8,128)S(1)}, u32[]{:S(2)}, u32[]{:S(2)}) collective-permute-start(f32[96,1024]{1,0:T(8,128)S(1)} %get-tuple-element.56), channel_id=1, source_target_pairs={{0,8},{8,0},{16,24},{24,16},{32,40},{40,32},{48,56},{56,48},{64,72... | collective-permute-start | bytes 1179656 | tf_op jit(solution)/shard_map/ppermute | solution.py:642
  13.8 38.9 %collective-permute-start.9 = (f32[96,1024]{1,0:T(8,128)S(1)}, f32[96,1024]{1,0:T(8,128)S(1)}, u32[]{:S(2)}, u32[]{:S(2)}) collective-permute-start(f32[96,1024]{1,0:T(8,128)S(1)} %get-tuple-element.57), channel_id=1, source_target_pairs={{0,16},{8,24},{16,0},{24,8},{32,48},{40,56},{48,32},{56,40},{64,80... | collective-permute-start | bytes 1179656 | tf_op jit(solution)/shard_map/ppermute | solution.py:642
  15.4 37.3 %collective-permute-start.10 = (f32[96,1024]{1,0:T(8,128)S(1)}, f32[96,1024]{1,0:T(8,128)S(1)}, u32[]{:S(2)}, u32[]{:S(2)}) collective-permute-start(f32[96,1024]{1,0:T(8,128)S(1)} %get-tuple-element.58), channel_id=1, source_target_pairs={{0,32},{8,40},{16,48},{24,56},{32,0},{40,8},{48,16},{56,24},{64,96... | collective-permute-start | bytes 1179656 | tf_op jit(solution)/shard_map/ppermute | solution.py:642
  17.6 35.1 %collective-permute-start.11 = (f32[96,1024]{1,0:T(8,128)S(1)}, f32[96,1024]{1,0:T(8,128)S(1)}, u32[]{:S(2)}, u32[]{:S(2)}) collective-permute-start(f32[96,1024]{1,0:T(8,128)S(1)} %get-tuple-element.59), channel_id=1, source_target_pairs={{0,64},{8,72},{16,80},{24,88},{32,96},{40,104},{48,112},{56,120},{... | collective-permute-start | bytes 1179656 | tf_op jit(solution)/shard_map/ppermute | solution.py:642
  20.7 8.2 %collective-permute-start.1 = (s32[64]{0:T(128)S(1)}, s32[64]{0:T(128)S(1)}, u32[]{:S(2)}, u32[]{:S(2)}) collective-permute-start(s32[64]{0:T(128)S(1)} %pad_add_fusion.mine), channel_id=1, source_target_pairs={{8,16},{16,8},{24,32},{32,24},{40,48},{48,40},{56,64},{64,56},{72,... | collective-permute-start | bytes 776 | tf_op jit(solution)/shard_map/ppermute | solution.py:647
  28.9 3.7 %collective-permute-start = (s32[64]{0:T(128)S(1)}, s32[64]{0:T(128)S(1)}, u32[]{:S(2)}, u32[]{:S(2)}) collective-permute-start(s32[64]{0:T(128)S(1)} %pad_add_fusion.mine), channel_id=1, source_target_pairs={{0,8},{8,0},{16,24},{24,16},{32,40},{40,32},{48,56},{56,48},{64,72... | collective-permute-start | bytes 776 | tf_op jit(solution)/shard_map/ppermute | solution.py:642
  32.6 5.3 %collective-permute-start.6 = (f32[40,8,128]{2,1,0:T(8,128)S(1)}, f32[40,8,128]{2,1,0:T(8,128)S(1)}, u32[]{:S(2)}, u32[]{:S(2)}) collective-permute-start(f32[40,8,128]{2,1,0:T(8,128)S(1)} %get-tuple-element.53.ye), channel_id=1, source_target_pairs={{0,8},{8,0},{16,24},{24,16},{32,40},{40,32},{48,56},{56,48},{64,72... | collective-permute-start | bytes 491528 | tf_op jit(solution)/shard_map/ppermute | solution.py:642
  37.9 14.8 %collective-permute-start.7 = (f32[40,8,128]{2,1,0:T(8,128)S(1)}, f32[40,8,128]{2,1,0:T(8,128)S(1)}, u32[]{:S(2)}, u32[]{:S(2)}) collective-permute-start(f32[40,8,128]{2,1,0:T(8,128)S(1)} %get-tuple-element.54.yo), channel_id=1, source_target_pairs={{8,16},{16,8},{24,32},{32,24},{40,48},{48,40},{56,64},{64,56},{72,... | collective-permute-start | bytes 491528 | tf_op jit(solution)/shard_map/ppermute | solution.py:647
  74.5 11.5 %collective-permute-start.12 = (f32[16,8,128]{2,1,0:T(8,128)S(1)}, f32[16,8,128]{2,1,0:T(8,128)S(1)}, u32[]{:S(2)}, u32[]{:S(2)}) collective-permute-start(f32[16,8,128]{2,1,0:T(8,128)S(1)} %get-tuple-element.65.ye), channel_id=1, source_target_pairs={{0,8},{8,0},{16,24},{24,16},{32,40},{40,32},{48,56},{56,48},{64,72... | collective-permute-start | bytes 196616 | tf_op jit(solution)/shard_map/ppermute | solution.py:642
  74.6 11.4 %collective-permute-start.13 = (f32[16,8,128]{2,1,0:T(8,128)S(1)}, f32[16,8,128]{2,1,0:T(8,128)S(1)}, u32[]{:S(2)}, u32[]{:S(2)}) collective-permute-start(f32[16,8,128]{2,1,0:T(8,128)S(1)} %get-tuple-element.66.yo), channel_id=1, source_target_pairs={{8,16},{16,8},{24,32},{32,24},{40,48},{48,40},{56,64},{64,56},{72,... | collective-permute-start | bytes 196616 | tf_op jit(solution)/shard_map/ppermute | solution.py:647

commit v2 on v1

v2 whole, which is shorter than its diff:
```python
import jax
import jax.numpy as jnp
from jax import lax
from jax.experimental import pallas as pl
from jax.experimental.pallas import tpu as pltpu
from jax.sharding import PartitionSpec as P

OMEGA = 0.8
SLOTS = 8
EDGE = 32
PLANE = EDGE * EDGE
ROWS = SLOTS * EDGE
LANES = 128
COLS = PLANE // LANES
FIELD = (ROWS, PLANE)
TURNED = (ROWS + EDGE, PLANE)
FACES = 2 * SLOTS
TILE = (8, LANES)
BITS = 4
V1, V2, C1, C2, F1 = range(5)
KINDS = 5
SEND = 4 * SLOTS
RECV = SEND + FACES
LISTS = RECV + FACES
SMEM = pl.BlockSpec(memory_space=pltpu.SMEM)
VMEM = pl.BlockSpec(memory_space=pltpu.VMEM)
HBM = pl.BlockSpec(memory_space=pltpu.HBM)


def f32(*shape):
    return jax.ShapeDtypeStruct(shape, jnp.float32)


def tiles(count):
    return f32(count, *TILE)


def scratch(*shape):
    return pltpu.VMEM(shape, jnp.float32)


def params(mib):
    return pltpu.CompilerParams(vmem_limit_bytes=mib << 20)


def cost(flops, bytes_accessed):
    return pl.CostEstimate(flops=flops, bytes_accessed=bytes_accessed, transcendentals=0)


def column(c):
    return slice(c * LANES, (c + 1) * LANES)


def block_rows(j):
    return pl.ds(pl.multiple_of(j * EDGE, EDGE), EDGE)


def iotas(shape):
    rank = len(shape)
    sub = lax.broadcasted_iota(jnp.int32, shape, rank - 2)
    lane = lax.broadcasted_iota(jnp.int32, shape, rank - 1)
    return sub, lane


def slot_or(entry, none):
    return jnp.where(entry >= 0, jnp.maximum(entry, 0) % SLOTS, none)


def layer_tile(field, row, out, index):
    for c in range(COLS):
        out[index, c : c + 1, :] = field[row : row + 1, column(c)]


def face_of(cells, side, forth=None, back=None):
    group = lax.broadcasted_iota(jnp.int32, TILE, 1) // EDGE
    turned = {0: cells, EDGE: forth, LANES - EDGE: back}
    face = None
    for g in range(4):
        turn = (EDGE * g + EDGE * side) % LANES
        rows = slice(8 * g, 8 * g + 8)
        done = turned.get(turn)
        part = pltpu.roll(cells[rows], turn, 1) if done is None else done[rows]
        face = part if face is None else jnp.where(group == g, part, face)
    return face


def face_tile(field, first_row, side):
    return face_of(field[first_row : first_row + EDGE, column(COLS - 1 if side else 0)], side)


def unpack_face(face, side):
    parts = []
    for g in range(4):
        turn = (-EDGE * g - EDGE * side) % LANES
        parts.append(pltpu.roll(face, turn, 1) if turn else face)
    return jnp.concatenate(parts, axis=0)


def pick_faces(faces, mine, out, offset, stride):
    for entry in range(FACES):
        face = mine[SEND + entry]
        out[(entry // 2) * stride + entry % 2 + offset] = faces[jnp.maximum(face, 0)] * (face >= 0).astype(
            jnp.float32
        )


def place_faces(arrived, mine, ghost, offset, stride):
    ghost[...] = jnp.zeros(ghost.shape, jnp.float32)
    for entry in range(FACES):
        face = mine[RECV + entry]
        ghost[jnp.where(face >= 0, face, FACES)] = arrived[(entry // 2) * stride + entry % 2 + offset]


class Lists:
    def __init__(self, lists, side):
        self.lists, self.side = lists, side

    def at(self, i):
        return self.lists[self.side, i]

    def neighbour(self, slot, direction):
        return self.at(4 * slot + direction)

    def send(self, entry):
        return self.at(SEND + entry)

    def recv(self, entry):
        return self.at(RECV + entry)


def lists_tile(mine):
    sub, lane = iotas(TILE)
    tile = jnp.zeros(TILE, jnp.float32)
    for i in range(LISTS):
        tile = jnp.where(lane == i, mine[i].astype(jnp.float32), tile)
    return jnp.where(sub == 0, tile, 0.0)


def list_copies(ie, io, held, sems):
    return [
        pltpu.make_async_copy(source.at[KINDS * SLOTS], held.at[k], sems.at[k]) for k, source in enumerate((ie, io))
    ]


def read_lists(even, held, lists):
    for side in range(2):
        source = jnp.where(even, 1 - side, side)
        for i in range(LISTS):
            lists[side, i] = held[source, 0, i].astype(jnp.int32)
    return [Lists(lists, side) for side in range(2)]


def sheet_of(even, from_even, from_odd, kind, side):
    rows = slice(kind * SLOTS, (kind + 1) * SLOTS)
    pair = (from_even[rows], from_odd[rows])
    return jnp.where(even, *(pair if side else pair[::-1]))


def own_end(even, to_even, to_odd, kind, side):
    return sheet_of(even, to_even, to_odd, kind, side)


def fill_sheet(store, value):
    store[:SLOTS] = value
    store[SLOTS] = jnp.zeros(TILE, jnp.float32)


def pack_lines(sheets, lists, out, tile, stride):
    sub, lane = iotas(TILE)
    for peer in range(SLOTS):
        total = jnp.zeros(TILE, jnp.float32)
        row = 0
        for side in range(2):
            for i in range(2):
                face = lists[side].send(2 * peer + i)
                slot = jnp.where(face >= 0, jnp.maximum(face, 0) // 2, SLOTS)
                high = jnp.maximum(face, 0) % 2 == 1
                for store in sheets[side]:
                    line = store[slot]
                    low_line = line[0:1, :]
                    high_line = pltpu.roll(line, EDGE, 1)[7:8, :]
                    total = jnp.where(sub == row, jnp.where(high, high_line, low_line), total)
                    row += 1
        out[peer * stride + tile] = total


def place_lines(arrived, lists, edges, tile, stride):
    for pair in edges:
        for store in pair:
            store[...] = jnp.zeros(store.shape, jnp.float32)
    sub, lane = iotas(TILE)
    first = (sub == 0) & (lane < EDGE)
    final = (sub == 7) & (lane >= LANES - EDGE)
    for peer in range(SLOTS):
        got = arrived[peer * stride + tile]
        turned = pltpu.roll(got, LANES - EDGE, 1)
        row = 0
        for side in range(2):
            for i in range(2):
                ghost = lists[side].recv(2 * peer + i)
                slot = jnp.where(ghost >= 0, jnp.maximum(ghost, 0) // 2, SLOTS)
                high = jnp.maximum(ghost, 0) % 2 == 1
                for store in edges[side]:
                    low_part = jnp.where(first, got[row : row + 1, :], 0.0)
                    high_part = jnp.where(final, turned[row : row + 1, :], 0.0)
                    store[slot] = store[slot] + jnp.where(high, high_part, low_part)
                    row += 1


def sheet_around(store, inner, outer_tiles, edge, lists, side, gathered):
    shape = (SLOTS,) + TILE
    sub, lane = iotas(shape)
    x = lane % EDGE
    minus, plus, outer = gathered
    for slot in range(SLOTS):
        minus[slot] = store[slot_or(lists.neighbour(slot, 0), SLOTS)]
        plus[slot] = store[slot_or(lists.neighbour(slot, 1), SLOTS)]
        entry = lists.neighbour(slot, 2 if side else 3)
        outer[slot] = outer_tiles[slot_or(entry, 0)] * (entry >= 0).astype(jnp.float32)
    value = store[:SLOTS]
    edges = edge[:SLOTS]
    forth = pltpu.roll(value, EDGE, 2)
    back = pltpu.roll(value, LANES - EDGE, 2)
    before = jnp.where(lane < EDGE, pltpu.roll(forth, 1, 1), forth)
    after = jnp.where(lane >= LANES - EDGE, pltpu.roll(back, 7, 1), back)
    out = outer[...]
    return (
        jnp.where(x == 0, pltpu.roll(minus[...], LANES - EDGE + 1, 2), pltpu.roll(value, 1, 2)),
        jnp.where(x == EDGE - 1, pltpu.roll(plus[...], EDGE - 1, 2), pltpu.roll(value, LANES - 1, 2)),
        jnp.where((lane < EDGE) & (sub == 0), edges, before),
        jnp.where((lane >= LANES - EDGE) & (sub == 7), edges, after),
        out if side else inner,
        inner if side else out,
    )


def weights(k, around):
    faces = [0.5 * (k + jnp.where(other > 0.0, other, k)) for other in around]
    total = faces[0]
    for face in faces[1:]:
        total = total + face
    alive = k > 0.0
    weight = jnp.where(alive, OMEGA / jnp.where(alive, total, 1.0), 0.0)
    return [weight * face for face in faces], weight, jnp.where(alive, total * (1.0 / OMEGA), 0.0)


def six_turned(field, forth, back, j, mine, ghost, below, above):
    _, lane = iotas((EDGE, LANES))
    x = lane % EDGE
    xm, xp, zm, zp = [slot_or(mine[4 * j + side], SLOTS) for side in range(4)]
    under_face, over_face = below[zm], above[zp]
    own, minus_rows, plus_rows = block_rows(j), block_rows(xm), block_rows(xp)
    for c in range(COLS):
        v = field[own, column(c)]
        before = forth[own, column(c - 1)] if c else unpack_face(ghost[2 * j], 0)
        after = back[own, column(c + 1)] if c < COLS - 1 else unpack_face(ghost[2 * j + 1], 1)
        yield (
            c,
            v,
            (
                pltpu.roll(jnp.where(x == EDGE - 1, back[minus_rows, column(c)], v), 1, 1),
                pltpu.roll(jnp.where(x == 0, forth[plus_rows, column(c)], v), LANES - 1, 1),
                jnp.where(lane < EDGE, before, forth[own, column(c)]),
                jnp.where(lane >= LANES - EDGE, after, back[own, column(c)]),
                jnp.concatenate([under_face[c : c + 1, :], v[: EDGE - 1]], axis=0),
                jnp.concatenate([v[1:], over_face[c : c + 1, :]], axis=0),
            ),
        )


def store_swept(total, n, j, u, forth, back, faces):
    rows = block_rows(j)
    ahead, behind = pltpu.roll(total, EDGE, 1), pltpu.roll(total, LANES - EDGE, 1)
    u[rows, column(n)] = total
    forth[rows, column(n)] = ahead
    back[rows, column(n)] = behind
    if n in (0, COLS - 1):
        side = n // (COLS - 1)
        faces[2 * j + side] = face_of(total, side, ahead, behind)


def turn_block(field, j, forth, back):
    rows = block_rows(j)
    for c in range(COLS):
        cells = field[rows, column(c)]
        forth[rows, column(c)] = pltpu.roll(cells, EDGE, 1)
        back[rows, column(c)] = pltpu.roll(cells, LANES - EDGE, 1)


def end_turned(forth, back):
    for turned in (forth, back):
        turned[ROWS:, :] = jnp.zeros((EDGE, PLANE), jnp.float32)


def sweep_blocks(turned, mine, ghost, below, above, wk, wf, u, forth, back, faces):
    def one(j, carry):
        rows = block_rows(j)
        for n, centre, around in six_turned(*turned, j, mine, ghost, below, above):
            total = wf[rows, column(n)] + (1.0 - OMEGA) * centre
            for d in range(6):
                total = total + wk[d, rows, column(n)] * around[d]
            store_swept(total, n, j, u, forth, back, faces)
        return carry

    lax.fori_loop(0, SLOTS, one, 0)
    end_turned(forth, back)


def pair_slot(pairs, owner, bit):
    return pairs[0, owner[0] ^ (1 << bit)]


def block_tiles(v, f, c, row, out):
    for end in range(2):
        for kind, field, depth in ((V1, v, 0), (V2, v, 1), (C1, c, 0), (C2, c, 1), (F1, f, 0)):
            layer_tile(field, row + (depth if end else EDGE - 1 - depth), out, end * KINDS + kind)
    for k, field in enumerate((v, c)):
        for side in range(2):
            out[2 * KINDS + 2 * k + side] = face_tile(field, row, side)


def swap_pack_kernel(bits, pairs, owner, occupied, guess, rhs, coef, *refs):
    bulk, sems = refs[: len(bits)], refs[len(bits)]
    slots = [jnp.maximum(pair_slot(pairs, owner, bit), 0) for bit in bits]

    def copies(n):
        return [
            pltpu.make_async_copy(
                source.at[block_rows(slots[n])], bulk[n].at[pl.ds(k * EDGE, EDGE)], sems.at[n, k]
            )
            for k, source in enumerate((guess, rhs, coef))
        ]

    for n in range(len(bits)):
        for copy in copies(n):
            copy.start()
    for n in range(len(bits)):
        for copy in copies(n):
            copy.wait()

        @pl.when(occupied[slots[n]] == 0)
        def _(n=n):
            bulk[n][...] = jnp.zeros((3 * EDGE, PLANE), jnp.float32)


def swap_pack(fields, occupied, pairs, owner, bits):
    return pl.pallas_call(
        lambda *refs: swap_pack_kernel(bits, *refs),
        in_specs=[SMEM] * 3 + [HBM] * 3,
        out_specs=[VMEM] * len(bits),
        out_shape=[f32(3 * EDGE, PLANE)] * len(bits),
        scratch_shapes=[pltpu.SemaphoreType.DMA((len(bits), 3))],
        compiler_params=params(8),
        cost_estimate=cost(1 << 19, len(bits) * (768 << 10)),
        name="swap_pack",
    )(pairs, owner, occupied, *fields)


def local_kernel(
    occupied, neighbours, send_list, recv_list, guess, rhs, coef, top, bottom, faces, mine, v, f, c, forth_v, back_v, forth_c, back_c, sems
):
    copies = [
        pltpu.make_async_copy(source, target, sems.at[k])
        for k, (source, target) in enumerate(((guess, v), (coef, c), (rhs, f)))
    ]
    for copy in copies:
        copy.start()
    for slot in range(SLOTS):
        for side in range(4):
            mine[4 * slot + side] = neighbours[slot, side]
    for entry in range(FACES):
        mine[SEND + entry] = send_list[0, entry]
        mine[RECV + entry] = recv_list[0, entry]
    for k, (field, kinds) in enumerate(((v, (V1, V2)), (c, (C1, C2)), (f, (F1,)))):
        copies[k].wait()
        for j in range(SLOTS):

            @pl.when(occupied[j] == 0)
            def _(field=field, j=j):
                field[j * EDGE : (j + 1) * EDGE, :] = jnp.zeros((EDGE, PLANE), jnp.float32)

        for j in range(SLOTS):
            for depth, kind in enumerate(kinds):
                for end, out in enumerate((top, bottom)):
                    row = j * EDGE + (depth if end else EDGE - 1 - depth)
                    layer_tile(field, row, out, kind * SLOTS + j)
            if len(kinds) == 2:
                for side in range(2):
                    faces[k * FACES + 2 * j + side] = face_tile(field, j * EDGE, side)
    for field, forth, back in ((v, forth_v, back_v), (c, forth_c, back_c)):

        def one(j, carry, field=field, forth=forth, back=back):
            turn_block(field, j, forth, back)
            return carry

        lax.fori_loop(0, SLOTS, one, 0)
        end_turned(forth, back)


def local(fields, occupied, neighbours, send_list, recv_list):
    return pl.pallas_call(
        local_kernel,
        in_specs=[SMEM] * 4 + [HBM] * 3,
        out_specs=[VMEM] * 3 + [SMEM] + [VMEM] * 7,
        out_shape=[tiles(KINDS * SLOTS)] * 2
        + [tiles(2 * FACES), jax.ShapeDtypeStruct((LISTS,), jnp.int32)]
        + [f32(*FIELD)] * 3
        + [f32(*TURNED)] * 4,
        scratch_shapes=[pltpu.SemaphoreType.DMA((3,))],
        compiler_params=params(8),
        cost_estimate=cost(1 << 20, 4 << 20),
        name="local",
    )(occupied, neighbours, send_list, recv_list, *fields)


def ends_kernel(pairs, owner, mine, parity, top, bottom, faces, *refs):
    bulk = refs[:BITS]
    ze, zo, ys, held, fresh = refs[BITS:]
    even = parity[0] == 0
    ze[: KINDS * SLOTS] = jnp.where(even, top[...], bottom[...])
    zo[: KINDS * SLOTS] = jnp.where(even, bottom[...], top[...])
    ze[KINDS * SLOTS] = zo[KINDS * SLOTS] = lists_tile(mine)
    held[...] = faces[...]
    for bit in range(BITS):
        slot = pair_slot(pairs, owner, bit)

        @pl.when(slot >= 0)
        def _(bit=bit, slot=jnp.maximum(slot, 0)):
            block_tiles(*(bulk[bit].at[pl.ds(k * EDGE, EDGE)] for k in range(3)), 0, fresh)
            for kind in range(KINDS):
                high, low = fresh[kind], fresh[KINDS + kind]
                ze[kind * SLOTS + slot] = jnp.where(even, high, low)
                zo[kind * SLOTS + slot] = jnp.where(even, low, high)
            for k in range(2):
                for side in range(2):
                    held[k * FACES + 2 * slot + side] = fresh[2 * KINDS + 2 * k + side]

    for k in range(2):
        pick_faces(held.at[pl.ds(k * FACES, FACES)], mine, ys, 2 * k, 4)

def ends(top, bottom, faces, bulk, pairs, owner, mine, parity):
    return pl.pallas_call(
        ends_kernel,
        in_specs=[SMEM] * 4 + [VMEM] * (3 + BITS),
        out_specs=[VMEM] * 3,
        out_shape=[tiles(KINDS * SLOTS + 1)] * 2 + [tiles(2 * FACES)],
        scratch_shapes=[scratch(2 * FACES, *TILE), scratch(2 * KINDS + 4, *TILE)],
        compiler_params=params(8),
        cost_estimate=cost(1 << 18, 1 << 20),
        name="ends",
    )(pairs, owner, mine, parity, top, bottom, faces, *bulk)


def first_kernel(pairs, owner, mine, parity, ie, io, ya, *refs):
    bulk, refs = refs[:BITS], refs[BITS + len(MERGED) :]
    v, f, c, forth_v, back_v, forth_c, back_c = refs[: len(MERGED)]
    wk, wf, dg, u, forth, back, ys, lists_out = refs[len(MERGED) : len(MERGED) + 8]
    ghost, ghost_c, below, above, below_c, above_c, faces, held, list_sems, sems = refs[len(MERGED) + 8 :]
    even = parity[0] == 0
    slots = [pair_slot(pairs, owner, bit) for bit in range(BITS)]

    def merges(k):
        for bit in range(BITS):
            copy = pltpu.make_async_copy(
                bulk[bit].at[pl.ds(k * EDGE, EDGE)],
                (v, f, c)[k].at[block_rows(jnp.maximum(slots[bit], 0))],
                sems.at[bit, k],
            )
            yield slots[bit], copy

    def start(k):
        for slot, copy in merges(k):

            @pl.when(slot >= 0)
            def _(copy=copy):
                copy.start()

    def settle(k, field=None, forth=None, back=None):
        for slot, copy in merges(k):

            @pl.when(slot >= 0)
            def _(slot=jnp.maximum(slot, 0), copy=copy):
                copy.wait()
                if field is not None:
                    turn_block(field, slot, forth, back)

    copies = list_copies(ie, io, held, list_sems)
    for copy in copies:
        copy.start()
    for k in (2, 1, 0):
        start(k)
    sheets = ((below, below_c), (above, above_c))
    for side in range(2):
        for store, kind in zip(sheets[side], (V1, C1)):
            fill_sheet(store, sheet_of(even, ie, io, kind, side))
    place_faces(ya, mine, ghost, 0, 4)
    place_faces(ya, mine, ghost_c, 2, 4)
    for copy in copies:
        copy.wait()
    lists = read_lists(even, held, lists_out)
    pack_lines(sheets, lists, ys, 2, 3)
    settle(2, c, forth_c, back_c)
    settle(1)

    def one(j, carry):
        rows = block_rows(j)
        for n, k, around in six_turned(c, forth_c, back_c, j, mine, ghost_c, below_c, above_c):
            scaled, weight, inverse = weights(k, around)
            for d in range(6):
                wk[d, rows, column(n)] = scaled[d]
            wf[rows, column(n)] = weight * f[rows, column(n)]
            dg[rows, column(n)] = inverse
        return carry

    lax.fori_loop(0, SLOTS, one, 0)
    settle(0, v, forth_v, back_v)
    sweep_blocks((v, forth_v, back_v), mine, ghost, below, above, wk, wf, u, forth, back, faces)
    pick_faces(faces, mine, ys, 0, 3)


SHEET = scratch(SLOTS + 1, *TILE)
GHOSTS = scratch(FACES + 1, *TILE)
GATHERED = [scratch(SLOTS, *TILE)] * 3


MERGED = [f32(*FIELD)] * 3 + [f32(*TURNED)] * 4


def first(merged, bulk, ends_in, ya, pairs, owner, mine, parity):
    outs = pl.pallas_call(
        first_kernel,
        in_specs=[SMEM] * 4 + [VMEM] * (3 + BITS + len(MERGED)),
        out_specs=[VMEM] * (len(MERGED) + 7) + [SMEM],
        out_shape=MERGED
        + [f32(6, *FIELD)]
        + [f32(*FIELD)] * 3
        + [f32(*TURNED)] * 2
        + [tiles(3 * SLOTS), jax.ShapeDtypeStruct((2, LISTS), jnp.int32)],
        input_output_aliases={7 + BITS + k: k for k in range(len(MERGED))},
        scratch_shapes=[GHOSTS] * 2
        + [SHEET] * 4
        + [scratch(FACES, *TILE), pltpu.SMEM((2,) + TILE, jnp.float32), pltpu.SemaphoreType.DMA((2,))]
        + [pltpu.SemaphoreType.DMA((BITS, 3))],
        compiler_params=params(20),
        cost_estimate=cost(1 << 24, 12 << 20),
        name="first",
    )(pairs, owner, mine, parity, *ends_in, ya, *bulk, *merged)
    return outs[len(MERGED) :]


def second_kernel(
    mine, parity, lists_in,
    v, forth_in, back_in, wk, wf, ye, yo, ie, io, ya,
    u, forth, back, ze, zo, ys, kept,
    ghost, below, above, below_c, above_c, edge_bv, edge_bc, edge_av, edge_ac, gm, gp, go, faces, ends_out,
):
    even = parity[0] == 0
    lists = [Lists(lists_in, side) for side in range(2)]
    place_faces(ya, mine, ghost, 0, 3)
    edges = ((edge_bv, edge_bc), (edge_av, edge_ac))
    place_lines(ya, lists, edges, 2, 3)
    for side, (store, store_c) in enumerate(((below, below_c), (above, above_c))):
        fill_sheet(store, sheet_of(even, ie, io, V1, side))
        fill_sheet(store_c, sheet_of(even, ie, io, C1, side))
        k = store_c[:SLOTS]
        ends_out[...] = own_end(even, ye, yo, C1, side)
        inner = sheet_of(even, ie, io, C2, side)
        around = sheet_around(store_c, inner, ends_out, edges[side][1], lists[side], side, (gm, gp, go))
        scaled, weight, _ = weights(k, around)
        forced = weight * sheet_of(even, ie, io, F1, side)
        for d in range(6):
            kept[(side * 7 + d) * SLOTS : (side * 7 + d + 1) * SLOTS] = scaled[d]
        kept[(side * 7 + 6) * SLOTS : (side * 7 + 7) * SLOTS] = forced
        ends_out[...] = own_end(even, ye, yo, V1, side)
        inner = sheet_of(even, ie, io, V2, side)
        around = sheet_around(store, inner, ends_out, edges[side][0], lists[side], side, (gm, gp, go))
        total = forced + (1.0 - OMEGA) * store[:SLOTS]
        for d in range(6):
            total = total + scaled[d] * around[d]
        store[:SLOTS] = total
    sweep_blocks((v, forth_in, back_in), mine, ghost, below, above, wk, wf, u, forth, back, faces)
    pick_faces(faces, mine, ys, 0, 2)
    for j in range(SLOTS):
        for depth in range(2):
            layer_tile(u, j * EDGE + EDGE - 1 - depth, ends_out, 0)
            layer_tile(u, j * EDGE + depth, ends_out, 1)
            ze[depth * SLOTS + j] = jnp.where(even, ends_out[0], ends_out[1])
            zo[depth * SLOTS + j] = jnp.where(even, ends_out[1], ends_out[0])


def second(turned, wk, wf, sent, got, ya, mine, parity, lists):
    return pl.pallas_call(
        second_kernel,
        in_specs=[SMEM] * 3 + [VMEM] * 10,
        out_specs=[VMEM] * 7,
        out_shape=[f32(*FIELD), f32(*TURNED), f32(*TURNED), tiles(2 * SLOTS), tiles(2 * SLOTS), tiles(FACES), tiles(14 * SLOTS)],
        scratch_shapes=[GHOSTS] + [SHEET] * 8 + GATHERED + [scratch(FACES, *TILE), scratch(SLOTS, *TILE)],
        compiler_params=params(16),
        cost_estimate=cost(1 << 22, 9 << 20),
        name="second",
    )(mine, parity, lists, *turned, wk, wf, *sent, *got, ya)


def third_kernel(
    mine, parity, lists_in,
    v, forth_in, back_in, wk, wf, ie, io, ya,
    u, forth, back, ys,
    ghost, below, above, faces,
):
    even = parity[0] == 0
    lists = [Lists(lists_in, side) for side in range(2)]
    place_faces(ya, mine, ghost, 0, 2)
    for side, store in enumerate((below, above)):
        fill_sheet(store, sheet_of(even, ie, io, V1, side))
    pack_lines(((below,), (above,)), lists, ys, 2, 3)
    sweep_blocks((v, forth_in, back_in), mine, ghost, below, above, wk, wf, u, forth, back, faces)
    pick_faces(faces, mine, ys, 0, 3)


def third(turned, wk, wf, got, ya, mine, parity, lists):
    return pl.pallas_call(
        third_kernel,
        in_specs=[SMEM] * 3 + [VMEM] * 8,
        out_specs=[VMEM] * 4,
        out_shape=[f32(*FIELD), f32(*TURNED), f32(*TURNED), tiles(3 * SLOTS)],
        scratch_shapes=[GHOSTS] + [SHEET] * 2 + [scratch(FACES, *TILE)],
        compiler_params=params(16),
        cost_estimate=cost(1 << 22, 9 << 20),
        name="third",
    )(mine, parity, lists, *turned, wk, wf, *got, ya)


def last_kernel(
    mine, parity, lists_in,
    v, forth_in, back_in, wk, wf, dg, kept, ye, yo, ie, io, ya,
    out, coarse,
    ghost, below, above, edge_b, edge_a, gm, gp, go, ends_out, residual, sem,
):
    write = pltpu.make_async_copy(v, out, sem)
    write.start()
    even = parity[0] == 0
    lists = [Lists(lists_in, side) for side in range(2)]
    place_faces(ya, mine, ghost, 0, 3)
    edges = ((edge_b,), (edge_a,))
    place_lines(ya, lists, edges, 2, 3)
    for side, store in enumerate((below, above)):
        fill_sheet(store, sheet_of(even, ie, io, V1, side))
        ends_out[...] = own_end(even, ye, yo, V1, side)
        inner = sheet_of(even, ie, io, V2, side)
        around = sheet_around(store, inner, ends_out, edges[side][0], lists[side], side, (gm, gp, go))
        total = kept[(side * 7 + 6) * SLOTS : (side * 7 + 7) * SLOTS] + (1.0 - OMEGA) * store[:SLOTS]
        for d in range(6):
            total = total + kept[(side * 7 + d) * SLOTS : (side * 7 + d + 1) * SLOTS] * around[d]
        store[:SLOTS] = total

    def one(j, carry):
        rows = block_rows(j)
        for n, centre, around in six_turned(v, forth_in, back_in, j, mine, ghost, below, above):
            total = wf[rows, column(n)] - OMEGA * centre
            for d in range(6):
                total = total + wk[d, rows, column(n)] * around[d]
            residual[n, rows, :] = total * dg[rows, column(n)]
        return carry

    lax.fori_loop(0, SLOTS, one, 0)
    lane = lax.broadcasted_iota(jnp.int32, (LANES, LANES), 0)
    target = lax.broadcasted_iota(jnp.int32, (LANES, LANES), 1)
    place = (lane // (2 * EDGE)) * (EDGE // 2) + (lane % EDGE) // 2
    half = ROWS // 2
    for part in range(2):
        total = jnp.zeros((half, LANES), jnp.float32)
        for n in range(4):
            column_sum = (
                residual[part * 4 + n, pl.ds(0, half, stride=2), :]
                + residual[part * 4 + n, pl.ds(1, half, stride=2), :]
            )
            gather = jnp.where(place + EDGE * n == target, 0.125, 0.0)
            total = total + jnp.dot(
                column_sum, gather, precision=lax.Precision.HIGHEST, preferred_element_type=jnp.float32
            )
        coarse[:, part * LANES : (part + 1) * LANES] = total
    write.wait()


def last(turned, wk, wf, dg, kept, sent, got, ya, mine, parity, lists):
    return pl.pallas_call(
        last_kernel,
        in_specs=[SMEM] * 3 + [VMEM] * 12,
        out_specs=[HBM, VMEM],
        out_shape=[f32(*FIELD), f32(ROWS // 2, PLANE // 4)],
        scratch_shapes=[GHOSTS] + [SHEET] * 4 + GATHERED + [scratch(SLOTS, *TILE), scratch(COLS, ROWS, LANES), pltpu.SemaphoreType.DMA]
       ,
        compiler_params=params(16),
        cost_estimate=cost(1 << 24, 10 << 20),
        name="last",
    )(mine, parity, lists, *turned, wk, wf, dg, kept, *sent, *got, ya)


def pair_swap(values, stride):
    count = lax.axis_size("owner")
    return lax.ppermute(values, "owner", [(i, i ^ stride) for i in range(count)])


def odd_pair_swap(values):
    count = lax.axis_size("owner")
    return lax.ppermute(values, "owner", [(i, ((i - 1) ^ 1) + 1) for i in range(1, count - 1)])


def in_hbm(values):
    return pltpu.with_memory_space_constraint(values, pltpu.HBM)


def segment_swap(ys):
    return lax.all_to_all(ys, "sub", split_axis=0, concat_axis=0, tiled=True)


def body(guess, rhs, coef, occupied, neighbours, swap_slot, send_list, recv_list):
    my_owner = lax.axis_index("owner").astype(jnp.int32)
    owner = my_owner.reshape(1)
    parity = (my_owner % 2).reshape(1)
    fields = tuple(values.reshape(FIELD) for values in (guess, rhs, coef))
    fields = tuple(in_hbm(x) for x in fields)
    occupied, swap_slot = in_hbm(occupied), in_hbm(swap_slot)
    bulk = [None] * BITS
    for bits in ((0, 2, 1, 3),):
        for bit, block in zip(bits, swap_pack(fields, occupied, swap_slot, owner, bits)):
            bulk[bit] = pair_swap(block, 1 << bit)
    top, bottom, faces, mine, *merged = local(fields, occupied, neighbours, in_hbm(send_list), in_hbm(recv_list))
    ze, zo, ys = ends(top, bottom, faces, bulk, swap_slot, owner, mine, parity)
    sent, got, ya = (ze, zo), (pair_swap(ze, 1), odd_pair_swap(zo)), segment_swap(ys)
    wk, wf, dg, v, forth, back, ys, lists = first(merged, bulk, got, ya, swap_slot, owner, mine, parity)
    turned = v, forth, back
    *turned, ze, zo, ys, kept = second(turned, wk, wf, sent, got, segment_swap(ys), mine, parity, lists)
    sent, got = (ze, zo), (pair_swap(ze, 1), odd_pair_swap(zo))
    *turned, ys = third(turned, wk, wf, got, segment_swap(ys), mine, parity, lists)
    v, coarse = last(turned, wk, wf, dg, kept, sent, got, segment_swap(ys), mine, parity, lists)
    return v.reshape(SLOTS, EDGE, PLANE), coarse.reshape(SLOTS, EDGE // 2, PLANE // 4)


def solution(mesh):
    wide, flat, single = P(("owner", "sub"), None, None), P(("owner", "sub"), None), P(("owner", "sub"))
    return jax.shard_map(
        body,
        mesh=mesh,
        in_specs=(wide, wide, wide, single, flat, flat, flat, flat),
        out_specs=(wide, wide),
        check_vma=False,
    )
```

time: 104 us -> 94.8 us (0.912)
  starting transfers between devices: 27.7 us -> 18.1 us
  Pallas kernels: 27.5 us -> 29.7 us
  waiting for transfers between devices: 10 us -> 11.2 us
    ppermute x11 -> x6, starting transfers between devices: 14.4 us -> 8.25 us  [pair_swap(): lax.ppermute(values, 'owner', [(i, i ^ stride) for i in range(count)])]
    ppermute x3 -> x2, starting transfers between devices: 13.4 us -> 9.9 us  [odd_pair_swap(): lax.ppermute(values, 'owner', [(i, (i - 1 ^ 1) + 1) for i in range(1, cou...]
    pallas_call x6, Pallas kernels: 26.7 us -> 28.7 us  [the longest x1 10.1 us: first(): pl.pallas_call(first_kernel, in_specs=[SMEM] * 4 + [VMEM] * (3 + BITS + l...]
    ppermute x11 -> x6, waiting for transfers between devices: 10 us -> 11.2 us  [pair_swap(): lax.ppermute(values, 'owner', [(i, i ^ stride) for i in range(count)])]
  transfers between devices with their start and end apart: 14 -> 8, of which waited for: 3 -> 2; matrix products, arithmetic and copies ran while one was open for 2% -> 0% of each run, Pallas kernels for 4% -> 6%
where the time goes in v2:
time: 94.8 us; the launch traced here: 94.4 us
  blocking collectives  34.5 us (36%)
  Pallas kernels  29.7 us (31%)
  starting transfers between devices  18.1 us (19%)
  waiting for transfers between devices  11.2 us (12%)
    all_to_all x4, blocking collectives, segment_swap(): return lax.all_to_all(ys, 'sub', split_axis=0, concat_axis=0, tiled=True)  34.5 us
    ppermute x6, waiting for transfers between devices, pair_swap(): lax.ppermute(values, 'owner', [(i, i ^ stride) for i in range(count)])  11.2 us
    pallas_call x1, Pallas kernels, first(): pl.pallas_call(first_kernel, in_specs=[SMEM] * 4 + [VMEM] * (3 + BITS + l...  10.1 us
    ppermute x2, starting transfers between devices, odd_pair_swap(): lax.ppermute(values, 'owner', [(i, (i - 1 ^ 1) + 1) for i in range(1, cou...  9.9 us
    ppermute x6, starting transfers between devices, pair_swap(): lax.ppermute(values, 'owner', [(i, i ^ stride) for i in range(count)])  8.25 us
    pallas_call x1, Pallas kernels, local(): pl.pallas_call(local_kernel, in_specs=[SMEM] * 4 + [HBM] * 3, out_specs=[...  5.37 us
    pallas_call x1, Pallas kernels, second(): pl.pallas_call(second_kernel, in_specs=[SMEM] * 3 + [VMEM] * 10, out_spec...  3.8 us
    pallas_call x1, Pallas kernels, last(): pl.pallas_call(last_kernel, in_specs=[SMEM] * 3 + [VMEM] * 12, out_specs=...  3.78 us
  transfers between devices with their start and end apart: 8, of which 2 were waited for; matrix products, arithmetic and copies ran while one was open for 0% of the time, Pallas kernels for 6%

profile of v2, /device:TPU:32, one launch (start us, length us, event | category | flops | bytes accessed | tf_op | source)
XLA Modules:
  0.0 94.4 jit_solution(15549774421443585740)
XLA Ops:
  0.6 0.0 copy-start
  0.6 2.2 %swap_pack.1 = (f32[96,1024]{1,0:T(8,128)S(1)}, f32[96,1024]{1,0:T(8,128)S(1)}, f32[96,1024]{1,0:T(8,128)S(1)}, f32[96,1024]{1,0:T(8,128)S(1)}) custom-call(s32[1,16]{1,0:T(1,128)} %pairs.3, s32[1]{0:T(128)} %bitcast.4.refs_1_.owner, s32[8]{0:T(128)} %refs_2_.1, f32[256,1024]{1,0:T(8,128)} %bitcast.7, f32[256,1024]{1,0:T(8,128)} %bitcast.9, f32[256,1024]{1,0:T(8,128)} %bitcast.11), custom_call_target="tpu_custom_call" | custom-call | flops 524288 | bytes 3145728 | tf_op jit(solution)/shard_map/swap_pack/pallas_call | solution.py:347
  2.9 1.7 %collective-permute-start = (f32[96,1024]{1,0:T(8,128)S(1)}, f32[96,1024]{1,0:T(8,128)S(1)}, u32[]{:S(2)}, u32[]{:S(2)}) collective-permute-start(f32[96,1024]{1,0:T(8,128)S(1)} %get-tuple-element.45), channel_id=1, source_target_pairs={{0,8},{8,0},{16,24},{24,16},{32,40},{40,32},{48,56},{56,48},{64,72... | collective-permute-start | bytes 1179656 | tf_op jit(solution)/shard_map/ppermute | solution.py:701
  4.6 2.9 %collective-permute-start.1 = (f32[96,1024]{1,0:T(8,128)S(1)}, f32[96,1024]{1,0:T(8,128)S(1)}, u32[]{:S(2)}, u32[]{:S(2)}) collective-permute-start(f32[96,1024]{1,0:T(8,128)S(1)} %get-tuple-element.46), channel_id=1, source_target_pairs={{0,16},{8,24},{16,0},{24,8},{32,48},{40,56},{48,32},{56,40},{64,80... | collective-permute-start | bytes 1179656 | tf_op jit(solution)/shard_map/ppermute | solution.py:701
  7.5 0.1 collective-permute-start.2
  7.5 3.3 %collective-permute-start.3 = (f32[96,1024]{1,0:T(8,128)S(1)}, f32[96,1024]{1,0:T(8,128)S(1)}, u32[]{:S(2)}, u32[]{:S(2)}) collective-permute-start(f32[96,1024]{1,0:T(8,128)S(1)} %get-tuple-element.48), channel_id=1, source_target_pairs={{0,64},{8,72},{16,80},{24,88},{32,96},{40,104},{48,112},{56,120},{... | collective-permute-start | bytes 1179656 | tf_op jit(solution)/shard_map/ppermute | solution.py:701
  10.8 0.0 copy-done
  10.8 0.1 copy.17.neighbours
  10.9 5.4 %local.1 = (f32[40,8,128]{2,1,0:T(8,128)S(1)}, f32[40,8,128]{2,1,0:T(8,128)S(1)}, f32[32,8,128]{2,1,0:T(8,128)S(1)}, s32[64]{0:T(128)S(1)}, f32[256,1024]{1,0:T(...) custom-call(s32[8]{0:T(128)} %refs_2_.1, ...), custom_call_target="tpu_custom_call" | custom-call | flops 1048576 | bytes 4194304 | tf_op jit(solution)/shard_map/local/pallas_call | solution.py:401
  16.3 0.0 collective-permute-done.refs_0_
  16.3 8.4 %collective-permute-done.1.refs_1_ = f32[96,1024]{1,0:T(8,128)S(1)} collective-permute-done((f32[96,1024]{1,0:T(8,128)S(1)}, f32[96,1024]{1,0:T(8,128)S(1)}, u32[]{:S(2)}, u32[]{:S(2)}) %collective-permute-start.1) | collective-permute-done | bytes 393248 | tf_op jit(solution)/shard_map/ppermute | solution.py:701
  24.7 0.0 collective-permute-done.2.refs_2_
  24.7 2.8 %collective-permute-done.3.refs_3_ = f32[96,1024]{1,0:T(8,128)S(1)} collective-permute-done((f32[96,1024]{1,0:T(8,128)S(1)}, f32[96,1024]{1,0:T(8,128)S(1)}, u32[]{:S(2)}, u32[]{:S(2)}) %collective-permute-start.3) | collective-permute-done | bytes 393248 | tf_op jit(solution)/shard_map/ppermute | solution.py:701
  27.5 1.1 %ends.1 = (f32[41,8,128]{2,1,0:T(8,128)S(1)}, f32[41,8,128]{2,1,0:T(8,128)S(1)}, f32[32,8,128]{2,1,0:T(8,128)S(1)}) custom-call(s32[1,16]{1,0:T(1,128)} %pairs.3, s32[1]{0:T(128)} %bitcast.4.refs_1_.owner, s32[64]{0:T(128)S(1)} %get-tuple-element.41.mine, s32[1]{0:T(128)} %bitcast.3.parity, f32[40,8,128]{2,1,0:T(8,128)S(1)} %get-tuple-element.42.top, ...), custom_call_target="tpu_custom_call" | custom-call | flops 262144 | bytes 1048576 | tf_op jit(solution)/shard_map/ends/pallas_call | solution.py:442
  28.6 0.2 collective-permute-start.4
  28.8 4.5 %collective-permute-start.5 = (f32[41,8,128]{2,1,0:T(8,128)S(1)}, f32[41,8,128]{2,1,0:T(8,128)S(1)}, u32[]{:S(2)}, u32[]{:S(2)}) collective-permute-start(f32[41,8,128]{2,1,0:T(8,128)S(1)} %get-tuple-element.50.yo), channel_id=1, source_target_pairs={{8,16},{16,8},{24,32},{32,24},{40,48},{48,40},{56,64},{64,56},{72,... | collective-permute-start | bytes 503816 | tf_op jit(solution)/shard_map/ppermute | solution.py:706
  33.4 10.2 %all_to_all.20.ya = f32[32,8,128]{2,1,0:T(8,128)S(1)} all-to-all(f32[32,8,128]{2,1,0:T(8,128)S(1)} %get-tuple-element.51), channel_id=1, replica_groups=mesh['owner'=16,'sub'=8] {'sub'}, dimensions={0} | all-to-all | bytes 262144 | tf_op jit(solution)/shard_map/all_to_all | solution.py:714
  43.5 0.0 collective-permute-done.4.ie
  43.5 0.0 collective-permute-done.5.io
  43.5 10.1 %first.1 = (f32[256,1024]{1,0:T(8,128)S(1)}, f32[256,1024]{1,0:T(8,128)S(1)}, f32[256,1024]{1,0:T(8,128)S(1)}, f32[288,1024]{1,0:T(8,128)S(1)}, f32[288,1024]{1,...) custom-call(s32[1,16]{1,0:T(1,128)} %pairs.3, ...), custom_call_target="tpu_custom_call", output_to_operand_aliasing={{0}: (11, {}), {1}: (12, {}), {2}: (13, {}), {3}: (14, {}),... | custom-call | flops 16777216 | bytes 12582912 | tf_op jit(solution)/shard_map/first/pallas_call | solution.py:530
  53.6 8.2 %all_to_all.21.ya = f32[24,8,128]{2,1,0:T(8,128)S(1)} all-to-all(f32[24,8,128]{2,1,0:T(8,128)S(1)} %get-tuple-element.65), channel_id=1, replica_groups=mesh['owner'=16,'sub'=8] {'sub'}, dimensions={0} | all-to-all | bytes 196608 | tf_op jit(solution)/shard_map/all_to_all | solution.py:714
  61.8 3.8 %second.1 = (f32[256,1024]{1,0:T(8,128)S(1)}, f32[288,1024]{1,0:T(8,128)S(1)}, f32[288,1024]{1,0:T(8,128)S(1)}, f32[16,8,128]{2,1,0:T(8,128)S(1)}, f32[16,8,128]...) custom-call(s32[64]{0:T(128)S(1)} %get-tuple-element.41.mine, s32[1]{0:T(128)} %bitcast.3.parity, ...), custom_call_target="tpu_custom_call" | custom-call | flops 4194304 | bytes 9437184 | tf_op jit(solution)/shard_map/second/pallas_call | solution.py:592
  65.6 0.1 collective-permute-start.6
  65.7 5.4 %collective-permute-start.7 = (f32[16,8,128]{2,1,0:T(8,128)S(1)}, f32[16,8,128]{2,1,0:T(8,128)S(1)}, u32[]{:S(2)}, u32[]{:S(2)}) collective-permute-start(f32[16,8,128]{2,1,0:T(8,128)S(1)} %get-tuple-element.70.yo), channel_id=1, source_target_pairs={{8,16},{16,8},{24,32},{32,24},{40,48},{48,40},{56,64},{64,56},{72,... | collective-permute-start | bytes 196616 | tf_op jit(solution)/shard_map/ppermute | solution.py:706
  71.1 8.0 %all_to_all.22.ya = f32[16,8,128]{2,1,0:T(8,128)S(1)} all-to-all(f32[16,8,128]{2,1,0:T(8,128)S(1)} %get-tuple-element.71), channel_id=1, replica_groups=mesh['owner'=16,'sub'=8] {'sub'}, dimensions={0} | all-to-all | bytes 131072 | tf_op jit(solution)/shard_map/all_to_all | solution.py:714
  79.1 0.0 collective-permute-done.6.ie
  79.1 0.0 collective-permute-done.7.io
  79.1 3.4 %third.1 = (f32[256,1024]{1,0:T(8,128)S(1)}, f32[288,1024]{1,0:T(8,128)S(1)}, f32[288,1024]{1,0:T(8,128)S(1)}, f32[24,8,128]{2,1,0:T(8,128)S(1)}) custom-call(s32[64]{0:T(128)S(1)} %get-tuple-element.41.mine, s32[1]{0:T(128)} %bitcast.3.parity, s32[2,64]{1,0:T(2,128)S(1)} %get-tuple-element.59.lists_in, f32[256,1024]{1,0:T(8,128)S(1)} %get-tuple-element.66.v, ...), custom_call_target="tpu_custom_call" | custom-call | flops 4194304 | bytes 9437184 | tf_op jit(solution)/shard_map/third/pallas_call | solution.py:621
  82.5 8.2 %all_to_all.23.ya = f32[24,8,128]{2,1,0:T(8,128)S(1)} all-to-all(f32[24,8,128]{2,1,0:T(8,128)S(1)} %get-tuple-element.77), channel_id=1, replica_groups=mesh['owner'=16,'sub'=8] {'sub'}, dimensions={0} | all-to-all | bytes 196608 | tf_op jit(solution)/shard_map/all_to_all | solution.py:714
  90.6 3.8 %last.1 = (f32[256,1024]{1,0:T(8,128)}, f32[128,256]{1,0:T(8,128)}) custom-call(s32[64]{0:T(128)S(1)} %get-tuple-element.41.mine, s32[1]{0:T(128)} %bitcast.3.parity, s32[2,64]{1,0:T(2,128)S(1)} %get-tuple-element.59.lists_in, f32[256,1024]{1,0:T(8,128)S(1)} %get-tuple-element.72.v, f32[288,1024]{1,0:T(8,128)S(1)} %get-tuple-element.73.forth_in, ...), custom_call_target="tpu_custom_call" | custom-call | flops 16777216 | bytes 10485760 | tf_op jit(solution)/shard_map/last/pallas_call | solution.py:686
Async XLA Ops:
  0.6 10.2 %copy-start = (s32[8,4]{0,1:T(4,128)S(1)}, s32[8,4]{0,1:T(4,128)}, u32[]{:S(2)}) copy-start(s32[8,4]{0,1:T(4,128)} %param.12) | copy-start | bytes 388
  2.9 13.4 %collective-permute-start = (f32[96,1024]{1,0:T(8,128)S(1)}, f32[96,1024]{1,0:T(8,128)S(1)}, u32[]{:S(2)}, u32[]{:S(2)}) collective-permute-start(f32[96,1024]{1,0:T(8,128)S(1)} %get-tuple-element.45), channel_id=1, source_target_pairs={{0,8},{8,0},{16,24},{24,16},{32,40},{40,32},{48,56},{56,48},{64,72... | collective-permute-start | bytes 1179656 | tf_op jit(solution)/shard_map/ppermute | solution.py:701
  4.6 20.1 %collective-permute-start.1 = (f32[96,1024]{1,0:T(8,128)S(1)}, f32[96,1024]{1,0:T(8,128)S(1)}, u32[]{:S(2)}, u32[]{:S(2)}) collective-permute-start(f32[96,1024]{1,0:T(8,128)S(1)} %get-tuple-element.46), channel_id=1, source_target_pairs={{0,16},{8,24},{16,0},{24,8},{32,48},{40,56},{48,32},{56,40},{64,80... | collective-permute-start | bytes 1179656 | tf_op jit(solution)/shard_map/ppermute | solution.py:701
  7.5 17.2 %collective-permute-start.2 = (f32[96,1024]{1,0:T(8,128)S(1)}, f32[96,1024]{1,0:T(8,128)S(1)}, u32[]{:S(2)}, u32[]{:S(2)}) collective-permute-start(f32[96,1024]{1,0:T(8,128)S(1)} %get-tuple-element.47), channel_id=1, source_target_pairs={{0,32},{8,40},{16,48},{24,56},{32,0},{40,8},{48,16},{56,24},{64,96... | collective-permute-start | bytes 1179656 | tf_op jit(solution)/shard_map/ppermute | solution.py:701
  7.5 20.0 %collective-permute-start.3 = (f32[96,1024]{1,0:T(8,128)S(1)}, f32[96,1024]{1,0:T(8,128)S(1)}, u32[]{:S(2)}, u32[]{:S(2)}) collective-permute-start(f32[96,1024]{1,0:T(8,128)S(1)} %get-tuple-element.48), channel_id=1, source_target_pairs={{0,64},{8,72},{16,80},{24,88},{32,96},{40,104},{48,112},{56,120},{... | collective-permute-start | bytes 1179656 | tf_op jit(solution)/shard_map/ppermute | solution.py:701
  28.6 14.9 %collective-permute-start.4 = (f32[41,8,128]{2,1,0:T(8,128)S(1)}, f32[41,8,128]{2,1,0:T(8,128)S(1)}, u32[]{:S(2)}, u32[]{:S(2)}) collective-permute-start(f32[41,8,128]{2,1,0:T(8,128)S(1)} %get-tuple-element.49.ye), channel_id=1, source_target_pairs={{0,8},{8,0},{16,24},{24,16},{32,40},{40,32},{48,56},{56,48},{64,72... | collective-permute-start | bytes 503816 | tf_op jit(solution)/shard_map/ppermute | solution.py:701
  28.8 14.7 %collective-permute-start.5 = (f32[41,8,128]{2,1,0:T(8,128)S(1)}, f32[41,8,128]{2,1,0:T(8,128)S(1)}, u32[]{:S(2)}, u32[]{:S(2)}) collective-permute-start(f32[41,8,128]{2,1,0:T(8,128)S(1)} %get-tuple-element.50.yo), channel_id=1, source_target_pairs={{8,16},{16,8},{24,32},{32,24},{40,48},{48,40},{56,64},{64,56},{72,... | collective-permute-start | bytes 503816 | tf_op jit(solution)/shard_map/ppermute | solution.py:706
  65.6 13.5 %collective-permute-start.6 = (f32[16,8,128]{2,1,0:T(8,128)S(1)}, f32[16,8,128]{2,1,0:T(8,128)S(1)}, u32[]{:S(2)}, u32[]{:S(2)}) collective-permute-start(f32[16,8,128]{2,1,0:T(8,128)S(1)} %get-tuple-element.69.ye), channel_id=1, source_target_pairs={{0,8},{8,0},{16,24},{24,16},{32,40},{40,32},{48,56},{56,48},{64,72... | collective-permute-start | bytes 196616 | tf_op jit(solution)/shard_map/ppermute | solution.py:701
  65.7 13.4 %collective-permute-start.7 = (f32[16,8,128]{2,1,0:T(8,128)S(1)}, f32[16,8,128]{2,1,0:T(8,128)S(1)}, u32[]{:S(2)}, u32[]{:S(2)}) collective-permute-start(f32[16,8,128]{2,1,0:T(8,128)S(1)} %get-tuple-element.70.yo), channel_id=1, source_target_pairs={{8,16},{16,8},{24,32},{32,24},{40,48},{48,40},{56,64},{64,56},{72,... | collective-permute-start | bytes 196616 | tf_op jit(solution)/shard_map/ppermute | solution.py:706

commit v3 on v2

--- a/solution.py
+++ b/solution.py
@@ -17,6 +17,7 @@
 FACES = 2 * SLOTS
 TILE = (8, LANES)
 BITS = 4
+ORDER = (0, 2, 1, 3)
 V1, V2, C1, C2, F1 = range(5)
 KINDS = 5
 SEND = 4 * SLOTS
@@ -235,13 +236,11 @@
 
 
 def weights(k, around):
-    faces = [0.5 * (k + jnp.where(other > 0.0, other, k)) for other in around]
-    total = faces[0]
-    for face in faces[1:]:
-        total = total + face
+    faces = [k + jnp.where(other > 0.0, other, k) for other in around]
+    total = (faces[0] + faces[1]) + (faces[2] + faces[3]) + (faces[4] + faces[5])
     alive = k > 0.0
-    weight = jnp.where(alive, OMEGA / jnp.where(alive, total, 1.0), 0.0)
-    return [weight * face for face in faces], weight, jnp.where(alive, total * (1.0 / OMEGA), 0.0)
+    factor = jnp.where(alive, OMEGA / total, 0.0)
+    return [factor * face for face in faces], 2.0 * factor, jnp.where(alive, total * (0.5 / OMEGA), 0.0)
 
 
 def six_turned(field, forth, back, j, mine, ghost, below, above):
@@ -414,7 +413,7 @@
 
 
 def ends_kernel(pairs, owner, mine, parity, top, bottom, faces, *refs):
-    bulk = refs[:BITS]
+    bulk = dict(zip(ORDER, refs))
     ze, zo, ys, held, fresh = refs[BITS:]
     even = parity[0] == 0
     ze[: KINDS * SLOTS] = jnp.where(even, top[...], bottom[...])
@@ -452,7 +451,7 @@
 
 
 def first_kernel(pairs, owner, mine, parity, ie, io, ya, *refs):
-    bulk, refs = refs[:BITS], refs[BITS + len(MERGED) :]
+    bulk, refs = dict(zip(ORDER, refs)), refs[BITS + len(MERGED) :]
     v, f, c, forth_v, back_v, forth_c, back_c = refs[: len(MERGED)]
     wk, wf, dg, u, forth, back, ys, lists_out = refs[len(MERGED) : len(MERGED) + 8]
     ghost, ghost_c, below, above, below_c, above_c, faces, held, list_sems, sems = refs[len(MERGED) + 8 :]
@@ -501,20 +500,26 @@
     pack_lines(sheets, lists, ys, 2, 3)
     settle(2, c, forth_c, back_c)
     settle(1)
+    settle(0, v, forth_v, back_v)
 
     def one(j, carry):
         rows = block_rows(j)
-        for n, k, around in six_turned(c, forth_c, back_c, j, mine, ghost_c, below_c, above_c):
-            scaled, weight, inverse = weights(k, around)
+        conduct = six_turned(c, forth_c, back_c, j, mine, ghost_c, below_c, above_c)
+        iterate = six_turned(v, forth_v, back_v, j, mine, ghost, below, above)
+        for (n, k, around_k), (_, centre, around) in zip(conduct, iterate):
+            scaled, weight, inverse = weights(k, around_k)
+            forced = weight * f[rows, column(n)]
+            wf[rows, column(n)] = forced
+            dg[rows, column(n)] = inverse
+            total = forced + (1.0 - OMEGA) * centre
             for d in range(6):
                 wk[d, rows, column(n)] = scaled[d]
-            wf[rows, column(n)] = weight * f[rows, column(n)]
-            dg[rows, column(n)] = inverse
+                total = total + scaled[d] * around[d]
+            store_swept(total, n, j, u, forth, back, faces)
         return carry
 
     lax.fori_loop(0, SLOTS, one, 0)
-    settle(0, v, forth_v, back_v)
-    sweep_blocks((v, forth_v, back_v), mine, ghost, below, above, wk, wf, u, forth, back, faces)
+    end_turned(forth, back)
     pick_faces(faces, mine, ys, 0, 3)
 
 
@@ -721,10 +726,8 @@
     fields = tuple(values.reshape(FIELD) for values in (guess, rhs, coef))
     fields = tuple(in_hbm(x) for x in fields)
     occupied, swap_slot = in_hbm(occupied), in_hbm(swap_slot)
-    bulk = [None] * BITS
-    for bits in ((0, 2, 1, 3),):
-        for bit, block in zip(bits, swap_pack(fields, occupied, swap_slot, owner, bits)):
-            bulk[bit] = pair_swap(block, 1 << bit)
+    bulk = swap_pack(fields, occupied, swap_slot, owner, ORDER)
+    bulk = [pair_swap(block, 1 << bit) for bit, block in zip(ORDER, bulk)]
     top, bottom, faces, mine, *merged = local(fields, occupied, neighbours, in_hbm(send_list), in_hbm(recv_list))
     ze, zo, ys = ends(top, bottom, faces, bulk, swap_slot, owner, mine, parity)
     sent, got, ya = (ze, zo), (pair_swap(ze, 1), odd_pair_swap(zo)), segment_swap(ys)

time: 94.8 us -> 91.2 us (0.962); the launches traced: 94.4 us -> 89.4 us
  waiting for transfers between devices: 11.2 us -> 8.59 us
  Pallas kernels: 29.7 us -> 27.8 us
    ppermute x6, waiting for transfers between devices: 11.2 us -> 8.59 us  [pair_swap(): lax.ppermute(values, 'owner', [(i, i ^ stride) for i in range(count)])]
    pallas_call x1, Pallas kernels: 10.1 us -> 8.19 us  [first(): pl.pallas_call(first_kernel, in_specs=[SMEM] * 4 + [VMEM] * (3 + BITS + l...]
  transfers between devices with their start and end apart: 8 -> 8, of which waited for: 2 -> 3; matrix products, arithmetic and copies ran while one was open for 0% -> 0% of each run, Pallas kernels for 6% -> 6%
where the time goes in v3:
time: 91.2 us; the launch traced here: 89.4 us
  blocking collectives  34.6 us (38%)
  Pallas kernels  27.8 us (30%)
  starting transfers between devices  17.6 us (19%)
  waiting for transfers between devices  8.59 us (9%)
    all_to_all x4, blocking collectives, segment_swap(): return lax.all_to_all(ys, 'sub', split_axis=0, concat_axis=0, tiled=True)  34.6 us
    ppermute x2, starting transfers between devices, odd_pair_swap(): lax.ppermute(values, 'owner', [(i, (i - 1 ^ 1) + 1) for i in range(1, cou...  9.05 us
    ppermute x6, waiting for transfers between devices, pair_swap(): lax.ppermute(values, 'owner', [(i, i ^ stride) for i in range(count)])  8.59 us
    ppermute x6, starting transfers between devices, pair_swap(): lax.ppermute(values, 'owner', [(i, i ^ stride) for i in range(count)])  8.54 us
    pallas_call x1, Pallas kernels, first(): pl.pallas_call(first_kernel, in_specs=[SMEM] * 4 + [VMEM] * (3 + BITS + l...  8.19 us
    pallas_call x1, Pallas kernels, local(): pl.pallas_call(local_kernel, in_specs=[SMEM] * 4 + [HBM] * 3, out_specs=[...  5.41 us
    pallas_call x1, Pallas kernels, second(): pl.pallas_call(second_kernel, in_specs=[SMEM] * 3 + [VMEM] * 10, out_spec...  3.84 us
    pallas_call x1, Pallas kernels, last(): pl.pallas_call(last_kernel, in_specs=[SMEM] * 3 + [VMEM] * 12, out_specs=...  3.78 us
  transfers between devices with their start and end apart: 8, of which 3 were waited for; matrix products, arithmetic and copies ran while one was open for 0% of the time, Pallas kernels for 6%

profile of v3, /device:TPU:32, one launch (start us, length us, event | category | flops | bytes accessed | tf_op | source)
XLA Modules:
  0.0 89.4 jit_solution(17677736978211143649)
XLA Ops:
  0.6 0.0 copy-start
  0.6 2.2 %swap_pack.1 = (f32[96,1024]{1,0:T(8,128)S(1)}, f32[96,1024]{1,0:T(8,128)S(1)}, f32[96,1024]{1,0:T(8,128)S(1)}, f32[96,1024]{1,0:T(8,128)S(1)}) custom-call(s32[1,16]{1,0:T(1,128)} %pairs.3, s32[1]{0:T(128)} %bitcast.4.refs_1_.owner, s32[8]{0:T(128)} %refs_2_.1, f32[256,1024]{1,0:T(8,128)} %bitcast.7, f32[256,1024]{1,0:T(8,128)} %bitcast.9, f32[256,1024]{1,0:T(8,128)} %bitcast.11), custom_call_target="tpu_custom_call" | custom-call | flops 524288 | bytes 3145728 | tf_op jit(solution)/shard_map/swap_pack/pallas_call | solution.py:346
  2.9 1.7 %collective-permute-start = (f32[96,1024]{1,0:T(8,128)S(1)}, f32[96,1024]{1,0:T(8,128)S(1)}, u32[]{:S(2)}, u32[]{:S(2)}) collective-permute-start(f32[96,1024]{1,0:T(8,128)S(1)} %get-tuple-element.45), channel_id=1, source_target_pairs={{0,8},{8,0},{16,24},{24,16},{32,40},{40,32},{48,56},{56,48},{64,72... | collective-permute-start | bytes 1179656 | tf_op jit(solution)/shard_map/ppermute | solution.py:706
  4.5 0.1 collective-permute-start.1
  4.6 2.9 %collective-permute-start.2 = (f32[96,1024]{1,0:T(8,128)S(1)}, f32[96,1024]{1,0:T(8,128)S(1)}, u32[]{:S(2)}, u32[]{:S(2)}) collective-permute-start(f32[96,1024]{1,0:T(8,128)S(1)} %get-tuple-element.47), channel_id=1, source_target_pairs={{0,16},{8,24},{16,0},{24,8},{32,48},{40,56},{48,32},{56,40},{64,80... | collective-permute-start | bytes 1179656 | tf_op jit(solution)/shard_map/ppermute | solution.py:706
  7.5 3.3 %collective-permute-start.3 = (f32[96,1024]{1,0:T(8,128)S(1)}, f32[96,1024]{1,0:T(8,128)S(1)}, u32[]{:S(2)}, u32[]{:S(2)}) collective-permute-start(f32[96,1024]{1,0:T(8,128)S(1)} %get-tuple-element.48), channel_id=1, source_target_pairs={{0,64},{8,72},{16,80},{24,88},{32,96},{40,104},{48,112},{56,120},{... | collective-permute-start | bytes 1179656 | tf_op jit(solution)/shard_map/ppermute | solution.py:706
  10.8 0.0 copy-done
  10.8 0.1 copy.17.neighbours
  10.9 5.4 %local.1 = (f32[40,8,128]{2,1,0:T(8,128)S(1)}, f32[40,8,128]{2,1,0:T(8,128)S(1)}, f32[32,8,128]{2,1,0:T(8,128)S(1)}, s32[64]{0:T(128)S(1)}, f32[256,1024]{1,0:T(...) custom-call(s32[8]{0:T(128)} %refs_2_.1, ...), custom_call_target="tpu_custom_call" | custom-call | flops 1048576 | bytes 4194304 | tf_op jit(solution)/shard_map/local/pallas_call | solution.py:400
  16.3 0.0 collective-permute-done.refs_0_
  16.3 0.2 collective-permute-done.1.refs_1_
  16.6 8.1 %collective-permute-done.2.refs_2_ = f32[96,1024]{1,0:T(8,128)S(1)} collective-permute-done((f32[96,1024]{1,0:T(8,128)S(1)}, f32[96,1024]{1,0:T(8,128)S(1)}, u32[]{:S(2)}, u32[]{:S(2)}) %collective-permute-start.2) | collective-permute-done | bytes 393248 | tf_op jit(solution)/shard_map/ppermute | solution.py:706
  24.7 0.2 collective-permute-done.3.refs_3_
  24.9 1.0 %ends.1 = (f32[41,8,128]{2,1,0:T(8,128)S(1)}, f32[41,8,128]{2,1,0:T(8,128)S(1)}, f32[32,8,128]{2,1,0:T(8,128)S(1)}) custom-call(s32[1,16]{1,0:T(1,128)} %pairs.3, s32[1]{0:T(128)} %bitcast.4.refs_1_.owner, s32[64]{0:T(128)S(1)} %get-tuple-element.41.mine, s32[1]{0:T(128)} %bitcast.3.parity, f32[40,8,128]{2,1,0:T(8,128)S(1)} %get-tuple-element.42.top, ...), custom_call_target="tpu_custom_call" | custom-call | flops 262144 | bytes 1048576 | tf_op jit(solution)/shard_map/ends/pallas_call | solution.py:441
  25.9 0.5 collective-permute-start.4
  26.4 6.5 %collective-permute-start.5 = (f32[41,8,128]{2,1,0:T(8,128)S(1)}, f32[41,8,128]{2,1,0:T(8,128)S(1)}, u32[]{:S(2)}, u32[]{:S(2)}) collective-permute-start(f32[41,8,128]{2,1,0:T(8,128)S(1)} %get-tuple-element.50.yo), channel_id=1, source_target_pairs={{8,16},{16,8},{24,32},{32,24},{40,48},{48,40},{56,64},{64,56},{72,... | collective-permute-start | bytes 503816 | tf_op jit(solution)/shard_map/ppermute | solution.py:711
  32.9 10.3 %all_to_all.20.ya = f32[32,8,128]{2,1,0:T(8,128)S(1)} all-to-all(f32[32,8,128]{2,1,0:T(8,128)S(1)} %get-tuple-element.51), channel_id=1, replica_groups=mesh['owner'=16,'sub'=8] {'sub'}, dimensions={0} | all-to-all | bytes 262144 | tf_op jit(solution)/shard_map/all_to_all | solution.py:719
  43.2 0.0 collective-permute-done.4.ie
  43.2 0.0 collective-permute-done.5.io
  43.2 8.2 %first.1 = (f32[256,1024]{1,0:T(8,128)S(1)}, f32[256,1024]{1,0:T(8,128)S(1)}, f32[256,1024]{1,0:T(8,128)S(1)}, f32[288,1024]{1,0:T(8,128)S(1)}, f32[288,1024]{1,...) custom-call(s32[1,16]{1,0:T(1,128)} %pairs.3, ...), custom_call_target="tpu_custom_call", output_to_operand_aliasing={{0}: (11, {}), {1}: (12, {}), {2}: (13, {}), {3}: (14, {}),... | custom-call | flops 16777216 | bytes 12582912 | tf_op jit(solution)/shard_map/first/pallas_call | solution.py:535
  51.4 8.2 %all_to_all.21.ya = f32[24,8,128]{2,1,0:T(8,128)S(1)} all-to-all(f32[24,8,128]{2,1,0:T(8,128)S(1)} %get-tuple-element.65), channel_id=1, replica_groups=mesh['owner'=16,'sub'=8] {'sub'}, dimensions={0} | all-to-all | bytes 196608 | tf_op jit(solution)/shard_map/all_to_all | solution.py:719
  59.6 3.8 %second.1 = (f32[256,1024]{1,0:T(8,128)S(1)}, f32[288,1024]{1,0:T(8,128)S(1)}, f32[288,1024]{1,0:T(8,128)S(1)}, f32[16,8,128]{2,1,0:T(8,128)S(1)}, f32[16,8,128]...) custom-call(s32[64]{0:T(128)S(1)} %get-tuple-element.41.mine, s32[1]{0:T(128)} %bitcast.3.parity, ...), custom_call_target="tpu_custom_call" | custom-call | flops 4194304 | bytes 9437184 | tf_op jit(solution)/shard_map/second/pallas_call | solution.py:597
  63.4 0.1 collective-permute-start.6
  63.5 2.5 %collective-permute-start.7 = (f32[16,8,128]{2,1,0:T(8,128)S(1)}, f32[16,8,128]{2,1,0:T(8,128)S(1)}, u32[]{:S(2)}, u32[]{:S(2)}) collective-permute-start(f32[16,8,128]{2,1,0:T(8,128)S(1)} %get-tuple-element.70.yo), channel_id=1, source_target_pairs={{8,16},{16,8},{24,32},{32,24},{40,48},{48,40},{56,64},{64,56},{72,... | collective-permute-start | bytes 196616 | tf_op jit(solution)/shard_map/ppermute | solution.py:711
  66.1 8.0 %all_to_all.22.ya = f32[16,8,128]{2,1,0:T(8,128)S(1)} all-to-all(f32[16,8,128]{2,1,0:T(8,128)S(1)} %get-tuple-element.71), channel_id=1, replica_groups=mesh['owner'=16,'sub'=8] {'sub'}, dimensions={0} | all-to-all | bytes 131072 | tf_op jit(solution)/shard_map/all_to_all | solution.py:719
  74.1 0.0 collective-permute-done.6.ie
  74.1 0.0 collective-permute-done.7.io
  74.1 3.4 %third.1 = (f32[256,1024]{1,0:T(8,128)S(1)}, f32[288,1024]{1,0:T(8,128)S(1)}, f32[288,1024]{1,0:T(8,128)S(1)}, f32[24,8,128]{2,1,0:T(8,128)S(1)}) custom-call(s32[64]{0:T(128)S(1)} %get-tuple-element.41.mine, s32[1]{0:T(128)} %bitcast.3.parity, s32[2,64]{1,0:T(2,128)S(1)} %get-tuple-element.59.lists_in, f32[256,1024]{1,0:T(8,128)S(1)} %get-tuple-element.66.v, ...), custom_call_target="tpu_custom_call" | custom-call | flops 4194304 | bytes 9437184 | tf_op jit(solution)/shard_map/third/pallas_call | solution.py:626
  77.5 8.2 %all_to_all.23.ya = f32[24,8,128]{2,1,0:T(8,128)S(1)} all-to-all(f32[24,8,128]{2,1,0:T(8,128)S(1)} %get-tuple-element.77), channel_id=1, replica_groups=mesh['owner'=16,'sub'=8] {'sub'}, dimensions={0} | all-to-all | bytes 196608 | tf_op jit(solution)/shard_map/all_to_all | solution.py:719
  85.7 3.8 %last.1 = (f32[256,1024]{1,0:T(8,128)}, f32[128,256]{1,0:T(8,128)}) custom-call(s32[64]{0:T(128)S(1)} %get-tuple-element.41.mine, s32[1]{0:T(128)} %bitcast.3.parity, s32[2,64]{1,0:T(2,128)S(1)} %get-tuple-element.59.lists_in, f32[256,1024]{1,0:T(8,128)S(1)} %get-tuple-element.72.v, f32[288,1024]{1,0:T(8,128)S(1)} %get-tuple-element.73.forth_in, ...), custom_call_target="tpu_custom_call" | custom-call | flops 16777216 | bytes 10485760 | tf_op jit(solution)/shard_map/last/pallas_call | solution.py:691
Async XLA Ops:
  0.6 10.2 %copy-start = (s32[8,4]{0,1:T(4,128)S(1)}, s32[8,4]{0,1:T(4,128)}, u32[]{:S(2)}) copy-start(s32[8,4]{0,1:T(4,128)} %param.12) | copy-start | bytes 388
  2.9 13.4 %collective-permute-start = (f32[96,1024]{1,0:T(8,128)S(1)}, f32[96,1024]{1,0:T(8,128)S(1)}, u32[]{:S(2)}, u32[]{:S(2)}) collective-permute-start(f32[96,1024]{1,0:T(8,128)S(1)} %get-tuple-element.45), channel_id=1, source_target_pairs={{0,8},{8,0},{16,24},{24,16},{32,40},{40,32},{48,56},{56,48},{64,72... | collective-permute-start | bytes 1179656 | tf_op jit(solution)/shard_map/ppermute | solution.py:706
  4.5 12.0 %collective-permute-start.1 = (f32[96,1024]{1,0:T(8,128)S(1)}, f32[96,1024]{1,0:T(8,128)S(1)}, u32[]{:S(2)}, u32[]{:S(2)}) collective-permute-start(f32[96,1024]{1,0:T(8,128)S(1)} %get-tuple-element.46), channel_id=1, source_target_pairs={{0,32},{8,40},{16,48},{24,56},{32,0},{40,8},{48,16},{56,24},{64,96... | collective-permute-start | bytes 1179656 | tf_op jit(solution)/shard_map/ppermute | solution.py:706
  4.6 20.1 %collective-permute-start.2 = (f32[96,1024]{1,0:T(8,128)S(1)}, f32[96,1024]{1,0:T(8,128)S(1)}, u32[]{:S(2)}, u32[]{:S(2)}) collective-permute-start(f32[96,1024]{1,0:T(8,128)S(1)} %get-tuple-element.47), channel_id=1, source_target_pairs={{0,16},{8,24},{16,0},{24,8},{32,48},{40,56},{48,32},{56,40},{64,80... | collective-permute-start | bytes 1179656 | tf_op jit(solution)/shard_map/ppermute | solution.py:706
  7.5 17.4 %collective-permute-start.3 = (f32[96,1024]{1,0:T(8,128)S(1)}, f32[96,1024]{1,0:T(8,128)S(1)}, u32[]{:S(2)}, u32[]{:S(2)}) collective-permute-start(f32[96,1024]{1,0:T(8,128)S(1)} %get-tuple-element.48), channel_id=1, source_target_pairs={{0,64},{8,72},{16,80},{24,88},{32,96},{40,104},{48,112},{56,120},{... | collective-permute-start | bytes 1179656 | tf_op jit(solution)/shard_map/ppermute | solution.py:706
  25.9 17.3 %collective-permute-start.4 = (f32[41,8,128]{2,1,0:T(8,128)S(1)}, f32[41,8,128]{2,1,0:T(8,128)S(1)}, u32[]{:S(2)}, u32[]{:S(2)}) collective-permute-start(f32[41,8,128]{2,1,0:T(8,128)S(1)} %get-tuple-element.49.ye), channel_id=1, source_target_pairs={{0,8},{8,0},{16,24},{24,16},{32,40},{40,32},{48,56},{56,48},{64,72... | collective-permute-start | bytes 503816 | tf_op jit(solution)/shard_map/ppermute | solution.py:706
  26.4 16.8 %collective-permute-start.5 = (f32[41,8,128]{2,1,0:T(8,128)S(1)}, f32[41,8,128]{2,1,0:T(8,128)S(1)}, u32[]{:S(2)}, u32[]{:S(2)}) collective-permute-start(f32[41,8,128]{2,1,0:T(8,128)S(1)} %get-tuple-element.50.yo), channel_id=1, source_target_pairs={{8,16},{16,8},{24,32},{32,24},{40,48},{48,40},{56,64},{64,56},{72,... | collective-permute-start | bytes 503816 | tf_op jit(solution)/shard_map/ppermute | solution.py:711
  63.4 10.6 %collective-permute-start.6 = (f32[16,8,128]{2,1,0:T(8,128)S(1)}, f32[16,8,128]{2,1,0:T(8,128)S(1)}, u32[]{:S(2)}, u32[]{:S(2)}) collective-permute-start(f32[16,8,128]{2,1,0:T(8,128)S(1)} %get-tuple-element.69.ye), channel_id=1, source_target_pairs={{0,8},{8,0},{16,24},{24,16},{32,40},{40,32},{48,56},{56,48},{64,72... | collective-permute-start | bytes 196616 | tf_op jit(solution)/shard_map/ppermute | solution.py:706
  63.5 10.6 %collective-permute-start.7 = (f32[16,8,128]{2,1,0:T(8,128)S(1)}, f32[16,8,128]{2,1,0:T(8,128)S(1)}, u32[]{:S(2)}, u32[]{:S(2)}) collective-permute-start(f32[16,8,128]{2,1,0:T(8,128)S(1)} %get-tuple-element.70.yo), channel_id=1, source_target_pairs={{8,16},{16,8},{24,32},{32,24},{40,48},{48,40},{56,64},{64,56},{72,... | collective-permute-start | bytes 196616 | tf_op jit(solution)/shard_map/ppermute | solution.py:711

commit v4 on v3

--- a/solution.py
+++ b/solution.py
@@ -17,9 +17,10 @@
 FACES = 2 * SLOTS
 TILE = (8, LANES)
 BITS = 4
-ORDER = (0, 2, 1, 3)
-V1, V2, C1, C2, F1 = range(5)
-KINDS = 5
+ORDER = (2, 0, 3, 1)
+V, C, F = 0, 4, 8
+KINDS = 11
+DEPTHS = (3, 2, 1)
 SEND = 4 * SLOTS
 RECV = SEND + FACES
 LISTS = RECV + FACES
@@ -169,7 +170,7 @@
 def pack_lines(sheets, lists, out, tile, stride):
     sub, lane = iotas(TILE)
     for peer in range(SLOTS):
-        total = jnp.zeros(TILE, jnp.float32)
+        totals = []
         row = 0
         for side in range(2):
             for i in range(2):
@@ -180,21 +181,27 @@
                     line = store[slot]
                     low_line = line[0:1, :]
                     high_line = pltpu.roll(line, EDGE, 1)[7:8, :]
-                    total = jnp.where(sub == row, jnp.where(high, high_line, low_line), total)
+                    if row % 8 == 0:
+                        totals.append(jnp.zeros(TILE, jnp.float32))
+                    totals[-1] = jnp.where(sub == row % 8, jnp.where(high, high_line, low_line), totals[-1])
                     row += 1
+        total = totals[0]
+        for group, part in enumerate(totals[1:], 1):
+            total = jnp.where(lane // EDGE == group, pltpu.roll(part, EDGE * group, 1), total)
         out[peer * stride + tile] = total
 
 
 def place_lines(arrived, lists, edges, tile, stride):
-    for pair in edges:
-        for store in pair:
+    for stores in edges:
+        for store in stores:
             store[...] = jnp.zeros(store.shape, jnp.float32)
     sub, lane = iotas(TILE)
     first = (sub == 0) & (lane < EDGE)
     final = (sub == 7) & (lane >= LANES - EDGE)
+    groups = (4 * len(edges[0]) + 7) // 8
     for peer in range(SLOTS):
         got = arrived[peer * stride + tile]
-        turned = pltpu.roll(got, LANES - EDGE, 1)
+        turned = [got] + [pltpu.roll(got, LANES - EDGE * g, 1) for g in range(1, groups + 1)]
         row = 0
         for side in range(2):
             for i in range(2):
@@ -202,37 +209,87 @@
                 slot = jnp.where(ghost >= 0, jnp.maximum(ghost, 0) // 2, SLOTS)
                 high = jnp.maximum(ghost, 0) % 2 == 1
                 for store in edges[side]:
-                    low_part = jnp.where(first, got[row : row + 1, :], 0.0)
-                    high_part = jnp.where(final, turned[row : row + 1, :], 0.0)
+                    group, at = row // 8, row % 8
+                    low_part = jnp.where(first, turned[group][at : at + 1, :], 0.0)
+                    high_part = jnp.where(final, turned[group + 1][at : at + 1, :], 0.0)
                     store[slot] = store[slot] + jnp.where(high, high_part, low_part)
                     row += 1
 
 
-def sheet_around(store, inner, outer_tiles, edge, lists, side, gathered):
+def beyond(ends, lists, side, gathered):
+    for slot in range(SLOTS):
+        entry = lists.neighbour(slot, 2 if side else 3)
+        gathered[slot] = ends[slot_or(entry, 0)] * (entry >= 0).astype(jnp.float32)
+    return gathered[...]
+
+
+def sheet_around(store, inner, outer, edge, lists, side, gathered):
     shape = (SLOTS,) + TILE
     sub, lane = iotas(shape)
     x = lane % EDGE
-    minus, plus, outer = gathered
+    minus, plus = gathered
     for slot in range(SLOTS):
         minus[slot] = store[slot_or(lists.neighbour(slot, 0), SLOTS)]
         plus[slot] = store[slot_or(lists.neighbour(slot, 1), SLOTS)]
-        entry = lists.neighbour(slot, 2 if side else 3)
-        outer[slot] = outer_tiles[slot_or(entry, 0)] * (entry >= 0).astype(jnp.float32)
     value = store[:SLOTS]
     edges = edge[:SLOTS]
     forth = pltpu.roll(value, EDGE, 2)
     back = pltpu.roll(value, LANES - EDGE, 2)
     before = jnp.where(lane < EDGE, pltpu.roll(forth, 1, 1), forth)
     after = jnp.where(lane >= LANES - EDGE, pltpu.roll(back, 7, 1), back)
-    out = outer[...]
     return (
         jnp.where(x == 0, pltpu.roll(minus[...], LANES - EDGE + 1, 2), pltpu.roll(value, 1, 2)),
         jnp.where(x == EDGE - 1, pltpu.roll(plus[...], EDGE - 1, 2), pltpu.roll(value, LANES - 1, 2)),
         jnp.where((lane < EDGE) & (sub == 0), edges, before),
         jnp.where((lane >= LANES - EDGE) & (sub == 7), edges, after),
-        out if side else inner,
-        inner if side else out,
+        outer if side else inner,
+        inner if side else outer,
     )
+
+
+def layers(ref, index):
+    return ref[index * SLOTS : (index + 1) * SLOTS]
+
+
+def keep_layers(ref, index, value):
+    ref[index * SLOTS : (index + 1) * SLOTS] = value
+
+
+def swept(value, forced, scaled, around):
+    total = forced + (1.0 - OMEGA) * value
+    for d in range(6):
+        total = total + scaled[d] * around[d]
+    return total
+
+
+def kept_index(side, depth):
+    return 7 * (2 * side + depth)
+
+
+def sweep_sheets(sheets, ends, kept, depths, stores, edges, lists, gathered):
+    minus, plus, touching = gathered
+    for side in range(2):
+        old = [layers(sheets, side * (depths + 1) + depth) for depth in range(depths + 1)]
+        for depth in range(depths):
+            fill_sheet(stores[side][depth], old[depth])
+        outer = beyond(ends.at[pl.ds(side * SLOTS, SLOTS)], lists[side], side, touching)
+        fresh = []
+        for depth in range(depths):
+            around = sheet_around(
+                stores[side][depth], old[depth + 1], outer, edges[side][depth], lists[side], side, (minus, plus)
+            )
+            at = kept_index(side, depth)
+            scaled = [layers(kept, at + d) for d in range(6)]
+            fresh.append(swept(old[depth], layers(kept, at + 6), scaled, around))
+            outer = old[depth]
+        for depth in range(depths):
+            fill_sheet(stores[side][depth], fresh[depth])
+
+
+def own_ends(v, out):
+    for j in range(SLOTS):
+        layer_tile(v, j * EDGE, out, j)
+        layer_tile(v, j * EDGE + EDGE - 1, out, SLOTS + j)
 
 
 def weights(k, around):
@@ -311,8 +368,9 @@
 
 def block_tiles(v, f, c, row, out):
     for end in range(2):
-        for kind, field, depth in ((V1, v, 0), (V2, v, 1), (C1, c, 0), (C2, c, 1), (F1, f, 0)):
-            layer_tile(field, row + (depth if end else EDGE - 1 - depth), out, end * KINDS + kind)
+        for kind, field, count in ((V, v, 4), (C, c, 4), (F, f, 3)):
+            for depth in range(count):
+                layer_tile(field, row + (depth if end else EDGE - 1 - depth), out, end * KINDS + kind + depth)
     for k, field in enumerate((v, c)):
         for side in range(2):
             out[2 * KINDS + 2 * k + side] = face_tile(field, row, side)
@@ -370,7 +428,7 @@
     for entry in range(FACES):
         mine[SEND + entry] = send_list[0, entry]
         mine[RECV + entry] = recv_list[0, entry]
-    for k, (field, kinds) in enumerate(((v, (V1, V2)), (c, (C1, C2)), (f, (F1,)))):
+    for k, (field, kinds) in enumerate(((v, range(V, C)), (c, range(C, F)), (f, range(F, KINDS)))):
         copies[k].wait()
         for j in range(SLOTS):
 
@@ -383,7 +441,7 @@
                 for end, out in enumerate((top, bottom)):
                     row = j * EDGE + (depth if end else EDGE - 1 - depth)
                     layer_tile(field, row, out, kind * SLOTS + j)
-            if len(kinds) == 2:
+            if k < 2:
                 for side in range(2):
                     faces[k * FACES + 2 * j + side] = face_tile(field, j * EDGE, side)
     for field, forth, back in ((v, forth_v, back_v), (c, forth_c, back_c)):
@@ -454,7 +512,7 @@
     bulk, refs = dict(zip(ORDER, refs)), refs[BITS + len(MERGED) :]
     v, f, c, forth_v, back_v, forth_c, back_c = refs[: len(MERGED)]
     wk, wf, dg, u, forth, back, ys, lists_out = refs[len(MERGED) : len(MERGED) + 8]
-    ghost, ghost_c, below, above, below_c, above_c, faces, held, list_sems, sems = refs[len(MERGED) + 8 :]
+    ghost, ghost_c, faces, held, list_sems, sems, *sheet_refs = refs[len(MERGED) + 8 :]
     even = parity[0] == 0
     slots = [pair_slot(pairs, owner, bit) for bit in range(BITS)]
 
@@ -488,10 +546,11 @@
         copy.start()
     for k in (2, 1, 0):
         start(k)
-    sheets = ((below, below_c), (above, above_c))
+    sheets = sheet_refs[:6], sheet_refs[6:]
     for side in range(2):
-        for store, kind in zip(sheets[side], (V1, C1)):
+        for store, kind in zip(sheets[side], (V, V + 1, V + 2, C, C + 1, C + 2)):
             fill_sheet(store, sheet_of(even, ie, io, kind, side))
+    (below, _, _, below_c, _, _), (above, _, _, above_c, _, _) = sheets
     place_faces(ya, mine, ghost, 0, 4)
     place_faces(ya, mine, ghost_c, 2, 4)
     for copy in copies:
@@ -543,9 +602,9 @@
         + [tiles(3 * SLOTS), jax.ShapeDtypeStruct((2, LISTS), jnp.int32)],
         input_output_aliases={7 + BITS + k: k for k in range(len(MERGED))},
         scratch_shapes=[GHOSTS] * 2
-        + [SHEET] * 4
         + [scratch(FACES, *TILE), pltpu.SMEM((2,) + TILE, jnp.float32), pltpu.SemaphoreType.DMA((2,))]
-        + [pltpu.SemaphoreType.DMA((BITS, 3))],
+        + [pltpu.SemaphoreType.DMA((BITS, 3))]
+        + [SHEET] * 12,
         compiler_params=params(20),
         cost_estimate=cost(1 << 24, 12 << 20),
         name="first",
@@ -556,41 +615,50 @@
 def second_kernel(
     mine, parity, lists_in,
     v, forth_in, back_in, wk, wf, ye, yo, ie, io, ya,
-    u, forth, back, ze, zo, ys, kept,
-    ghost, below, above, below_c, above_c, edge_bv, edge_bc, edge_av, edge_ac, gm, gp, go, faces, ends_out,
+    u, forth, back, ys, kept, sheets, ends,
+    ghost, faces, ends_out, minus, plus, touching, *sheet_refs,
 ):
     even = parity[0] == 0
     lists = [Lists(lists_in, side) for side in range(2)]
     place_faces(ya, mine, ghost, 0, 3)
-    edges = ((edge_bv, edge_bc), (edge_av, edge_ac))
+    own_ends(v, ends)
+    depths = DEPTHS[0]
+    stores, edges = (sheet_refs[:6], sheet_refs[6:12]), (sheet_refs[12:18], sheet_refs[18:])
     place_lines(ya, lists, edges, 2, 3)
-    for side, (store, store_c) in enumerate(((below, below_c), (above, above_c))):
-        fill_sheet(store, sheet_of(even, ie, io, V1, side))
-        fill_sheet(store_c, sheet_of(even, ie, io, C1, side))
-        k = store_c[:SLOTS]
-        ends_out[...] = own_end(even, ye, yo, C1, side)
-        inner = sheet_of(even, ie, io, C2, side)
-        around = sheet_around(store_c, inner, ends_out, edges[side][1], lists[side], side, (gm, gp, go))
-        scaled, weight, _ = weights(k, around)
-        forced = weight * sheet_of(even, ie, io, F1, side)
-        for d in range(6):
-            kept[(side * 7 + d) * SLOTS : (side * 7 + d + 1) * SLOTS] = scaled[d]
-        kept[(side * 7 + 6) * SLOTS : (side * 7 + 7) * SLOTS] = forced
-        ends_out[...] = own_end(even, ye, yo, V1, side)
-        inner = sheet_of(even, ie, io, V2, side)
-        around = sheet_around(store, inner, ends_out, edges[side][0], lists[side], side, (gm, gp, go))
-        total = forced + (1.0 - OMEGA) * store[:SLOTS]
-        for d in range(6):
-            total = total + scaled[d] * around[d]
-        store[:SLOTS] = total
+    for side in range(2):
+        iterate = [sheet_of(even, ie, io, V + depth, side) for depth in range(depths + 1)]
+        conduct = [sheet_of(even, ie, io, C + depth, side) for depth in range(depths + 1)]
+        for depth in range(depths):
+            fill_sheet(stores[side][depth], iterate[depth])
+            fill_sheet(stores[side][3 + depth], conduct[depth])
+        ends_out[...] = own_end(even, ye, yo, V, side)
+        outer = beyond(ends_out, lists[side], side, touching)
+        ends_out[...] = own_end(even, ye, yo, C, side)
+        outer_c = beyond(ends_out, lists[side], side, touching)
+        fresh = []
+        for depth in range(depths):
+            around_c = sheet_around(
+                stores[side][3 + depth], conduct[depth + 1], outer_c, edges[side][3 + depth], lists[side], side,
+                (minus, plus),
+            )
+            scaled, weight, _ = weights(conduct[depth], around_c)
+            forced = weight * sheet_of(even, ie, io, F + depth, side)
+            if depth < DEPTHS[1]:
+                for d in range(6):
+                    keep_layers(kept, kept_index(side, depth) + d, scaled[d])
+                keep_layers(kept, kept_index(side, depth) + 6, forced)
+            around = sheet_around(
+                stores[side][depth], iterate[depth + 1], outer, edges[side][depth], lists[side], side, (minus, plus)
+            )
+            fresh.append(swept(iterate[depth], forced, scaled, around))
+            outer, outer_c = iterate[depth], conduct[depth]
+        for depth in range(depths):
+            fill_sheet(stores[side][depth], fresh[depth])
+            keep_layers(sheets, side * depths + depth, fresh[depth])
+    pack_lines([stores[side][: DEPTHS[1]] for side in range(2)], lists, ys, 2, 3)
+    below, above = stores[0][0], stores[1][0]
     sweep_blocks((v, forth_in, back_in), mine, ghost, below, above, wk, wf, u, forth, back, faces)
-    pick_faces(faces, mine, ys, 0, 2)
-    for j in range(SLOTS):
-        for depth in range(2):
-            layer_tile(u, j * EDGE + EDGE - 1 - depth, ends_out, 0)
-            layer_tile(u, j * EDGE + depth, ends_out, 1)
-            ze[depth * SLOTS + j] = jnp.where(even, ends_out[0], ends_out[1])
-            zo[depth * SLOTS + j] = jnp.where(even, ends_out[1], ends_out[0])
+    pick_faces(faces, mine, ys, 0, 3)
 
 
 def second(turned, wk, wf, sent, got, ya, mine, parity, lists):
@@ -598,8 +666,9 @@
         second_kernel,
         in_specs=[SMEM] * 3 + [VMEM] * 10,
         out_specs=[VMEM] * 7,
-        out_shape=[f32(*FIELD), f32(*TURNED), f32(*TURNED), tiles(2 * SLOTS), tiles(2 * SLOTS), tiles(FACES), tiles(14 * SLOTS)],
-        scratch_shapes=[GHOSTS] + [SHEET] * 8 + GATHERED + [scratch(FACES, *TILE), scratch(SLOTS, *TILE)],
+        out_shape=[f32(*FIELD), f32(*TURNED), f32(*TURNED), tiles(3 * SLOTS)]
+        + [tiles(28 * SLOTS), tiles(2 * DEPTHS[0] * SLOTS), tiles(2 * SLOTS)],
+        scratch_shapes=[GHOSTS, scratch(FACES, *TILE), scratch(SLOTS, *TILE)] + GATHERED + [SHEET] * 24,
         compiler_params=params(16),
         cost_estimate=cost(1 << 22, 9 << 20),
         name="second",
@@ -607,56 +676,56 @@
 
 
 def third_kernel(
-    mine, parity, lists_in,
-    v, forth_in, back_in, wk, wf, ie, io, ya,
-    u, forth, back, ys,
-    ghost, below, above, faces,
+    mine, lists_in,
+    v, forth_in, back_in, wk, wf, kept, sheets_in, ends_in, ya,
+    u, forth, back, ys, sheets, ends,
+    ghost, faces, minus, plus, touching, *sheet_refs,
 ):
-    even = parity[0] == 0
     lists = [Lists(lists_in, side) for side in range(2)]
-    place_faces(ya, mine, ghost, 0, 2)
-    for side, store in enumerate((below, above)):
-        fill_sheet(store, sheet_of(even, ie, io, V1, side))
-    pack_lines(((below,), (above,)), lists, ys, 2, 3)
+    place_faces(ya, mine, ghost, 0, 3)
+    own_ends(v, ends)
+    depths = DEPTHS[1]
+    stores, edges = (sheet_refs[:2], sheet_refs[2:4]), (sheet_refs[4:6], sheet_refs[6:])
+    place_lines(ya, lists, edges, 2, 3)
+    sweep_sheets(sheets_in, ends_in, kept, depths, stores, edges, lists, (minus, plus, touching))
+    for side in range(2):
+        for depth in range(depths):
+            keep_layers(sheets, side * depths + depth, stores[side][depth][:SLOTS])
+    pack_lines([stores[side][: DEPTHS[2]] for side in range(2)], lists, ys, 2, 3)
+    below, above = stores[0][0], stores[1][0]
     sweep_blocks((v, forth_in, back_in), mine, ghost, below, above, wk, wf, u, forth, back, faces)
     pick_faces(faces, mine, ys, 0, 3)
 
 
-def third(turned, wk, wf, got, ya, mine, parity, lists):
+def third(turned, wk, wf, kept, sheets, ends, ya, mine, lists):
     return pl.pallas_call(
         third_kernel,
-        in_specs=[SMEM] * 3 + [VMEM] * 8,
-        out_specs=[VMEM] * 4,
-        out_shape=[f32(*FIELD), f32(*TURNED), f32(*TURNED), tiles(3 * SLOTS)],
-        scratch_shapes=[GHOSTS] + [SHEET] * 2 + [scratch(FACES, *TILE)],
+        in_specs=[SMEM] * 2 + [VMEM] * 9,
+        out_specs=[VMEM] * 6,
+        out_shape=[f32(*FIELD), f32(*TURNED), f32(*TURNED), tiles(3 * SLOTS)]
+        + [tiles(2 * DEPTHS[1] * SLOTS), tiles(2 * SLOTS)],
+        scratch_shapes=[GHOSTS, scratch(FACES, *TILE)] + GATHERED + [SHEET] * 8,
         compiler_params=params(16),
         cost_estimate=cost(1 << 22, 9 << 20),
         name="third",
-    )(mine, parity, lists, *turned, wk, wf, *got, ya)
+    )(mine, lists, *turned, wk, wf, kept, sheets, ends, ya)
 
 
 def last_kernel(
-    mine, parity, lists_in,
-    v, forth_in, back_in, wk, wf, dg, kept, ye, yo, ie, io, ya,
+    mine, lists_in,
+    v, forth_in, back_in, wk, wf, dg, kept, sheets_in, ends_in, ya,
     out, coarse,
-    ghost, below, above, edge_b, edge_a, gm, gp, go, ends_out, residual, sem,
+    ghost, below, above, edge_b, edge_a, minus, plus, touching, residual, sem,
 ):
     write = pltpu.make_async_copy(v, out, sem)
     write.start()
-    even = parity[0] == 0
     lists = [Lists(lists_in, side) for side in range(2)]
     place_faces(ya, mine, ghost, 0, 3)
     edges = ((edge_b,), (edge_a,))
     place_lines(ya, lists, edges, 2, 3)
-    for side, store in enumerate((below, above)):
-        fill_sheet(store, sheet_of(even, ie, io, V1, side))
-        ends_out[...] = own_end(even, ye, yo, V1, side)
-        inner = sheet_of(even, ie, io, V2, side)
-        around = sheet_around(store, inner, ends_out, edges[side][0], lists[side], side, (gm, gp, go))
-        total = kept[(side * 7 + 6) * SLOTS : (side * 7 + 7) * SLOTS] + (1.0 - OMEGA) * store[:SLOTS]
-        for d in range(6):
-            total = total + kept[(side * 7 + d) * SLOTS : (side * 7 + d + 1) * SLOTS] * around[d]
-        store[:SLOTS] = total
+    sweep_sheets(
+        sheets_in, ends_in, kept, DEPTHS[2], ((below,), (above,)), edges, lists, (minus, plus, touching)
+    )
 
     def one(j, carry):
         rows = block_rows(j)
@@ -687,18 +756,20 @@
     write.wait()
 
 
-def last(turned, wk, wf, dg, kept, sent, got, ya, mine, parity, lists):
+def last(turned, wk, wf, dg, kept, sheets, ends, ya, mine, lists):
     return pl.pallas_call(
         last_kernel,
-        in_specs=[SMEM] * 3 + [VMEM] * 12,
+        in_specs=[SMEM] * 2 + [VMEM] * 10,
         out_specs=[HBM, VMEM],
         out_shape=[f32(*FIELD), f32(ROWS // 2, PLANE // 4)],
-        scratch_shapes=[GHOSTS] + [SHEET] * 4 + GATHERED + [scratch(SLOTS, *TILE), scratch(COLS, ROWS, LANES), pltpu.SemaphoreType.DMA]
-       ,
+        scratch_shapes=[GHOSTS]
+        + [SHEET] * 4
+        + GATHERED
+        + [scratch(COLS, ROWS, LANES), pltpu.SemaphoreType.DMA],
         compiler_params=params(16),
         cost_estimate=cost(1 << 24, 10 << 20),
         name="last",
-    )(mine, parity, lists, *turned, wk, wf, dg, kept, *sent, *got, ya)
+    )(mine, lists, *turned, wk, wf, dg, kept, sheets, ends, ya)
 
 
 def pair_swap(values, stride):
@@ -733,10 +804,9 @@
     sent, got, ya = (ze, zo), (pair_swap(ze, 1), odd_pair_swap(zo)), segment_swap(ys)
     wk, wf, dg, v, forth, back, ys, lists = first(merged, bulk, got, ya, swap_slot, owner, mine, parity)
     turned = v, forth, back
-    *turned, ze, zo, ys, kept = second(turned, wk, wf, sent, got, segment_swap(ys), mine, parity, lists)
-    sent, got = (ze, zo), (pair_swap(ze, 1), odd_pair_swap(zo))
-    *turned, ys = third(turned, wk, wf, got, segment_swap(ys), mine, parity, lists)
-    v, coarse = last(turned, wk, wf, dg, kept, sent, got, segment_swap(ys), mine, parity, lists)
+    *turned, ys, kept, sheets, ends_of = second(turned, wk, wf, sent, got, segment_swap(ys), mine, parity, lists)
+    *turned, ys, sheets, ends_of = third(turned, wk, wf, kept, sheets, ends_of, segment_swap(ys), mine, lists)
+    v, coarse = last(turned, wk, wf, dg, kept, sheets, ends_of, segment_swap(ys), mine, lists)
     return v.reshape(SLOTS, EDGE, PLANE), coarse.reshape(SLOTS, EDGE // 2, PLANE // 4)
 
 

time: 91.2 us -> 87.9 us (0.964); the launches traced: 89.4 us -> 87.3 us
  starting transfers between devices: 17.6 us -> 14.1 us
  blocking collectives: 34.6 us -> 35.6 us
    ppermute x2 -> x1, starting transfers between devices: 9.05 us -> 5.67 us  [odd_pair_swap(): lax.ppermute(values, 'owner', [(i, (i - 1 ^ 1) + 1) for i in range(1, cou...]
    all_to_all x4, blocking collectives: 34.6 us -> 35.6 us  [segment_swap(): return lax.all_to_all(ys, 'sub', split_axis=0, concat_axis=0, tiled=True)]
    ppermute x6 -> x5, waiting for transfers between devices: 8.59 us -> 8.36 us  [pair_swap(): lax.ppermute(values, 'owner', [(i, i ^ stride) for i in range(count)])]
    ppermute x6 -> x5, starting transfers between devices: 8.54 us -> 8.45 us  [pair_swap(): lax.ppermute(values, 'owner', [(i, i ^ stride) for i in range(count)])]
  transfers between devices with their start and end apart: 8 -> 6, of which waited for: 3 -> 2; matrix products, arithmetic and copies ran while one was open for 0% -> 0% of each run, Pallas kernels for 6% -> 6%
where the time goes in v4:
time: 87.9 us; the launch traced here: 87.3 us
  blocking collectives  35.6 us (41%)
  Pallas kernels  28.5 us (32%)
  starting transfers between devices  14.1 us (16%)
  waiting for transfers between devices  8.36 us (10%)
    all_to_all x4, blocking collectives, segment_swap(): return lax.all_to_all(ys, 'sub', split_axis=0, concat_axis=0, tiled=True)  35.6 us
    ppermute x5, starting transfers between devices, pair_swap(): lax.ppermute(values, 'owner', [(i, i ^ stride) for i in range(count)])  8.45 us
    ppermute x5, waiting for transfers between devices, pair_swap(): lax.ppermute(values, 'owner', [(i, i ^ stride) for i in range(count)])  8.36 us
    pallas_call x1, Pallas kernels, first(): pl.pallas_call(first_kernel, in_specs=[SMEM] * 4 + [VMEM] * (3 + BITS + l...  7.73 us
    ppermute x1, starting transfers between devices, odd_pair_swap(): lax.ppermute(values, 'owner', [(i, (i - 1 ^ 1) + 1) for i in range(1, cou...  5.67 us
    pallas_call x1, Pallas kernels, local(): pl.pallas_call(local_kernel, in_specs=[SMEM] * 4 + [HBM] * 3, out_specs=[...  5.5 us
    pallas_call x1, Pallas kernels, second(): pl.pallas_call(second_kernel, in_specs=[SMEM] * 3 + [VMEM] * 10, out_spec...  4.45 us
    pallas_call x1, Pallas kernels, third(): pl.pallas_call(third_kernel, in_specs=[SMEM] * 2 + [VMEM] * 9, out_specs=...  3.81 us
  transfers between devices with their start and end apart: 6, of which 2 were waited for; matrix products, arithmetic and copies ran while one was open for 0% of the time, Pallas kernels for 6%

profile of v4, /device:TPU:32, one launch (start us, length us, event | category | flops | bytes accessed | tf_op | source)
XLA Modules:
  0.0 87.3 jit_solution(17269935727151517878)
XLA Ops:
  0.6 0.0 copy-start
  0.6 2.3 %swap_pack.1 = (f32[96,1024]{1,0:T(8,128)S(1)}, f32[96,1024]{1,0:T(8,128)S(1)}, f32[96,1024]{1,0:T(8,128)S(1)}, f32[96,1024]{1,0:T(8,128)S(1)}) custom-call(s32[1,16]{1,0:T(1,128)} %pairs.3, s32[1]{0:T(128)} %bitcast.3.refs_1_.owner, s32[8]{0:T(128)} %refs_2_.1, f32[256,1024]{1,0:T(8,128)} %bitcast.7, f32[256,1024]{1,0:T(8,128)} %bitcast.9, f32[256,1024]{1,0:T(8,128)} %bitcast.11), custom_call_target="tpu_custom_call" | custom-call | flops 524288 | bytes 3145728 | tf_op jit(solution)/shard_map/swap_pack/pallas_call | solution.py:404
  2.9 0.1 collective-permute-start
  3.0 1.6 %collective-permute-start.1 = (f32[96,1024]{1,0:T(8,128)S(1)}, f32[96,1024]{1,0:T(8,128)S(1)}, u32[]{:S(2)}, u32[]{:S(2)}) collective-permute-start(f32[96,1024]{1,0:T(8,128)S(1)} %get-tuple-element.48), channel_id=1, source_target_pairs={{0,8},{8,0},{16,24},{24,16},{32,40},{40,32},{48,56},{56,48},{64,72... | collective-permute-start | bytes 1179656 | tf_op jit(solution)/shard_map/ppermute | solution.py:777
  4.6 3.3 %collective-permute-start.2 = (f32[96,1024]{1,0:T(8,128)S(1)}, f32[96,1024]{1,0:T(8,128)S(1)}, u32[]{:S(2)}, u32[]{:S(2)}) collective-permute-start(f32[96,1024]{1,0:T(8,128)S(1)} %get-tuple-element.49), channel_id=1, source_target_pairs={{0,64},{8,72},{16,80},{24,88},{32,96},{40,104},{48,112},{56,120},{... | collective-permute-start | bytes 1179656 | tf_op jit(solution)/shard_map/ppermute | solution.py:777
  7.9 2.9 %collective-permute-start.3 = (f32[96,1024]{1,0:T(8,128)S(1)}, f32[96,1024]{1,0:T(8,128)S(1)}, u32[]{:S(2)}, u32[]{:S(2)}) collective-permute-start(f32[96,1024]{1,0:T(8,128)S(1)} %get-tuple-element.50), channel_id=1, source_target_pairs={{0,16},{8,24},{16,0},{24,8},{32,48},{40,56},{48,32},{56,40},{64,80... | collective-permute-start | bytes 1179656 | tf_op jit(solution)/shard_map/ppermute | solution.py:777
  10.8 0.0 copy-done
  10.8 0.1 copy.17.neighbours
  10.9 5.5 %local.1 = (f32[88,8,128]{2,1,0:T(8,128)S(1)}, f32[88,8,128]{2,1,0:T(8,128)S(1)}, f32[32,8,128]{2,1,0:T(8,128)S(1)}, s32[64]{0:T(128)S(1)}, f32[256,1024]{1,0:T(...) custom-call(s32[8]{0:T(128)} %refs_2_.1, ...), custom_call_target="tpu_custom_call" | custom-call | flops 1048576 | bytes 4194304 | tf_op jit(solution)/shard_map/local/pallas_call | solution.py:458
  16.4 0.0 collective-permute-done.refs_0_
  16.4 0.0 collective-permute-done.1.refs_1_
  16.4 7.2 %collective-permute-done.2.refs_2_ = f32[96,1024]{1,0:T(8,128)S(1)} collective-permute-done((f32[96,1024]{1,0:T(8,128)S(1)}, f32[96,1024]{1,0:T(8,128)S(1)}, u32[]{:S(2)}, u32[]{:S(2)}) %collective-permute-start.2) | collective-permute-done | bytes 393248 | tf_op jit(solution)/shard_map/ppermute | solution.py:777
  23.6 1.2 %collective-permute-done.3.refs_3_ = f32[96,1024]{1,0:T(8,128)S(1)} collective-permute-done((f32[96,1024]{1,0:T(8,128)S(1)}, f32[96,1024]{1,0:T(8,128)S(1)}, u32[]{:S(2)}, u32[]{:S(2)}) %collective-permute-start.3) | collective-permute-done | bytes 393248 | tf_op jit(solution)/shard_map/ppermute | solution.py:777
  24.8 1.0 %ends.1 = (f32[89,8,128]{2,1,0:T(8,128)S(1)}, f32[89,8,128]{2,1,0:T(8,128)S(1)}, f32[32,8,128]{2,1,0:T(8,128)S(1)}) custom-call(s32[1,16]{1,0:T(1,128)} %pairs.3, s32[1]{0:T(128)} %bitcast.3.refs_1_.owner, s32[64]{0:T(128)S(1)} %get-tuple-element.43.mine, s32[1]{0:T(128)} %bitcast.4.parity, f32[88,8,128]{2,1,0:T(8,128)S(1)} %get-tuple-element.44.top, ...), custom_call_target="tpu_custom_call" | custom-call | flops 262144 | bytes 1048576 | tf_op jit(solution)/shard_map/ends/pallas_call | solution.py:499
  25.8 0.5 collective-permute-start.4
  26.3 5.7 %collective-permute-start.5 = (f32[89,8,128]{2,1,0:T(8,128)S(1)}, f32[89,8,128]{2,1,0:T(8,128)S(1)}, u32[]{:S(2)}, u32[]{:S(2)}) collective-permute-start(f32[89,8,128]{2,1,0:T(8,128)S(1)} %get-tuple-element.52.yo), channel_id=1, source_target_pairs={{8,16},{16,8},{24,32},{32,24},{40,48},{48,40},{56,64},{64,56},{72,... | collective-permute-start | bytes 1093640 | tf_op jit(solution)/shard_map/ppermute | solution.py:782
  32.0 10.2 %all_to_all.20.ya = f32[32,8,128]{2,1,0:T(8,128)S(1)} all-to-all(f32[32,8,128]{2,1,0:T(8,128)S(1)} %get-tuple-element.53), channel_id=1, replica_groups=mesh['owner'=16,'sub'=8] {'sub'}, dimensions={0} | all-to-all | bytes 262144 | tf_op jit(solution)/shard_map/all_to_all | solution.py:790
  42.2 0.0 collective-permute-done.4.ie
  42.2 0.0 collective-permute-done.5.io
  42.2 7.7 %first.1 = (f32[256,1024]{1,0:T(8,128)S(1)}, f32[256,1024]{1,0:T(8,128)S(1)}, f32[256,1024]{1,0:T(8,128)S(1)}, f32[288,1024]{1,0:T(8,128)S(1)}, f32[288,1024]{1,...) custom-call(s32[1,16]{1,0:T(1,128)} %pairs.3, ...), custom_call_target="tpu_custom_call", output_to_operand_aliasing={{0}: (11, {}), {1}: (12, {}), {2}: (13, {}), {3}: (14, {}),... | custom-call | flops 16777216 | bytes 12582912 | tf_op jit(solution)/shard_map/first/pallas_call | solution.py:594
  50.0 9.0 %all_to_all.21.ya = f32[24,8,128]{2,1,0:T(8,128)S(1)} all-to-all(f32[24,8,128]{2,1,0:T(8,128)S(1)} %get-tuple-element.67), channel_id=1, replica_groups=mesh['owner'=16,'sub'=8] {'sub'}, dimensions={0} | all-to-all | bytes 196608 | tf_op jit(solution)/shard_map/all_to_all | solution.py:790
  58.9 4.4 %second.1 = (f32[256,1024]{1,0:T(8,128)S(1)}, f32[288,1024]{1,0:T(8,128)S(1)}, f32[288,1024]{1,0:T(8,128)S(1)}, f32[24,8,128]{2,1,0:T(8,128)S(1)}, f32[224,8,128...) custom-call(s32[64]{0:T(128)S(1)} %get-tuple-element.43.mine, s32[1]{0:T(128)} %bitcast.4.parity, ...), custom_call_target="tpu_custom_call" | custom-call | flops 4194304 | bytes 9437184 | tf_op jit(solution)/shard_map/second/pallas_call | solution.py:665
  63.4 8.2 %all_to_all.22.ya = f32[24,8,128]{2,1,0:T(8,128)S(1)} all-to-all(f32[24,8,128]{2,1,0:T(8,128)S(1)} %get-tuple-element.74), channel_id=1, replica_groups=mesh['owner'=16,'sub'=8] {'sub'}, dimensions={0} | all-to-all | bytes 196608 | tf_op jit(solution)/shard_map/all_to_all | solution.py:790
  71.6 3.8 %third.1 = (f32[256,1024]{1,0:T(8,128)S(1)}, f32[288,1024]{1,0:T(8,128)S(1)}, f32[288,1024]{1,0:T(8,128)S(1)}, f32[24,8,128]{2,1,0:T(8,128)S(1)}, f32[32,8,128]{2,1,0:T(8,128)S(1)}, /*index=5*/f32[16,8,128]{2,1,0:T(8,128)S(1)}) custom-call(s32[64]{0:T(128)S(1)} %get-tuple-element.43.mine, s32[2,64]{1,0:T(2,128)S(1)} %get-tuple-element.61.lists_in, ...), custom_call_target="tpu_custom_call" | custom-call | flops 4194304 | bytes 9437184 | tf_op jit(solution)/shard_map/third/pallas_call | solution.py:701
  75.4 8.2 %all_to_all.23.ya = f32[24,8,128]{2,1,0:T(8,128)S(1)} all-to-all(f32[24,8,128]{2,1,0:T(8,128)S(1)} %get-tuple-element.81), channel_id=1, replica_groups=mesh['owner'=16,'sub'=8] {'sub'}, dimensions={0} | all-to-all | bytes 196608 | tf_op jit(solution)/shard_map/all_to_all | solution.py:790
  83.6 3.7 %last.1 = (f32[256,1024]{1,0:T(8,128)}, f32[128,256]{1,0:T(8,128)}) custom-call(s32[64]{0:T(128)S(1)} %get-tuple-element.43.mine, s32[2,64]{1,0:T(2,128)S(1)} %get-tuple-element.61.lists_in, f32[256,1024]{1,0:T(8,128)S(1)} %get-tuple-element.75.v, f32[288,1024]{1,0:T(8,128)S(1)} %get-tuple-element.76.forth_in, f32[288,1024]{1,0:T(8,128)S(1)} %get-tuple-element.77.back_in, ...), custom_call_target="tpu_custom_call" | custom-call | flops 16777216 | bytes 10485760 | tf_op jit(solution)/shard_map/last/pallas_call | solution.py:760
Async XLA Ops:
  0.6 10.2 %copy-start = (s32[8,4]{0,1:T(4,128)S(1)}, s32[8,4]{0,1:T(4,128)}, u32[]{:S(2)}) copy-start(s32[8,4]{0,1:T(4,128)} %param.12) | copy-start | bytes 388
  2.9 13.5 %collective-permute-start = (f32[96,1024]{1,0:T(8,128)S(1)}, f32[96,1024]{1,0:T(8,128)S(1)}, u32[]{:S(2)}, u32[]{:S(2)}) collective-permute-start(f32[96,1024]{1,0:T(8,128)S(1)} %get-tuple-element.47), channel_id=1, source_target_pairs={{0,32},{8,40},{16,48},{24,56},{32,0},{40,8},{48,16},{56,24},{64,96... | collective-permute-start | bytes 1179656 | tf_op jit(solution)/shard_map/ppermute | solution.py:777
  3.0 13.4 %collective-permute-start.1 = (f32[96,1024]{1,0:T(8,128)S(1)}, f32[96,1024]{1,0:T(8,128)S(1)}, u32[]{:S(2)}, u32[]{:S(2)}) collective-permute-start(f32[96,1024]{1,0:T(8,128)S(1)} %get-tuple-element.48), channel_id=1, source_target_pairs={{0,8},{8,0},{16,24},{24,16},{32,40},{40,32},{48,56},{56,48},{64,72... | collective-permute-start | bytes 1179656 | tf_op jit(solution)/shard_map/ppermute | solution.py:777
  4.6 18.9 %collective-permute-start.2 = (f32[96,1024]{1,0:T(8,128)S(1)}, f32[96,1024]{1,0:T(8,128)S(1)}, u32[]{:S(2)}, u32[]{:S(2)}) collective-permute-start(f32[96,1024]{1,0:T(8,128)S(1)} %get-tuple-element.49), channel_id=1, source_target_pairs={{0,64},{8,72},{16,80},{24,88},{32,96},{40,104},{48,112},{56,120},{... | collective-permute-start | bytes 1179656 | tf_op jit(solution)/shard_map/ppermute | solution.py:777
  7.9 16.9 %collective-permute-start.3 = (f32[96,1024]{1,0:T(8,128)S(1)}, f32[96,1024]{1,0:T(8,128)S(1)}, u32[]{:S(2)}, u32[]{:S(2)}) collective-permute-start(f32[96,1024]{1,0:T(8,128)S(1)} %get-tuple-element.50), channel_id=1, source_target_pairs={{0,16},{8,24},{16,0},{24,8},{32,48},{40,56},{48,32},{56,40},{64,80... | collective-permute-start | bytes 1179656 | tf_op jit(solution)/shard_map/ppermute | solution.py:777
  25.8 16.5 %collective-permute-start.4 = (f32[89,8,128]{2,1,0:T(8,128)S(1)}, f32[89,8,128]{2,1,0:T(8,128)S(1)}, u32[]{:S(2)}, u32[]{:S(2)}) collective-permute-start(f32[89,8,128]{2,1,0:T(8,128)S(1)} %get-tuple-element.51.ye), channel_id=1, source_target_pairs={{0,8},{8,0},{16,24},{24,16},{32,40},{40,32},{48,56},{56,48},{64,72... | collective-permute-start | bytes 1093640 | tf_op jit(solution)/shard_map/ppermute | solution.py:777
  26.3 15.9 %collective-permute-start.5 = (f32[89,8,128]{2,1,0:T(8,128)S(1)}, f32[89,8,128]{2,1,0:T(8,128)S(1)}, u32[]{:S(2)}, u32[]{:S(2)}) collective-permute-start(f32[89,8,128]{2,1,0:T(8,128)S(1)} %get-tuple-element.52.yo), channel_id=1, source_target_pairs={{8,16},{16,8},{24,32},{32,24},{40,48},{48,40},{56,64},{64,56},{72,... | collective-permute-start | bytes 1093640 | tf_op jit(solution)/shard_map/ppermute | solution.py:782

commit v5 on v4

--- a/solution.py
+++ b/solution.py
@@ -17,7 +17,9 @@
 FACES = 2 * SLOTS
 TILE = (8, LANES)
 BITS = 4
+GROUP = 8
 ORDER = (2, 0, 3, 1)
+SOON, LATE = ORDER[:2], ORDER[2:]
 V, C, F = 0, 4, 8
 KINDS = 11
 DEPTHS = (3, 2, 1)
@@ -293,14 +295,19 @@
 
 
 def weights(k, around):
-    faces = [k + jnp.where(other > 0.0, other, k) for other in around]
+    faces = [k + other for other in around]
     total = (faces[0] + faces[1]) + (faces[2] + faces[3]) + (faces[4] + faces[5])
-    alive = k > 0.0
-    factor = jnp.where(alive, OMEGA / total, 0.0)
-    return [factor * face for face in faces], 2.0 * factor, jnp.where(alive, total * (0.5 / OMEGA), 0.0)
-
-
-def six_turned(field, forth, back, j, mine, ghost, below, above):
+    inverse = pl.reciprocal(total, approx=True)
+    inverse = inverse * (2.0 - total * inverse)
+    factor = jnp.where(k > 0.0, OMEGA * inverse, 0.0)
+    return [factor * face for face in faces], 2.0 * factor, total * (0.5 / OMEGA)
+
+
+def filled(other, own):
+    return jnp.where(other > 0.0, other, own)
+
+
+def six_turned(field, forth, back, j, mine, ghost, below, above, fill=False):
     _, lane = iotas((EDGE, LANES))
     x = lane % EDGE
     xm, xp, zm, zp = [slot_or(mine[4 * j + side], SLOTS) for side in range(4)]
@@ -310,18 +317,20 @@
         v = field[own, column(c)]
         before = forth[own, column(c - 1)] if c else unpack_face(ghost[2 * j], 0)
         after = back[own, column(c + 1)] if c < COLS - 1 else unpack_face(ghost[2 * j + 1], 1)
-        yield (
-            c,
-            v,
-            (
-                pltpu.roll(jnp.where(x == EDGE - 1, back[minus_rows, column(c)], v), 1, 1),
-                pltpu.roll(jnp.where(x == 0, forth[plus_rows, column(c)], v), LANES - 1, 1),
-                jnp.where(lane < EDGE, before, forth[own, column(c)]),
-                jnp.where(lane >= LANES - EDGE, after, back[own, column(c)]),
-                jnp.concatenate([under_face[c : c + 1, :], v[: EDGE - 1]], axis=0),
-                jnp.concatenate([v[1:], over_face[c : c + 1, :]], axis=0),
-            ),
-        )
+        under, over = under_face[c : c + 1, :], over_face[c : c + 1, :]
+        around = [
+            pltpu.roll(jnp.where(x == EDGE - 1, back[minus_rows, column(c)], v), 1, 1),
+            pltpu.roll(jnp.where(x == 0, forth[plus_rows, column(c)], v), LANES - 1, 1),
+            jnp.where(lane < EDGE, before, forth[own, column(c)]),
+            jnp.where(lane >= LANES - EDGE, after, back[own, column(c)]),
+        ]
+        if fill:
+            ends = (True, True, c == 0, c == COLS - 1)
+            around = [filled(other, v) if end else other for other, end in zip(around, ends)]
+            under, over = filled(under, v[:1]), filled(over, v[EDGE - 1 :])
+        around.append(jnp.concatenate([under, v[: EDGE - 1]], axis=0))
+        around.append(jnp.concatenate([v[1:], over], axis=0))
+        yield c, v, around
 
 
 def store_swept(total, n, j, u, forth, back, faces):
@@ -351,11 +360,16 @@
 def sweep_blocks(turned, mine, ghost, below, above, wk, wf, u, forth, back, faces):
     def one(j, carry):
         rows = block_rows(j)
+        ready = []
         for n, centre, around in six_turned(*turned, j, mine, ghost, below, above):
             total = wf[rows, column(n)] + (1.0 - OMEGA) * centre
             for d in range(6):
                 total = total + wk[d, rows, column(n)] * around[d]
-            store_swept(total, n, j, u, forth, back, faces)
+            ready.append((total, n))
+            if len(ready) == GROUP:
+                for total, n in ready:
+                    store_swept(total, n, j, u, forth, back, faces)
+                ready = []
         return carry
 
     lax.fori_loop(0, SLOTS, one, 0)
@@ -470,15 +484,61 @@
     )(occupied, neighbours, send_list, recv_list, *fields)
 
 
+def soon_kernel(pairs, owner, *refs):
+    bulk = dict(zip(SOON, refs))
+    top, bottom, faces, v, f, c, forth_v, back_v, forth_c, back_c, fresh, sems = refs[len(SOON) + 3 + len(MERGED) :]
+
+    def merges(bit, slot):
+        return [
+            pltpu.make_async_copy(bulk[bit].at[pl.ds(k * EDGE, EDGE)], field.at[block_rows(slot)], sems.at[bit, k])
+            for k, field in enumerate((v, f, c))
+        ]
+
+    for bit in SOON:
+        slot = pair_slot(pairs, owner, bit)
+
+        @pl.when(slot >= 0)
+        def _(bit=bit, slot=jnp.maximum(slot, 0)):
+            for copy in merges(bit, slot):
+                copy.start()
+            block_tiles(*(bulk[bit].at[pl.ds(k * EDGE, EDGE)] for k in range(3)), 0, fresh)
+            for kind in range(KINDS):
+                top[kind * SLOTS + slot] = fresh[kind]
+                bottom[kind * SLOTS + slot] = fresh[KINDS + kind]
+            for k in range(2):
+                for side in range(2):
+                    faces[k * FACES + 2 * slot + side] = fresh[2 * KINDS + 2 * k + side]
+            for copy in merges(bit, slot):
+                copy.wait()
+            turn_block(v, slot, forth_v, back_v)
+            turn_block(c, slot, forth_c, back_c)
+
+
+def soon(tops, merged, bulk, pairs, owner):
+    count = 3 + len(MERGED)
+    outs = pl.pallas_call(
+        soon_kernel,
+        in_specs=[SMEM] * 2 + [VMEM] * (len(SOON) + count),
+        out_specs=[VMEM] * count,
+        out_shape=[tiles(KINDS * SLOTS)] * 2 + [tiles(2 * FACES)] + MERGED,
+        input_output_aliases={2 + len(SOON) + k: k for k in range(count)},
+        scratch_shapes=[scratch(2 * KINDS + 4, *TILE), pltpu.SemaphoreType.DMA((BITS, 3))],
+        compiler_params=params(8),
+        cost_estimate=cost(1 << 18, 2 << 20),
+        name="soon",
+    )(pairs, owner, *bulk, *tops, *merged)
+    return outs[:3], outs[3:]
+
+
 def ends_kernel(pairs, owner, mine, parity, top, bottom, faces, *refs):
-    bulk = dict(zip(ORDER, refs))
-    ze, zo, ys, held, fresh = refs[BITS:]
+    bulk = dict(zip(LATE, refs))
+    ze, zo, ys, held, fresh = refs[len(LATE) :]
     even = parity[0] == 0
     ze[: KINDS * SLOTS] = jnp.where(even, top[...], bottom[...])
     zo[: KINDS * SLOTS] = jnp.where(even, bottom[...], top[...])
     ze[KINDS * SLOTS] = zo[KINDS * SLOTS] = lists_tile(mine)
     held[...] = faces[...]
-    for bit in range(BITS):
+    for bit in LATE:
         slot = pair_slot(pairs, owner, bit)
 
         @pl.when(slot >= 0)
@@ -498,7 +558,7 @@
 def ends(top, bottom, faces, bulk, pairs, owner, mine, parity):
     return pl.pallas_call(
         ends_kernel,
-        in_specs=[SMEM] * 4 + [VMEM] * (3 + BITS),
+        in_specs=[SMEM] * 4 + [VMEM] * (3 + len(LATE)),
         out_specs=[VMEM] * 3,
         out_shape=[tiles(KINDS * SLOTS + 1)] * 2 + [tiles(2 * FACES)],
         scratch_shapes=[scratch(2 * FACES, *TILE), scratch(2 * KINDS + 4, *TILE)],
@@ -509,15 +569,15 @@
 
 
 def first_kernel(pairs, owner, mine, parity, ie, io, ya, *refs):
-    bulk, refs = dict(zip(ORDER, refs)), refs[BITS + len(MERGED) :]
+    bulk, refs = dict(zip(LATE, refs)), refs[len(LATE) + len(MERGED) :]
     v, f, c, forth_v, back_v, forth_c, back_c = refs[: len(MERGED)]
     wk, wf, dg, u, forth, back, ys, lists_out = refs[len(MERGED) : len(MERGED) + 8]
     ghost, ghost_c, faces, held, list_sems, sems, *sheet_refs = refs[len(MERGED) + 8 :]
     even = parity[0] == 0
-    slots = [pair_slot(pairs, owner, bit) for bit in range(BITS)]
+    slots = {bit: pair_slot(pairs, owner, bit) for bit in LATE}
 
     def merges(k):
-        for bit in range(BITS):
+        for bit in LATE:
             copy = pltpu.make_async_copy(
                 bulk[bit].at[pl.ds(k * EDGE, EDGE)],
                 (v, f, c)[k].at[block_rows(jnp.maximum(slots[bit], 0))],
@@ -563,7 +623,7 @@
 
     def one(j, carry):
         rows = block_rows(j)
-        conduct = six_turned(c, forth_c, back_c, j, mine, ghost_c, below_c, above_c)
+        conduct = six_turned(c, forth_c, back_c, j, mine, ghost_c, below_c, above_c, fill=True)
         iterate = six_turned(v, forth_v, back_v, j, mine, ghost, below, above)
         for (n, k, around_k), (_, centre, around) in zip(conduct, iterate):
             scaled, weight, inverse = weights(k, around_k)
@@ -593,14 +653,14 @@
 def first(merged, bulk, ends_in, ya, pairs, owner, mine, parity):
     outs = pl.pallas_call(
         first_kernel,
-        in_specs=[SMEM] * 4 + [VMEM] * (3 + BITS + len(MERGED)),
+        in_specs=[SMEM] * 4 + [VMEM] * (3 + len(LATE) + len(MERGED)),
         out_specs=[VMEM] * (len(MERGED) + 7) + [SMEM],
         out_shape=MERGED
         + [f32(6, *FIELD)]
         + [f32(*FIELD)] * 3
         + [f32(*TURNED)] * 2
         + [tiles(3 * SLOTS), jax.ShapeDtypeStruct((2, LISTS), jnp.int32)],
-        input_output_aliases={7 + BITS + k: k for k in range(len(MERGED))},
+        input_output_aliases={7 + len(LATE) + k: k for k in range(len(MERGED))},
         scratch_shapes=[GHOSTS] * 2
         + [scratch(FACES, *TILE), pltpu.SMEM((2,) + TILE, jnp.float32), pltpu.SemaphoreType.DMA((2,))]
         + [pltpu.SemaphoreType.DMA((BITS, 3))]
@@ -641,7 +701,7 @@
                 stores[side][3 + depth], conduct[depth + 1], outer_c, edges[side][3 + depth], lists[side], side,
                 (minus, plus),
             )
-            scaled, weight, _ = weights(conduct[depth], around_c)
+            scaled, weight, _ = weights(conduct[depth], [filled(other, conduct[depth]) for other in around_c])
             forced = weight * sheet_of(even, ie, io, F + depth, side)
             if depth < DEPTHS[1]:
                 for d in range(6):
@@ -800,9 +860,10 @@
     bulk = swap_pack(fields, occupied, swap_slot, owner, ORDER)
     bulk = [pair_swap(block, 1 << bit) for bit, block in zip(ORDER, bulk)]
     top, bottom, faces, mine, *merged = local(fields, occupied, neighbours, in_hbm(send_list), in_hbm(recv_list))
-    ze, zo, ys = ends(top, bottom, faces, bulk, swap_slot, owner, mine, parity)
+    (top, bottom, faces), merged = soon((top, bottom, faces), merged, bulk[:2], swap_slot, owner)
+    ze, zo, ys = ends(top, bottom, faces, bulk[2:], swap_slot, owner, mine, parity)
     sent, got, ya = (ze, zo), (pair_swap(ze, 1), odd_pair_swap(zo)), segment_swap(ys)
-    wk, wf, dg, v, forth, back, ys, lists = first(merged, bulk, got, ya, swap_slot, owner, mine, parity)
+    wk, wf, dg, v, forth, back, ys, lists = first(merged, bulk[2:], got, ya, swap_slot, owner, mine, parity)
     turned = v, forth, back
     *turned, ys, kept, sheets, ends_of = second(turned, wk, wf, sent, got, segment_swap(ys), mine, parity, lists)
     *turned, ys, sheets, ends_of = third(turned, wk, wf, kept, sheets, ends_of, segment_swap(ys), mine, lists)

time: 87.9 us -> 86.5 us (0.984)
  waiting for transfers between devices: 8.36 us -> 5.69 us
  Pallas kernels: 28.5 us -> 29.8 us
    ppermute x5, waiting for transfers between devices: 8.36 us -> 5.68 us  [pair_swap(): lax.ppermute(values, 'owner', [(i, i ^ stride) for i in range(count)])]
    pallas_call x2 -> x3, Pallas kernels: 8.7 us -> 10.5 us  [the longest x1 7.02 us: first(): pl.pallas_call(first_kernel, in_specs=[SMEM] * 4 + [VMEM] * (3 + len(LATE...]
  transfers between devices with their start and end apart: 6 -> 6, of which waited for: 2 -> 2; matrix products, arithmetic and copies ran while one was open for 0% -> 0% of each run, Pallas kernels for 6% -> 9%
where the time goes in v5:
time: 86.5 us; the launch traced here: 85.9 us
  blocking collectives  35.5 us (41%)
  Pallas kernels  29.8 us (34%)
  starting transfers between devices  14.1 us (16%)
  waiting for transfers between devices  5.69 us (7%)
    all_to_all x4, blocking collectives, segment_swap(): return lax.all_to_all(ys, 'sub', split_axis=0, concat_axis=0, tiled=True)  35.5 us
    ppermute x5, starting transfers between devices, pair_swap(): lax.ppermute(values, 'owner', [(i, i ^ stride) for i in range(count)])  8.51 us
    pallas_call x1, Pallas kernels, first(): pl.pallas_call(first_kernel, in_specs=[SMEM] * 4 + [VMEM] * (3 + len(LATE...  7.02 us
    ppermute x5, waiting for transfers between devices, pair_swap(): lax.ppermute(values, 'owner', [(i, i ^ stride) for i in range(count)])  5.68 us
    ppermute x1, starting transfers between devices, odd_pair_swap(): lax.ppermute(values, 'owner', [(i, (i - 1 ^ 1) + 1) for i in range(1, cou...  5.57 us
    pallas_call x1, Pallas kernels, local(): pl.pallas_call(local_kernel, in_specs=[SMEM] * 4 + [HBM] * 3, out_specs=[...  5.51 us
    pallas_call x1, Pallas kernels, second(): pl.pallas_call(second_kernel, in_specs=[SMEM] * 3 + [VMEM] * 10, out_spec...  4.24 us
    pallas_call x1, Pallas kernels, last(): pl.pallas_call(last_kernel, in_specs=[SMEM] * 2 + [VMEM] * 10, out_specs=...  3.78 us
  transfers between devices with their start and end apart: 6, of which 2 were waited for; matrix products, arithmetic and copies ran while one was open for 0% of the time, Pallas kernels for 9%

profile of v5, /device:TPU:32, one launch (start us, length us, event | category | flops | bytes accessed | tf_op | source)
XLA Modules:
  0.0 85.9 jit_solution(14505588161506167672)
XLA Ops:
  0.6 0.0 copy-start
  0.6 2.3 %swap_pack.1 = (f32[96,1024]{1,0:T(8,128)S(1)}, f32[96,1024]{1,0:T(8,128)S(1)}, f32[96,1024]{1,0:T(8,128)S(1)}, f32[96,1024]{1,0:T(8,128)S(1)}) custom-call(s32[1,16]{1,0:T(1,128)} %pairs.5, s32[1]{0:T(128)} %bitcast.3.refs_1_.owner, s32[8]{0:T(128)} %refs_2_.1, f32[256,1024]{1,0:T(8,128)} %bitcast.7, f32[256,1024]{1,0:T(8,128)} %bitcast.9, f32[256,1024]{1,0:T(8,128)} %bitcast.11), custom_call_target="tpu_custom_call" | custom-call | flops 524288 | bytes 3145728 | tf_op jit(solution)/shard_map/swap_pack/pallas_call | solution.py:418
  2.9 0.1 collective-permute-start
  3.0 1.7 %collective-permute-start.1 = (f32[96,1024]{1,0:T(8,128)S(1)}, f32[96,1024]{1,0:T(8,128)S(1)}, u32[]{:S(2)}, u32[]{:S(2)}) collective-permute-start(f32[96,1024]{1,0:T(8,128)S(1)} %get-tuple-element.55), channel_id=1, source_target_pairs={{0,8},{8,0},{16,24},{24,16},{32,40},{40,32},{48,56},{56,48},{64,72... | collective-permute-start | bytes 1179656 | tf_op jit(solution)/shard_map/ppermute | solution.py:837
  4.7 3.3 %collective-permute-start.2 = (f32[96,1024]{1,0:T(8,128)S(1)}, f32[96,1024]{1,0:T(8,128)S(1)}, u32[]{:S(2)}, u32[]{:S(2)}) collective-permute-start(f32[96,1024]{1,0:T(8,128)S(1)} %get-tuple-element.69), channel_id=1, source_target_pairs={{0,64},{8,72},{16,80},{24,88},{32,96},{40,104},{48,112},{56,120},{... | collective-permute-start | bytes 1179656 | tf_op jit(solution)/shard_map/ppermute | solution.py:837
  7.9 2.9 %collective-permute-start.3 = (f32[96,1024]{1,0:T(8,128)S(1)}, f32[96,1024]{1,0:T(8,128)S(1)}, u32[]{:S(2)}, u32[]{:S(2)}) collective-permute-start(f32[96,1024]{1,0:T(8,128)S(1)} %get-tuple-element.70), channel_id=1, source_target_pairs={{0,16},{8,24},{16,0},{24,8},{32,48},{40,56},{48,32},{56,40},{64,80... | collective-permute-start | bytes 1179656 | tf_op jit(solution)/shard_map/ppermute | solution.py:837
  10.8 0.0 copy-done
  10.8 0.1 copy.27.neighbours
  10.9 5.5 %local.1 = (f32[88,8,128]{2,1,0:T(8,128)S(1)}, f32[88,8,128]{2,1,0:T(8,128)S(1)}, f32[32,8,128]{2,1,0:T(8,128)S(1)}, s32[64]{0:T(128)S(1)}, f32[256,1024]{1,0:T(...) custom-call(s32[8]{0:T(128)} %refs_2_.1, ...), custom_call_target="tpu_custom_call" | custom-call | flops 1048576 | bytes 4194304 | tf_op jit(solution)/shard_map/local/pallas_call | solution.py:472
  16.4 0.0 collective-permute-done.refs_0_
  16.5 0.0 collective-permute-done.1.refs_1_
  16.5 2.6 %soon.1 = (f32[88,8,128]{2,1,0:T(8,128)S(1)}, f32[88,8,128]{2,1,0:T(8,128)S(1)}, f32[32,8,128]{2,1,0:T(8,128)S(1)}, f32[256,1024]{1,0:T(8,128)S(1)}, f32[256,102...) custom-call(s32[1,16]{1,0:T(1,128)} %pairs.5, ...), custom_call_target="tpu_custom_call", output_to_operand_aliasing={{0}: (4, {}), {1}: (5, {}), {2}: (6, {}), {3}: (7, {}), {4}... | custom-call | flops 262144 | bytes 2097152 | tf_op jit(solution)/shard_map/soon/pallas_call | solution.py:519
  19.1 4.5 %collective-permute-done.2.refs_0_ = f32[96,1024]{1,0:T(8,128)S(1)} collective-permute-done((f32[96,1024]{1,0:T(8,128)S(1)}, f32[96,1024]{1,0:T(8,128)S(1)}, u32[]{:S(2)}, u32[]{:S(2)}) %collective-permute-start.2) | collective-permute-done | bytes 393248 | tf_op jit(solution)/shard_map/ppermute | solution.py:837
  23.6 1.2 %collective-permute-done.3.refs_1_ = f32[96,1024]{1,0:T(8,128)S(1)} collective-permute-done((f32[96,1024]{1,0:T(8,128)S(1)}, f32[96,1024]{1,0:T(8,128)S(1)}, u32[]{:S(2)}, u32[]{:S(2)}) %collective-permute-start.3) | collective-permute-done | bytes 393248 | tf_op jit(solution)/shard_map/ppermute | solution.py:837
  24.8 0.9 %ends.1 = (f32[89,8,128]{2,1,0:T(8,128)S(1)}, f32[89,8,128]{2,1,0:T(8,128)S(1)}, f32[32,8,128]{2,1,0:T(8,128)S(1)}) custom-call(s32[1,16]{1,0:T(1,128)} %pairs.5, s32[1]{0:T(128)} %bitcast.3.refs_1_.owner, s32[64]{0:T(128)S(1)} %get-tuple-element.53.mine, s32[1]{0:T(128)} %bitcast.4.parity, f32[88,8,128]{2,1,0:T(8,128)S(1)} %get-tuple-element.66.top, ...), custom_call_target="tpu_custom_call" | custom-call | flops 262144 | bytes 1048576 | tf_op jit(solution)/shard_map/ends/pallas_call | solution.py:559
  25.7 0.6 collective-permute-start.4
  26.2 5.6 %collective-permute-start.5 = (f32[89,8,128]{2,1,0:T(8,128)S(1)}, f32[89,8,128]{2,1,0:T(8,128)S(1)}, u32[]{:S(2)}, u32[]{:S(2)}) collective-permute-start(f32[89,8,128]{2,1,0:T(8,128)S(1)} %get-tuple-element.72.yo), channel_id=1, source_target_pairs={{8,16},{16,8},{24,32},{32,24},{40,48},{48,40},{56,64},{64,56},{72,... | collective-permute-start | bytes 1093640 | tf_op jit(solution)/shard_map/ppermute | solution.py:842
  31.8 10.4 %all_to_all.20.ya = f32[32,8,128]{2,1,0:T(8,128)S(1)} all-to-all(f32[32,8,128]{2,1,0:T(8,128)S(1)} %get-tuple-element.73), channel_id=1, replica_groups=mesh['owner'=16,'sub'=8] {'sub'}, dimensions={0} | all-to-all | bytes 262144 | tf_op jit(solution)/shard_map/all_to_all | solution.py:850
  42.2 0.0 collective-permute-done.4.ie
  42.2 0.0 collective-permute-done.5.io
  42.2 7.0 %first.1 = (f32[256,1024]{1,0:T(8,128)S(1)}, f32[256,1024]{1,0:T(8,128)S(1)}, f32[256,1024]{1,0:T(8,128)S(1)}, f32[288,1024]{1,0:T(8,128)S(1)}, f32[288,1024]{1,...) custom-call(s32[1,16]{1,0:T(1,128)} %pairs.5, ...), custom_call_target="tpu_custom_call", output_to_operand_aliasing={{0}: (9, {}), {1}: (10, {}), {2}: (11, {}), {3}: (12, {}), ... | custom-call | flops 16777216 | bytes 12582912 | tf_op jit(solution)/shard_map/first/pallas_call | solution.py:654
  49.2 8.8 %all_to_all.21.ya = f32[24,8,128]{2,1,0:T(8,128)S(1)} all-to-all(f32[24,8,128]{2,1,0:T(8,128)S(1)} %get-tuple-element.87), channel_id=1, replica_groups=mesh['owner'=16,'sub'=8] {'sub'}, dimensions={0} | all-to-all | bytes 196608 | tf_op jit(solution)/shard_map/all_to_all | solution.py:850
  58.0 4.2 %second.1 = (f32[256,1024]{1,0:T(8,128)S(1)}, f32[288,1024]{1,0:T(8,128)S(1)}, f32[288,1024]{1,0:T(8,128)S(1)}, f32[24,8,128]{2,1,0:T(8,128)S(1)}, f32[224,8,128...) custom-call(s32[64]{0:T(128)S(1)} %get-tuple-element.53.mine, s32[1]{0:T(128)} %bitcast.4.parity, ...), custom_call_target="tpu_custom_call" | custom-call | flops 4194304 | bytes 9437184 | tf_op jit(solution)/shard_map/second/pallas_call | solution.py:725
  62.2 8.2 %all_to_all.22.ya = f32[24,8,128]{2,1,0:T(8,128)S(1)} all-to-all(f32[24,8,128]{2,1,0:T(8,128)S(1)} %get-tuple-element.94), channel_id=1, replica_groups=mesh['owner'=16,'sub'=8] {'sub'}, dimensions={0} | all-to-all | bytes 196608 | tf_op jit(solution)/shard_map/all_to_all | solution.py:850
  70.4 3.5 %third.1 = (f32[256,1024]{1,0:T(8,128)S(1)}, f32[288,1024]{1,0:T(8,128)S(1)}, f32[288,1024]{1,0:T(8,128)S(1)}, f32[24,8,128]{2,1,0:T(8,128)S(1)}, f32[32,8,128]{2,1,0:T(8,128)S(1)}, /*index=5*/f32[16,8,128]{2,1,0:T(8,128)S(1)}) custom-call(s32[64]{0:T(128)S(1)} %get-tuple-element.53.mine, s32[2,64]{1,0:T(2,128)S(1)} %get-tuple-element.81.lists_in, ...), custom_call_target="tpu_custom_call" | custom-call | flops 4194304 | bytes 9437184 | tf_op jit(solution)/shard_map/third/pallas_call | solution.py:761
  73.9 8.2 %all_to_all.23.ya = f32[24,8,128]{2,1,0:T(8,128)S(1)} all-to-all(f32[24,8,128]{2,1,0:T(8,128)S(1)} %get-tuple-element.101), channel_id=1, replica_groups=mesh['owner'=16,'sub'=8] {'sub'}, dimensions={0} | all-to-all | bytes 196608 | tf_op jit(solution)/shard_map/all_to_all | solution.py:850
  82.1 3.8 %last.1 = (f32[256,1024]{1,0:T(8,128)}, f32[128,256]{1,0:T(8,128)}) custom-call(s32[64]{0:T(128)S(1)} %get-tuple-element.53.mine, s32[2,64]{1,0:T(2,128)S(1)} %get-tuple-element.81.lists_in, f32[256,1024]{1,0:T(8,128)S(1)} %get-tuple-element.95.v, f32[288,1024]{1,0:T(8,128)S(1)} %get-tuple-element.96.forth_in, f32[288,1024]{1,0:T(8,128)S(1)} %get-tuple-element.97.back_in, ...), custom_call_target="tpu_custom_call" | custom-call | flops 16777216 | bytes 10485760 | tf_op jit(solution)/shard_map/last/pallas_call | solution.py:820
Async XLA Ops:
  0.6 10.2 %copy-start = (s32[8,4]{0,1:T(4,128)S(1)}, s32[8,4]{0,1:T(4,128)}, u32[]{:S(2)}) copy-start(s32[8,4]{0,1:T(4,128)} %param.12) | copy-start | bytes 388
  2.9 13.5 %collective-permute-start = (f32[96,1024]{1,0:T(8,128)S(1)}, f32[96,1024]{1,0:T(8,128)S(1)}, u32[]{:S(2)}, u32[]{:S(2)}) collective-permute-start(f32[96,1024]{1,0:T(8,128)S(1)} %get-tuple-element.54), channel_id=1, source_target_pairs={{0,32},{8,40},{16,48},{24,56},{32,0},{40,8},{48,16},{56,24},{64,96... | collective-permute-start | bytes 1179656 | tf_op jit(solution)/shard_map/ppermute | solution.py:837
  3.0 13.4 %collective-permute-start.1 = (f32[96,1024]{1,0:T(8,128)S(1)}, f32[96,1024]{1,0:T(8,128)S(1)}, u32[]{:S(2)}, u32[]{:S(2)}) collective-permute-start(f32[96,1024]{1,0:T(8,128)S(1)} %get-tuple-element.55), channel_id=1, source_target_pairs={{0,8},{8,0},{16,24},{24,16},{32,40},{40,32},{48,56},{56,48},{64,72... | collective-permute-start | bytes 1179656 | tf_op jit(solution)/shard_map/ppermute | solution.py:837
  4.7 18.9 %collective-permute-start.2 = (f32[96,1024]{1,0:T(8,128)S(1)}, f32[96,1024]{1,0:T(8,128)S(1)}, u32[]{:S(2)}, u32[]{:S(2)}) collective-permute-start(f32[96,1024]{1,0:T(8,128)S(1)} %get-tuple-element.69), channel_id=1, source_target_pairs={{0,64},{8,72},{16,80},{24,88},{32,96},{40,104},{48,112},{56,120},{... | collective-permute-start | bytes 1179656 | tf_op jit(solution)/shard_map/ppermute | solution.py:837
  7.9 16.8 %collective-permute-start.3 = (f32[96,1024]{1,0:T(8,128)S(1)}, f32[96,1024]{1,0:T(8,128)S(1)}, u32[]{:S(2)}, u32[]{:S(2)}) collective-permute-start(f32[96,1024]{1,0:T(8,128)S(1)} %get-tuple-element.70), channel_id=1, source_target_pairs={{0,16},{8,24},{16,0},{24,8},{32,48},{40,56},{48,32},{56,40},{64,80... | collective-permute-start | bytes 1179656 | tf_op jit(solution)/shard_map/ppermute | solution.py:837
  25.7 16.5 %collective-permute-start.4 = (f32[89,8,128]{2,1,0:T(8,128)S(1)}, f32[89,8,128]{2,1,0:T(8,128)S(1)}, u32[]{:S(2)}, u32[]{:S(2)}) collective-permute-start(f32[89,8,128]{2,1,0:T(8,128)S(1)} %get-tuple-element.71.ye), channel_id=1, source_target_pairs={{0,8},{8,0},{16,24},{24,16},{32,40},{40,32},{48,56},{56,48},{64,72... | collective-permute-start | bytes 1093640 | tf_op jit(solution)/shard_map/ppermute | solution.py:837
  26.2 16.0 %collective-permute-start.5 = (f32[89,8,128]{2,1,0:T(8,128)S(1)}, f32[89,8,128]{2,1,0:T(8,128)S(1)}, u32[]{:S(2)}, u32[]{:S(2)}) collective-permute-start(f32[89,8,128]{2,1,0:T(8,128)S(1)} %get-tuple-element.72.yo), channel_id=1, source_target_pairs={{8,16},{16,8},{24,32},{32,24},{40,48},{48,40},{56,64},{64,56},{72,... | collective-permute-start | bytes 1093640 | tf_op jit(solution)/shard_map/ppermute | solution.py:842

commit v6 on v5

--- a/solution.py
+++ b/solution.py
@@ -625,6 +625,7 @@
         rows = block_rows(j)
         conduct = six_turned(c, forth_c, back_c, j, mine, ghost_c, below_c, above_c, fill=True)
         iterate = six_turned(v, forth_v, back_v, j, mine, ghost, below, above)
+        ready = []
         for (n, k, around_k), (_, centre, around) in zip(conduct, iterate):
             scaled, weight, inverse = weights(k, around_k)
             forced = weight * f[rows, column(n)]
@@ -634,6 +635,8 @@
             for d in range(6):
                 wk[d, rows, column(n)] = scaled[d]
                 total = total + scaled[d] * around[d]
+            ready.append((total, n))
+        for total, n in ready:
             store_swept(total, n, j, u, forth, back, faces)
         return carry
 
@@ -808,9 +811,12 @@
                 residual[part * 4 + n, pl.ds(0, half, stride=2), :]
                 + residual[part * 4 + n, pl.ds(1, half, stride=2), :]
             )
-            gather = jnp.where(place + EDGE * n == target, 0.125, 0.0)
-            total = total + jnp.dot(
-                column_sum, gather, precision=lax.Precision.HIGHEST, preferred_element_type=jnp.float32
+            gather = jnp.where(place + EDGE * n == target, 0.125, 0.0).astype(jnp.bfloat16)
+            high = column_sum.astype(jnp.bfloat16)
+            low = (column_sum - high.astype(jnp.float32)).astype(jnp.bfloat16)
+            total = total + (
+                jnp.dot(high, gather, preferred_element_type=jnp.float32)
+                + jnp.dot(low, gather, preferred_element_type=jnp.float32)
             )
         coarse[:, part * LANES : (part + 1) * LANES] = total
     write.wait()
@@ -857,8 +863,11 @@
     fields = tuple(values.reshape(FIELD) for values in (guess, rhs, coef))
     fields = tuple(in_hbm(x) for x in fields)
     occupied, swap_slot = in_hbm(occupied), in_hbm(swap_slot)
-    bulk = swap_pack(fields, occupied, swap_slot, owner, ORDER)
-    bulk = [pair_swap(block, 1 << bit) for bit, block in zip(ORDER, bulk)]
+    bulk = [
+        pair_swap(block, 1 << bit)
+        for bits in (SOON, LATE)
+        for bit, block in zip(bits, swap_pack(fields, occupied, swap_slot, owner, bits))
+    ]
     top, bottom, faces, mine, *merged = local(fields, occupied, neighbours, in_hbm(send_list), in_hbm(recv_list))
     (top, bottom, faces), merged = soon((top, bottom, faces), merged, bulk[:2], swap_slot, owner)
     ze, zo, ys = ends(top, bottom, faces, bulk[2:], swap_slot, owner, mine, parity)

time: 86.5 us -> 85.5 us (0.988)
  waiting for transfers between devices: 5.69 us -> 4.6 us
    pallas_call x1 -> x2, Pallas kernels: 2.25 us -> 3.92 us  [swap_pack(): pl.pallas_call(lambda *refs: swap_pack_kernel(bits, *refs), in_specs=[SME...]
    ppermute x5, waiting for transfers between devices: 5.68 us -> 4.6 us  [pair_swap(): lax.ppermute(values, 'owner', [(i, i ^ stride) for i in range(count)])]
    pallas_call x1, Pallas kernels: 2.64 us -> 1.72 us  [soon(): pl.pallas_call(soon_kernel, in_specs=[SMEM] * 2 + [VMEM] * (len(SOON) + c...]
  transfers between devices with their start and end apart: 6 -> 6, of which waited for: 2 -> 2; matrix products, arithmetic and copies ran while one was open for 0% -> 0% of each run, Pallas kernels for 9% -> 11%
where the time goes in v6:
time: 85.5 us; the launch traced here: 84.9 us
  blocking collectives  35.6 us (42%)
  Pallas kernels  29.6 us (35%)
  starting transfers between devices  14.2 us (17%)
  waiting for transfers between devices  4.6 us (5%)
    all_to_all x4, blocking collectives, segment_swap(): return lax.all_to_all(ys, 'sub', split_axis=0, concat_axis=0, tiled=True)  35.6 us
    ppermute x5, starting transfers between devices, pair_swap(): lax.ppermute(values, 'owner', [(i, i ^ stride) for i in range(count)])  8.6 us
    pallas_call x1, Pallas kernels, first(): pl.pallas_call(first_kernel, in_specs=[SMEM] * 4 + [VMEM] * (3 + len(LATE...  6.47 us
    ppermute x1, starting transfers between devices, odd_pair_swap(): lax.ppermute(values, 'owner', [(i, (i - 1 ^ 1) + 1) for i in range(1, cou...  5.65 us
    pallas_call x1, Pallas kernels, local(): pl.pallas_call(local_kernel, in_specs=[SMEM] * 4 + [HBM] * 3, out_specs=[...  5.5 us
    ppermute x5, waiting for transfers between devices, pair_swap(): lax.ppermute(values, 'owner', [(i, i ^ stride) for i in range(count)])  4.6 us
    pallas_call x1, Pallas kernels, second(): pl.pallas_call(second_kernel, in_specs=[SMEM] * 3 + [VMEM] * 10, out_spec...  4.24 us
    pallas_call x2, Pallas kernels, swap_pack(): pl.pallas_call(lambda *refs: swap_pack_kernel(bits, *refs), in_specs=[SME...  3.92 us
  transfers between devices with their start and end apart: 6, of which 2 were waited for; matrix products, arithmetic and copies ran while one was open for 0% of the time, Pallas kernels for 11%

profile of v6, /device:TPU:32, one launch (start us, length us, event | category | flops | bytes accessed | tf_op | source)
XLA Modules:
  0.0 84.9 jit_solution(4773379376912214491)
XLA Ops:
  0.6 2.0 %swap_pack.2 = (f32[96,1024]{1,0:T(8,128)S(1)}, f32[96,1024]{1,0:T(8,128)S(1)}) custom-call(s32[1,16]{1,0:T(1,128)} %pairs.5, s32[1]{0:T(128)} %bitcast.3.refs_1_.owner, s32[8]{0:T(128)} %refs_2_.3, f32[256,1024]{1,0:T(8,128)} %bitcast.7, f32[256,1024]{1,0:T(8,128)} %bitcast.10, f32[256,1024]{1,0:T(8,128)} %bitcast.13), custom_call_target="tpu_custom_call" | custom-call | flops 524288 | bytes 1572864 | tf_op jit(solution)/shard_map/swap_pack/pallas_call | solution.py:418
  2.6 0.1 collective-permute-start
  2.7 0.0 copy-start
  2.7 1.7 %collective-permute-start.1 = (f32[96,1024]{1,0:T(8,128)S(1)}, f32[96,1024]{1,0:T(8,128)S(1)}, u32[]{:S(2)}, u32[]{:S(2)}) collective-permute-start(f32[96,1024]{1,0:T(8,128)S(1)} %get-tuple-element.55), channel_id=1, source_target_pairs={{0,8},{8,0},{16,24},{24,16},{32,40},{40,32},{48,56},{56,48},{64,72... | collective-permute-start | bytes 1179656 | tf_op jit(solution)/shard_map/ppermute | solution.py:843
  4.4 2.0 %swap_pack.3 = (f32[96,1024]{1,0:T(8,128)S(1)}, f32[96,1024]{1,0:T(8,128)S(1)}) custom-call(s32[1,16]{1,0:T(1,128)} %pairs.5, s32[1]{0:T(128)} %bitcast.3.refs_1_.owner, s32[8]{0:T(128)} %refs_2_.3, f32[256,1024]{1,0:T(8,128)} %bitcast.8, f32[256,1024]{1,0:T(8,128)} %bitcast.11, f32[256,1024]{1,0:T(8,128)} %bitcast.14), custom_call_target="tpu_custom_call" | custom-call | flops 524288 | bytes 1572864 | tf_op jit(solution)/shard_map/swap_pack/pallas_call | solution.py:418
  6.3 3.3 %collective-permute-start.2 = (f32[96,1024]{1,0:T(8,128)S(1)}, f32[96,1024]{1,0:T(8,128)S(1)}, u32[]{:S(2)}, u32[]{:S(2)}) collective-permute-start(f32[96,1024]{1,0:T(8,128)S(1)} %get-tuple-element.69), channel_id=1, source_target_pairs={{0,64},{8,72},{16,80},{24,88},{32,96},{40,104},{48,112},{56,120},{... | collective-permute-start | bytes 1179656 | tf_op jit(solution)/shard_map/ppermute | solution.py:843
  9.7 2.9 %collective-permute-start.3 = (f32[96,1024]{1,0:T(8,128)S(1)}, f32[96,1024]{1,0:T(8,128)S(1)}, u32[]{:S(2)}, u32[]{:S(2)}) collective-permute-start(f32[96,1024]{1,0:T(8,128)S(1)} %get-tuple-element.70), channel_id=1, source_target_pairs={{0,16},{8,24},{16,0},{24,8},{32,48},{40,56},{48,32},{56,40},{64,80... | collective-permute-start | bytes 1179656 | tf_op jit(solution)/shard_map/ppermute | solution.py:843
  12.6 0.0 copy-done
  12.6 0.1 copy.27.neighbours
  12.6 5.5 %local.1 = (f32[88,8,128]{2,1,0:T(8,128)S(1)}, f32[88,8,128]{2,1,0:T(8,128)S(1)}, f32[32,8,128]{2,1,0:T(8,128)S(1)}, s32[64]{0:T(128)S(1)}, f32[256,1024]{1,0:T(...) custom-call(s32[8]{0:T(128)} %refs_2_.3, ...), custom_call_target="tpu_custom_call" | custom-call | flops 1048576 | bytes 4194304 | tf_op jit(solution)/shard_map/local/pallas_call | solution.py:472
  18.2 0.0 collective-permute-done.refs_0_
  18.2 0.0 collective-permute-done.1.refs_1_
  18.2 1.7 %soon.1 = (f32[88,8,128]{2,1,0:T(8,128)S(1)}, f32[88,8,128]{2,1,0:T(8,128)S(1)}, f32[32,8,128]{2,1,0:T(8,128)S(1)}, f32[256,1024]{1,0:T(8,128)S(1)}, f32[256,102...) custom-call(s32[1,16]{1,0:T(1,128)} %pairs.5, ...), custom_call_target="tpu_custom_call", output_to_operand_aliasing={{0}: (4, {}), {1}: (5, {}), {2}: (6, {}), {3}: (7, {}), {4}... | custom-call | flops 262144 | bytes 2097152 | tf_op jit(solution)/shard_map/soon/pallas_call | solution.py:519
  19.9 3.4 %collective-permute-done.2.refs_0_ = f32[96,1024]{1,0:T(8,128)S(1)} collective-permute-done((f32[96,1024]{1,0:T(8,128)S(1)}, f32[96,1024]{1,0:T(8,128)S(1)}, u32[]{:S(2)}, u32[]{:S(2)}) %collective-permute-start.2) | collective-permute-done | bytes 393248 | tf_op jit(solution)/shard_map/ppermute | solution.py:843
  23.3 1.2 %collective-permute-done.3.refs_1_ = f32[96,1024]{1,0:T(8,128)S(1)} collective-permute-done((f32[96,1024]{1,0:T(8,128)S(1)}, f32[96,1024]{1,0:T(8,128)S(1)}, u32[]{:S(2)}, u32[]{:S(2)}) %collective-permute-start.3) | collective-permute-done | bytes 393248 | tf_op jit(solution)/shard_map/ppermute | solution.py:843
  24.5 0.8 ends.1
  25.3 0.6 collective-permute-start.4
  25.9 5.6 %collective-permute-start.5 = (f32[89,8,128]{2,1,0:T(8,128)S(1)}, f32[89,8,128]{2,1,0:T(8,128)S(1)}, u32[]{:S(2)}, u32[]{:S(2)}) collective-permute-start(f32[89,8,128]{2,1,0:T(8,128)S(1)} %get-tuple-element.72.yo), channel_id=1, source_target_pairs={{8,16},{16,8},{24,32},{32,24},{40,48},{48,40},{56,64},{64,56},{72,... | collective-permute-start | bytes 1093640 | tf_op jit(solution)/shard_map/ppermute | solution.py:848
  31.6 10.2 %all_to_all.20.ya = f32[32,8,128]{2,1,0:T(8,128)S(1)} all-to-all(f32[32,8,128]{2,1,0:T(8,128)S(1)} %get-tuple-element.73), channel_id=1, replica_groups=mesh['owner'=16,'sub'=8] {'sub'}, dimensions={0} | all-to-all | bytes 262144 | tf_op jit(solution)/shard_map/all_to_all | solution.py:856
  41.7 0.0 collective-permute-done.4.ie
  41.7 0.0 collective-permute-done.5.io
  41.8 6.5 %first.1 = (f32[256,1024]{1,0:T(8,128)S(1)}, f32[256,1024]{1,0:T(8,128)S(1)}, f32[256,1024]{1,0:T(8,128)S(1)}, f32[288,1024]{1,0:T(8,128)S(1)}, f32[288,1024]{1,...) custom-call(s32[1,16]{1,0:T(1,128)} %pairs.5, ...), custom_call_target="tpu_custom_call", output_to_operand_aliasing={{0}: (9, {}), {1}: (10, {}), {2}: (11, {}), {3}: (12, {}), ... | custom-call | flops 16777216 | bytes 12582912 | tf_op jit(solution)/shard_map/first/pallas_call | solution.py:657
  48.2 9.1 %all_to_all.21.ya = f32[24,8,128]{2,1,0:T(8,128)S(1)} all-to-all(f32[24,8,128]{2,1,0:T(8,128)S(1)} %get-tuple-element.87), channel_id=1, replica_groups=mesh['owner'=16,'sub'=8] {'sub'}, dimensions={0} | all-to-all | bytes 196608 | tf_op jit(solution)/shard_map/all_to_all | solution.py:856
  57.3 4.2 %second.1 = (f32[256,1024]{1,0:T(8,128)S(1)}, f32[288,1024]{1,0:T(8,128)S(1)}, f32[288,1024]{1,0:T(8,128)S(1)}, f32[24,8,128]{2,1,0:T(8,128)S(1)}, f32[224,8,128...) custom-call(s32[64]{0:T(128)S(1)} %get-tuple-element.53.mine, s32[1]{0:T(128)} %bitcast.4.parity, ...), custom_call_target="tpu_custom_call" | custom-call | flops 4194304 | bytes 9437184 | tf_op jit(solution)/shard_map/second/pallas_call | solution.py:728
  61.5 8.2 %all_to_all.22.ya = f32[24,8,128]{2,1,0:T(8,128)S(1)} all-to-all(f32[24,8,128]{2,1,0:T(8,128)S(1)} %get-tuple-element.94), channel_id=1, replica_groups=mesh['owner'=16,'sub'=8] {'sub'}, dimensions={0} | all-to-all | bytes 196608 | tf_op jit(solution)/shard_map/all_to_all | solution.py:856
  69.7 3.5 %third.1 = (f32[256,1024]{1,0:T(8,128)S(1)}, f32[288,1024]{1,0:T(8,128)S(1)}, f32[288,1024]{1,0:T(8,128)S(1)}, f32[24,8,128]{2,1,0:T(8,128)S(1)}, f32[32,8,128]{2,1,0:T(8,128)S(1)}, /*index=5*/f32[16,8,128]{2,1,0:T(8,128)S(1)}) custom-call(s32[64]{0:T(128)S(1)} %get-tuple-element.53.mine, s32[2,64]{1,0:T(2,128)S(1)} %get-tuple-element.81.lists_in, ...), custom_call_target="tpu_custom_call" | custom-call | flops 4194304 | bytes 9437184 | tf_op jit(solution)/shard_map/third/pallas_call | solution.py:764
  73.2 8.2 %all_to_all.23.ya = f32[24,8,128]{2,1,0:T(8,128)S(1)} all-to-all(f32[24,8,128]{2,1,0:T(8,128)S(1)} %get-tuple-element.101), channel_id=1, replica_groups=mesh['owner'=16,'sub'=8] {'sub'}, dimensions={0} | all-to-all | bytes 196608 | tf_op jit(solution)/shard_map/all_to_all | solution.py:856
  81.4 3.5 %last.1 = (f32[256,1024]{1,0:T(8,128)}, f32[128,256]{1,0:T(8,128)}) custom-call(s32[64]{0:T(128)S(1)} %get-tuple-element.53.mine, s32[2,64]{1,0:T(2,128)S(1)} %get-tuple-element.81.lists_in, f32[256,1024]{1,0:T(8,128)S(1)} %get-tuple-element.95.v, f32[288,1024]{1,0:T(8,128)S(1)} %get-tuple-element.96.forth_in, f32[288,1024]{1,0:T(8,128)S(1)} %get-tuple-element.97.back_in, ...), custom_call_target="tpu_custom_call" | custom-call | flops 16777216 | bytes 10485760 | tf_op jit(solution)/shard_map/last/pallas_call | solution.py:826
Async XLA Ops:
  2.6 15.6 %collective-permute-start = (f32[96,1024]{1,0:T(8,128)S(1)}, f32[96,1024]{1,0:T(8,128)S(1)}, u32[]{:S(2)}, u32[]{:S(2)}) collective-permute-start(f32[96,1024]{1,0:T(8,128)S(1)} %get-tuple-element.54), channel_id=1, source_target_pairs={{0,32},{8,40},{16,48},{24,56},{32,0},{40,8},{48,16},{56,24},{64,96... | collective-permute-start | bytes 1179656 | tf_op jit(solution)/shard_map/ppermute | solution.py:843
  2.7 9.9 %copy-start = (s32[8,4]{0,1:T(4,128)S(1)}, s32[8,4]{0,1:T(4,128)}, u32[]{:S(2)}) copy-start(s32[8,4]{0,1:T(4,128)} %param.12) | copy-start | bytes 388
  2.7 15.5 %collective-permute-start.1 = (f32[96,1024]{1,0:T(8,128)S(1)}, f32[96,1024]{1,0:T(8,128)S(1)}, u32[]{:S(2)}, u32[]{:S(2)}) collective-permute-start(f32[96,1024]{1,0:T(8,128)S(1)} %get-tuple-element.55), channel_id=1, source_target_pairs={{0,8},{8,0},{16,24},{24,16},{32,40},{40,32},{48,56},{56,48},{64,72... | collective-permute-start | bytes 1179656 | tf_op jit(solution)/shard_map/ppermute | solution.py:843
  6.3 17.0 %collective-permute-start.2 = (f32[96,1024]{1,0:T(8,128)S(1)}, f32[96,1024]{1,0:T(8,128)S(1)}, u32[]{:S(2)}, u32[]{:S(2)}) collective-permute-start(f32[96,1024]{1,0:T(8,128)S(1)} %get-tuple-element.69), channel_id=1, source_target_pairs={{0,64},{8,72},{16,80},{24,88},{32,96},{40,104},{48,112},{56,120},{... | collective-permute-start | bytes 1179656 | tf_op jit(solution)/shard_map/ppermute | solution.py:843
  9.7 14.8 %collective-permute-start.3 = (f32[96,1024]{1,0:T(8,128)S(1)}, f32[96,1024]{1,0:T(8,128)S(1)}, u32[]{:S(2)}, u32[]{:S(2)}) collective-permute-start(f32[96,1024]{1,0:T(8,128)S(1)} %get-tuple-element.70), channel_id=1, source_target_pairs={{0,16},{8,24},{16,0},{24,8},{32,48},{40,56},{48,32},{56,40},{64,80... | collective-permute-start | bytes 1179656 | tf_op jit(solution)/shard_map/ppermute | solution.py:843
  25.3 16.4 %collective-permute-start.4 = (f32[89,8,128]{2,1,0:T(8,128)S(1)}, f32[89,8,128]{2,1,0:T(8,128)S(1)}, u32[]{:S(2)}, u32[]{:S(2)}) collective-permute-start(f32[89,8,128]{2,1,0:T(8,128)S(1)} %get-tuple-element.71.ye), channel_id=1, source_target_pairs={{0,8},{8,0},{16,24},{24,16},{32,40},{40,32},{48,56},{56,48},{64,72... | collective-permute-start | bytes 1093640 | tf_op jit(solution)/shard_map/ppermute | solution.py:843
  25.9 15.8 %collective-permute-start.5 = (f32[89,8,128]{2,1,0:T(8,128)S(1)}, f32[89,8,128]{2,1,0:T(8,128)S(1)}, u32[]{:S(2)}, u32[]{:S(2)}) collective-permute-start(f32[89,8,128]{2,1,0:T(8,128)S(1)} %get-tuple-element.72.yo), channel_id=1, source_target_pairs={{8,16},{16,8},{24,32},{32,24},{40,48},{48,40},{56,64},{64,56},{72,... | collective-permute-start | bytes 1093640 | tf_op jit(solution)/shard_map/ppermute | solution.py:848

commit v7 on v6

--- a/solution.py
+++ b/solution.py
@@ -814,9 +814,10 @@
             gather = jnp.where(place + EDGE * n == target, 0.125, 0.0).astype(jnp.bfloat16)
             high = column_sum.astype(jnp.bfloat16)
             low = (column_sum - high.astype(jnp.float32)).astype(jnp.bfloat16)
-            total = total + (
-                jnp.dot(high, gather, preferred_element_type=jnp.float32)
-                + jnp.dot(low, gather, preferred_element_type=jnp.float32)
+            total = total + jnp.dot(
+                jnp.concatenate([high, low], axis=1),
+                jnp.concatenate([gather, gather], axis=0),
+                preferred_element_type=jnp.float32,
             )
         coarse[:, part * LANES : (part + 1) * LANES] = total
     write.wait()

time: 85.5 us -> 85.4 us (level)
  Pallas kernels: 29.6 us -> 30.5 us
    pallas_call x1, Pallas kernels: 1.72 us -> 2.64 us  [soon(): pl.pallas_call(soon_kernel, in_specs=[SMEM] * 2 + [VMEM] * (len(SOON) + c...]
  transfers between devices with their start and end apart: 6 -> 6, of which waited for: 2 -> 2; matrix products, arithmetic and copies ran while one was open for 0% -> 0% of each run, Pallas kernels for 11% -> 12%
where the time goes in v7:
time: 85.4 us; the launch traced here: 84.6 us
  blocking collectives  35.3 us (41%)
  Pallas kernels  30.5 us (36%)
  starting transfers between devices  14.2 us (17%)
  waiting for transfers between devices  3.75 us (4%)
    all_to_all x4, blocking collectives, segment_swap(): return lax.all_to_all(ys, 'sub', split_axis=0, concat_axis=0, tiled=True)  35.3 us
    ppermute x5, starting transfers between devices, pair_swap(): lax.ppermute(values, 'owner', [(i, i ^ stride) for i in range(count)])  8.57 us
    pallas_call x1, Pallas kernels, first(): pl.pallas_call(first_kernel, in_specs=[SMEM] * 4 + [VMEM] * (3 + len(LATE...  6.47 us
    ppermute x1, starting transfers between devices, odd_pair_swap(): lax.ppermute(values, 'owner', [(i, (i - 1 ^ 1) + 1) for i in range(1, cou...  5.67 us
    pallas_call x1, Pallas kernels, local(): pl.pallas_call(local_kernel, in_specs=[SMEM] * 4 + [HBM] * 3, out_specs=[...  5.49 us
    pallas_call x1, Pallas kernels, second(): pl.pallas_call(second_kernel, in_specs=[SMEM] * 3 + [VMEM] * 10, out_spec...  4.25 us
    pallas_call x2, Pallas kernels, swap_pack(): pl.pallas_call(lambda *refs: swap_pack_kernel(bits, *refs), in_specs=[SME...  3.89 us
    ppermute x5, waiting for transfers between devices, pair_swap(): lax.ppermute(values, 'owner', [(i, i ^ stride) for i in range(count)])  3.75 us
  transfers between devices with their start and end apart: 6, of which 2 were waited for; matrix products, arithmetic and copies ran while one was open for 0% of the time, Pallas kernels for 12%

profile of v7, /device:TPU:32, one launch (start us, length us, event | category | flops | bytes accessed | tf_op | source)
XLA Modules:
  0.0 84.6 jit_solution(4238029745799315608)
XLA Ops:
  0.6 1.9 %swap_pack.2 = (f32[96,1024]{1,0:T(8,128)S(1)}, f32[96,1024]{1,0:T(8,128)S(1)}) custom-call(s32[1,16]{1,0:T(1,128)} %pairs.5, s32[1]{0:T(128)} %bitcast.3.refs_1_.owner, s32[8]{0:T(128)} %refs_2_.3, f32[256,1024]{1,0:T(8,128)} %bitcast.7, f32[256,1024]{1,0:T(8,128)} %bitcast.10, f32[256,1024]{1,0:T(8,128)} %bitcast.13), custom_call_target="tpu_custom_call" | custom-call | flops 524288 | bytes 1572864 | tf_op jit(solution)/shard_map/swap_pack/pallas_call | solution.py:418
  2.6 0.1 collective-permute-start
  2.7 0.0 copy-start
  2.7 1.7 %collective-permute-start.1 = (f32[96,1024]{1,0:T(8,128)S(1)}, f32[96,1024]{1,0:T(8,128)S(1)}, u32[]{:S(2)}, u32[]{:S(2)}) collective-permute-start(f32[96,1024]{1,0:T(8,128)S(1)} %get-tuple-element.55), channel_id=1, source_target_pairs={{0,8},{8,0},{16,24},{24,16},{32,40},{40,32},{48,56},{56,48},{64,72... | collective-permute-start | bytes 1179656 | tf_op jit(solution)/shard_map/ppermute | solution.py:844
  4.3 2.0 %swap_pack.3 = (f32[96,1024]{1,0:T(8,128)S(1)}, f32[96,1024]{1,0:T(8,128)S(1)}) custom-call(s32[1,16]{1,0:T(1,128)} %pairs.5, s32[1]{0:T(128)} %bitcast.3.refs_1_.owner, s32[8]{0:T(128)} %refs_2_.3, f32[256,1024]{1,0:T(8,128)} %bitcast.8, f32[256,1024]{1,0:T(8,128)} %bitcast.11, f32[256,1024]{1,0:T(8,128)} %bitcast.14), custom_call_target="tpu_custom_call" | custom-call | flops 524288 | bytes 1572864 | tf_op jit(solution)/shard_map/swap_pack/pallas_call | solution.py:418
  6.3 3.3 %collective-permute-start.2 = (f32[96,1024]{1,0:T(8,128)S(1)}, f32[96,1024]{1,0:T(8,128)S(1)}, u32[]{:S(2)}, u32[]{:S(2)}) collective-permute-start(f32[96,1024]{1,0:T(8,128)S(1)} %get-tuple-element.69), channel_id=1, source_target_pairs={{0,64},{8,72},{16,80},{24,88},{32,96},{40,104},{48,112},{56,120},{... | collective-permute-start | bytes 1179656 | tf_op jit(solution)/shard_map/ppermute | solution.py:844
  9.6 2.9 %collective-permute-start.3 = (f32[96,1024]{1,0:T(8,128)S(1)}, f32[96,1024]{1,0:T(8,128)S(1)}, u32[]{:S(2)}, u32[]{:S(2)}) collective-permute-start(f32[96,1024]{1,0:T(8,128)S(1)} %get-tuple-element.70), channel_id=1, source_target_pairs={{0,16},{8,24},{16,0},{24,8},{32,48},{40,56},{48,32},{56,40},{64,80... | collective-permute-start | bytes 1179656 | tf_op jit(solution)/shard_map/ppermute | solution.py:844
  12.5 0.0 copy-done
  12.5 0.1 copy.27.neighbours
  12.6 5.5 %local.1 = (f32[88,8,128]{2,1,0:T(8,128)S(1)}, f32[88,8,128]{2,1,0:T(8,128)S(1)}, f32[32,8,128]{2,1,0:T(8,128)S(1)}, s32[64]{0:T(128)S(1)}, f32[256,1024]{1,0:T(...) custom-call(s32[8]{0:T(128)} %refs_2_.3, ...), custom_call_target="tpu_custom_call" | custom-call | flops 1048576 | bytes 4194304 | tf_op jit(solution)/shard_map/local/pallas_call | solution.py:472
  18.1 0.0 collective-permute-done.refs_0_
  18.1 0.0 collective-permute-done.1.refs_1_
  18.1 2.6 %soon.1 = (f32[88,8,128]{2,1,0:T(8,128)S(1)}, f32[88,8,128]{2,1,0:T(8,128)S(1)}, f32[32,8,128]{2,1,0:T(8,128)S(1)}, f32[256,1024]{1,0:T(8,128)S(1)}, f32[256,102...) custom-call(s32[1,16]{1,0:T(1,128)} %pairs.5, ...), custom_call_target="tpu_custom_call", output_to_operand_aliasing={{0}: (4, {}), {1}: (5, {}), {2}: (6, {}), {3}: (7, {}), {4}... | custom-call | flops 262144 | bytes 2097152 | tf_op jit(solution)/shard_map/soon/pallas_call | solution.py:519
  20.8 2.5 %collective-permute-done.2.refs_0_ = f32[96,1024]{1,0:T(8,128)S(1)} collective-permute-done((f32[96,1024]{1,0:T(8,128)S(1)}, f32[96,1024]{1,0:T(8,128)S(1)}, u32[]{:S(2)}, u32[]{:S(2)}) %collective-permute-start.2) | collective-permute-done | bytes 393248 | tf_op jit(solution)/shard_map/ppermute | solution.py:844
  23.3 1.2 %collective-permute-done.3.refs_1_ = f32[96,1024]{1,0:T(8,128)S(1)} collective-permute-done((f32[96,1024]{1,0:T(8,128)S(1)}, f32[96,1024]{1,0:T(8,128)S(1)}, u32[]{:S(2)}, u32[]{:S(2)}) %collective-permute-start.3) | collective-permute-done | bytes 393248 | tf_op jit(solution)/shard_map/ppermute | solution.py:844
  24.5 0.8 ends.1
  25.3 0.6 collective-permute-start.4
  25.9 5.7 %collective-permute-start.5 = (f32[89,8,128]{2,1,0:T(8,128)S(1)}, f32[89,8,128]{2,1,0:T(8,128)S(1)}, u32[]{:S(2)}, u32[]{:S(2)}) collective-permute-start(f32[89,8,128]{2,1,0:T(8,128)S(1)} %get-tuple-element.72.yo), channel_id=1, source_target_pairs={{8,16},{16,8},{24,32},{32,24},{40,48},{48,40},{56,64},{64,56},{72,... | collective-permute-start | bytes 1093640 | tf_op jit(solution)/shard_map/ppermute | solution.py:849
  31.6 10.2 %all_to_all.20.ya = f32[32,8,128]{2,1,0:T(8,128)S(1)} all-to-all(f32[32,8,128]{2,1,0:T(8,128)S(1)} %get-tuple-element.73), channel_id=1, replica_groups=mesh['owner'=16,'sub'=8] {'sub'}, dimensions={0} | all-to-all | bytes 262144 | tf_op jit(solution)/shard_map/all_to_all | solution.py:857
  41.8 0.0 collective-permute-done.4.ie
  41.8 0.0 collective-permute-done.5.io
  41.8 6.5 %first.1 = (f32[256,1024]{1,0:T(8,128)S(1)}, f32[256,1024]{1,0:T(8,128)S(1)}, f32[256,1024]{1,0:T(8,128)S(1)}, f32[288,1024]{1,0:T(8,128)S(1)}, f32[288,1024]{1,...) custom-call(s32[1,16]{1,0:T(1,128)} %pairs.5, ...), custom_call_target="tpu_custom_call", output_to_operand_aliasing={{0}: (9, {}), {1}: (10, {}), {2}: (11, {}), {3}: (12, {}), ... | custom-call | flops 16777216 | bytes 12582912 | tf_op jit(solution)/shard_map/first/pallas_call | solution.py:657
  48.3 8.7 %all_to_all.21.ya = f32[24,8,128]{2,1,0:T(8,128)S(1)} all-to-all(f32[24,8,128]{2,1,0:T(8,128)S(1)} %get-tuple-element.87), channel_id=1, replica_groups=mesh['owner'=16,'sub'=8] {'sub'}, dimensions={0} | all-to-all | bytes 196608 | tf_op jit(solution)/shard_map/all_to_all | solution.py:857
  57.0 4.2 %second.1 = (f32[256,1024]{1,0:T(8,128)S(1)}, f32[288,1024]{1,0:T(8,128)S(1)}, f32[288,1024]{1,0:T(8,128)S(1)}, f32[24,8,128]{2,1,0:T(8,128)S(1)}, f32[224,8,128...) custom-call(s32[64]{0:T(128)S(1)} %get-tuple-element.53.mine, s32[1]{0:T(128)} %bitcast.4.parity, ...), custom_call_target="tpu_custom_call" | custom-call | flops 4194304 | bytes 9437184 | tf_op jit(solution)/shard_map/second/pallas_call | solution.py:728
  61.3 8.2 %all_to_all.22.ya = f32[24,8,128]{2,1,0:T(8,128)S(1)} all-to-all(f32[24,8,128]{2,1,0:T(8,128)S(1)} %get-tuple-element.94), channel_id=1, replica_groups=mesh['owner'=16,'sub'=8] {'sub'}, dimensions={0} | all-to-all | bytes 196608 | tf_op jit(solution)/shard_map/all_to_all | solution.py:857
  69.4 3.5 %third.1 = (f32[256,1024]{1,0:T(8,128)S(1)}, f32[288,1024]{1,0:T(8,128)S(1)}, f32[288,1024]{1,0:T(8,128)S(1)}, f32[24,8,128]{2,1,0:T(8,128)S(1)}, f32[32,8,128]{2,1,0:T(8,128)S(1)}, /*index=5*/f32[16,8,128]{2,1,0:T(8,128)S(1)}) custom-call(s32[64]{0:T(128)S(1)} %get-tuple-element.53.mine, s32[2,64]{1,0:T(2,128)S(1)} %get-tuple-element.81.lists_in, ...), custom_call_target="tpu_custom_call" | custom-call | flops 4194304 | bytes 9437184 | tf_op jit(solution)/shard_map/third/pallas_call | solution.py:764
  72.9 8.2 %all_to_all.23.ya = f32[24,8,128]{2,1,0:T(8,128)S(1)} all-to-all(f32[24,8,128]{2,1,0:T(8,128)S(1)} %get-tuple-element.101), channel_id=1, replica_groups=mesh['owner'=16,'sub'=8] {'sub'}, dimensions={0} | all-to-all | bytes 196608 | tf_op jit(solution)/shard_map/all_to_all | solution.py:857
  81.1 3.5 %last.1 = (f32[256,1024]{1,0:T(8,128)}, f32[128,256]{1,0:T(8,128)}) custom-call(s32[64]{0:T(128)S(1)} %get-tuple-element.53.mine, s32[2,64]{1,0:T(2,128)S(1)} %get-tuple-element.81.lists_in, f32[256,1024]{1,0:T(8,128)S(1)} %get-tuple-element.95.v, f32[288,1024]{1,0:T(8,128)S(1)} %get-tuple-element.96.forth_in, f32[288,1024]{1,0:T(8,128)S(1)} %get-tuple-element.97.back_in, ...), custom_call_target="tpu_custom_call" | custom-call | flops 16777216 | bytes 10485760 | tf_op jit(solution)/shard_map/last/pallas_call | solution.py:827
Async XLA Ops:
  2.6 15.5 %collective-permute-start = (f32[96,1024]{1,0:T(8,128)S(1)}, f32[96,1024]{1,0:T(8,128)S(1)}, u32[]{:S(2)}, u32[]{:S(2)}) collective-permute-start(f32[96,1024]{1,0:T(8,128)S(1)} %get-tuple-element.54), channel_id=1, source_target_pairs={{0,32},{8,40},{16,48},{24,56},{32,0},{40,8},{48,16},{56,24},{64,96... | collective-permute-start | bytes 1179656 | tf_op jit(solution)/shard_map/ppermute | solution.py:844
  2.7 9.9 %copy-start = (s32[8,4]{0,1:T(4,128)S(1)}, s32[8,4]{0,1:T(4,128)}, u32[]{:S(2)}) copy-start(s32[8,4]{0,1:T(4,128)} %param.12) | copy-start | bytes 388
  2.7 15.4 %collective-permute-start.1 = (f32[96,1024]{1,0:T(8,128)S(1)}, f32[96,1024]{1,0:T(8,128)S(1)}, u32[]{:S(2)}, u32[]{:S(2)}) collective-permute-start(f32[96,1024]{1,0:T(8,128)S(1)} %get-tuple-element.55), channel_id=1, source_target_pairs={{0,8},{8,0},{16,24},{24,16},{32,40},{40,32},{48,56},{56,48},{64,72... | collective-permute-start | bytes 1179656 | tf_op jit(solution)/shard_map/ppermute | solution.py:844
  6.3 17.0 %collective-permute-start.2 = (f32[96,1024]{1,0:T(8,128)S(1)}, f32[96,1024]{1,0:T(8,128)S(1)}, u32[]{:S(2)}, u32[]{:S(2)}) collective-permute-start(f32[96,1024]{1,0:T(8,128)S(1)} %get-tuple-element.69), channel_id=1, source_target_pairs={{0,64},{8,72},{16,80},{24,88},{32,96},{40,104},{48,112},{56,120},{... | collective-permute-start | bytes 1179656 | tf_op jit(solution)/shard_map/ppermute | solution.py:844
  9.6 14.9 %collective-permute-start.3 = (f32[96,1024]{1,0:T(8,128)S(1)}, f32[96,1024]{1,0:T(8,128)S(1)}, u32[]{:S(2)}, u32[]{:S(2)}) collective-permute-start(f32[96,1024]{1,0:T(8,128)S(1)} %get-tuple-element.70), channel_id=1, source_target_pairs={{0,16},{8,24},{16,0},{24,8},{32,48},{40,56},{48,32},{56,40},{64,80... | collective-permute-start | bytes 1179656 | tf_op jit(solution)/shard_map/ppermute | solution.py:844
  25.3 16.5 %collective-permute-start.4 = (f32[89,8,128]{2,1,0:T(8,128)S(1)}, f32[89,8,128]{2,1,0:T(8,128)S(1)}, u32[]{:S(2)}, u32[]{:S(2)}) collective-permute-start(f32[89,8,128]{2,1,0:T(8,128)S(1)} %get-tuple-element.71.ye), channel_id=1, source_target_pairs={{0,8},{8,0},{16,24},{24,16},{32,40},{40,32},{48,56},{56,48},{64,72... | collective-permute-start | bytes 1093640 | tf_op jit(solution)/shard_map/ppermute | solution.py:844
  25.9 15.9 %collective-permute-start.5 = (f32[89,8,128]{2,1,0:T(8,128)S(1)}, f32[89,8,128]{2,1,0:T(8,128)S(1)}, u32[]{:S(2)}, u32[]{:S(2)}) collective-permute-start(f32[89,8,128]{2,1,0:T(8,128)S(1)} %get-tuple-element.72.yo), channel_id=1, source_target_pairs={{8,16},{16,8},{24,32},{32,24},{40,48},{48,40},{56,64},{64,56},{72,... | collective-permute-start | bytes 1093640 | tf_op jit(solution)/shard_map/ppermute | solution.py:849
